TPU v7x, 256 devices: a whole 4x4x8 slice. The times are simulated.
256 devices in a mesh: mx: 8 (over z), my: 32 (over x, y, core).
Axes of the slice: x: 4, y: 4, z: 8, core: 2. Of those that a mesh axis runs over, the one named last changes fastest.
Arguments:
- friction: float32 [2048, 4096], P('mx', 'my'), may hold values from 0.5 to 2
- taps_row: float32 [17], replicated, may hold values from 0.03 to 0.09
- taps_col: float32 [17], replicated, may hold values from 0.03 to 0.09
- probe: float32 [2048, 4096], P('mx', 'my'), may hold values from -6 to 6
- win_row: int32 [8, 32, 16], P('mx', 'my'), may hold values from 0 to 223
- win_col: int32 [8, 32, 16], P('mx', 'my'), may hold values from 0 to 95
- live_count: int32 [8, 32], P('mx', 'my'), may hold values from 1 to 16, as said below
Outputs:
- hessian_apply: float32 [2048, 4096], P('mx', 'my')
Inputs may be any that keep to these rules, and one draw needn't show every extreme that they name: `live_count`: every tile has at least one live slot; some tile has all 16 live in every draw.
All inputs are finite; a program needn't handle non-finite values.
Results may differ from a plain program's by a relative error of at most 0.0001.
Values sent between devices are 32-bit elements; how exact they have to be, the bound alone decides.
No kernel may reach another device: no remote copies, remote signals or barrier semaphores. Data moves between devices by JAX's collectives and lax.ppermute only.
A program may use at most 64 MiB of HBM per device.

v0:
```python
import ml_dtypes
import numpy as np

import jax
import jax.numpy as jnp
from jax import lax
from jax.experimental import pallas as pl
from jax.experimental.pallas import tpu as pltpu
from jax.sharding import PartitionSpec as P

SLOTS = 16
PATCH = 64
TILE_R = 256
LANES = 128
UP = 32
DOWN = 64
EXT_F = UP + TILE_R + DOWN
EXT_P = TILE_R + 32
OUT_R = TILE_R + 96
DEAD = -1.0e6
BF = jnp.bfloat16
F32 = jnp.float32
VMEM = pl.BlockSpec(memory_space=pltpu.VMEM)
SMEM = pl.BlockSpec(memory_space=pltpu.SMEM)


def split(x):
    hi = x.astype(BF)
    return hi, (x - hi.astype(F32)).astype(BF)


def dot(a, b):
    return jnp.dot(a, b, preferred_element_type=F32)


def halves(x, axis):
    n = x.shape[axis] // 2
    return lax.slice_in_dim(x, 0, n, axis=axis) + lax.slice_in_dim(x, n, 2 * n, axis=axis)


def np_split(x):
    hi = x.astype(ml_dtypes.bfloat16)
    return hi, (x - hi.astype(np.float64)).astype(ml_dtypes.bfloat16)


def transform_tables():
    theta = np.pi * (2 * np.arange(64) + 1) / 128
    short = np.outer(np.arange(64), theta)
    forward = np.concatenate([np.cos(short), np.sin(short)], 1)
    wide = np.zeros((128, 128))
    wide[32:96] = forward
    full = np.outer(theta, np.arange(128))
    inverse = np.concatenate([np.cos(full), np.sin(full)], 0) / 64
    hi, lo = np_split(wide)
    lane_fwd = np.block([[hi, lo], [hi, lo]])
    hi, lo = np_split(forward.T)
    row_fwd = np.block([[hi, hi], [lo, lo]])
    hi, lo = np_split(inverse)
    lane_inv = np.block([[hi, lo], [hi, lo]])
    hi, lo = np_split(inverse.T)
    row_inv = np.block([[hi, hi], [lo, lo]])
    return lane_fwd, row_fwd, lane_inv, row_inv


def bands_kernel(taps_row, taps_col, row_out, col_out):
    gap = lax.broadcasted_iota(jnp.int32, (112, 128), 1) - lax.broadcasted_iota(jnp.int32, (112, 128), 0)
    band = jnp.zeros((112, 128), F32)
    for t in range(17):
        band = jnp.where(gap == t, taps_row[t], band)
    hi, lo = split(band)
    row_out[0:112, :] = hi
    row_out[112:224, :] = lo
    gap = lax.broadcasted_iota(jnp.int32, (128, 128), 0) - lax.broadcasted_iota(jnp.int32, (128, 128), 1) + 8
    band = jnp.zeros((128, 128), F32)
    for t in range(17):
        band = jnp.where(gap == t, taps_col[t], band)
    hi, lo = split(band)
    pair = jnp.concatenate([hi, lo], 1)
    col_out[...] = jnp.concatenate([pair, pair], 0)


def info_block(win_row, win_col, live_count):
    sub = lax.broadcasted_iota(jnp.int32, (8, LANES), 0)
    lane = lax.broadcasted_iota(jnp.int32, (8, LANES), 1)
    block = jnp.full((8, LANES), DEAD, F32)
    live = live_count[0, 0]
    for k in range(SLOTS):
        half, m = (k % 4) // 2, 2 * (k // 4) + k % 2
        row = jnp.where(k < live, win_row[0, 0, k].astype(F32), DEAD)
        block = jnp.where((sub == half) & (lane == m), row, block)
        block = jnp.where((sub == half + 2) & (lane == m), win_col[0, 0, k].astype(F32), block)
    return block


def pack_rows_kernel(win_row, win_col, live_count, friction, probe, down, up):
    info = info_block(win_row, win_col, live_count)
    down[0:UP, :] = friction[TILE_R - UP : TILE_R, :]
    down[UP : UP + 8, :] = info
    up[0:DOWN, :] = friction[0:DOWN, :]
    up[DOWN : DOWN + 32, :] = probe[0:32, :]
    up[DOWN + 32 : DOWN + 40, :] = info


def pack_cols_kernel(edges, win_row, win_col, live_count, friction, probe, above, below, fa, pa, right, left):
    top, bottom = edges[0] == 0, edges[0] == edges[2] - 1
    info = info_block(win_row, win_col, live_count)
    fa[0:UP, :] = jnp.where(top, 0.0, above[0:UP, :])
    fa[UP : UP + TILE_R, :] = friction[...]
    fa[UP + TILE_R : EXT_F, :] = jnp.where(bottom, 0.0, below[0:DOWN, :])
    pa[0:TILE_R, :] = probe[...]
    pa[TILE_R:EXT_P, :] = jnp.where(bottom, 0.0, below[DOWN : DOWN + 32, :])
    infos = (
        info,
        jnp.where(top, DEAD, above[UP : UP + 8, :]),
        jnp.where(bottom, DEAD, below[DOWN + 32 : DOWN + 40, :]),
    )

    def packed(ref, rows, width, start):
        count = LANES // width
        part = rows // count
        lane = lax.broadcasted_iota(jnp.int32, (part, LANES), 1) // width
        total = jnp.zeros((part, LANES), F32)
        for i in range(count):
            piece = pltpu.roll(ref[i * part : (i + 1) * part, :], (width * i - start) % LANES, 1)
            total = jnp.where(lane == i, piece, total)
        return total

    right[0:88, :] = packed(fa, EXT_F, 32, 96)
    left[0:176, :] = packed(fa, EXT_F, 64, 0)
    left[176:248, :] = packed(pa, EXT_P, 32, 0)
    for n, block in enumerate(infos):
        right[88 + 8 * n : 96 + 8 * n, :] = block
        left[248 + 8 * n : 256 + 8 * n, :] = block


def window(a, b, start):
    turn = lax.rem(256 - start, 128)
    lane = lax.broadcasted_iota(jnp.int32, a.shape, 1) + start
    return jnp.where((lane >= 0) & (lane < LANES), pltpu.roll(a, turn, 1), pltpu.roll(b, turn, 1))


def core_kernel(
    edges, win_row, win_col, live_count, fa, pa, above, below, from_left, from_right, bands, col_band,
    lane_fwd, row_fwd, lane_inv, row_inv, oa, ob, fb, pb, fw, y2, z,
):
    top, bottom = edges[0] == 0, edges[0] == edges[2] - 1
    leftmost, rightmost = edges[1] == 0, edges[1] == edges[3] - 1
    lane = lax.broadcasted_iota(jnp.int32, (8, LANES), 1)
    for i in range(4):
        rows = slice(88 * i, 88 * i + 88)
        rim = pltpu.roll(from_left[0:88, :], 96 - 32 * i, 1)
        lane88 = lax.broadcasted_iota(jnp.int32, (88, LANES), 1)
        near = from_right[88 * (i % 2) : 88 * (i % 2) + 88, :]
        if i >= 2:
            near = pltpu.roll(near, 64, 1)
        keep_l = (lane88 >= 96) & jnp.logical_not(leftmost)
        keep_r = (lane88 < 64) & jnp.logical_not(rightmost)
        fb[rows, :] = jnp.where(keep_l, rim, jnp.where(keep_r, near, 0.0))
        lane72 = lax.broadcasted_iota(jnp.int32, (72, LANES), 1)
        near = pltpu.roll(from_right[176:248, :], (128 - 32 * i) % 128, 1)
        pb[72 * i : 72 * i + 72, :] = jnp.where((lane72 < 32) & jnp.logical_not(rightmost), near, 0.0)
    sub = lax.broadcasted_iota(jnp.int32, (8, LANES), 0)
    is_row = sub < 2
    cand = jnp.full((8, LANES), DEAD, F32)
    tile = 0
    for dc, mine in ((0, None), (-1, from_left), (1, from_right)):
        for n, dr in enumerate((0, -1, 1)):
            if dc == 0:
                if dr == 0:
                    block = info_block(win_row, win_col, live_count)
                elif dr == -1:
                    block = jnp.where(top, DEAD, above[UP : UP + 8, :])
                else:
                    block = jnp.where(bottom, DEAD, below[DOWN + 32 : DOWN + 40, :])
            elif dc == -1:
                block = jnp.where(leftmost, DEAD, from_left[88 + 8 * n : 96 + 8 * n, :])
            else:
                block = jnp.where(rightmost, DEAD, from_right[248 + 8 * n : 256 + 8 * n, :])
            block = block + jnp.where(is_row, float(TILE_R * dr), float(LANES * dc))
            cand = jnp.where(lane // 8 == tile, pltpu.roll(block, 8 * tile, 1), cand)
            tile += 1
    for k in range(SLOTS):
        rows = pl.ds(win_row[0, 0, k], 128)
        fw[k] = window(fa[rows, :], fb[rows, :], win_col[0, 0, k] - 32)
    sub_f = lax.broadcasted_iota(jnp.int32, (128, 128), 0).astype(F32)
    lane1 = lax.broadcasted_iota(jnp.int32, (1, LANES), 1)
    for k in range(0, SLOTS, 2):
        combs = []
        for kk in (k, k + 1):
            half = (kk % 4) // 2
            mine = lax.rem(lane1, 2) == kk % 2
            p = jnp.where(mine, cand[half : half + 1] - (win_row[0, 0, kk] - 64).astype(F32), -1.0)
            q = jnp.where(mine, cand[half + 2 : half + 3] - (win_col[0, 0, kk] - 64).astype(F32), -1.0)
            at_row = (sub_f == p).astype(F32).astype(BF)
            at_col = jnp.where(sub_f == q, 64.0, 0.0).astype(BF)
            comb = lax.dot_general(at_row, at_col, (((1,), (1,)), ((), ())), preferred_element_type=F32)
            combs.append(comb.astype(BF))
        t = halves(dot(bands[...], jnp.concatenate(combs, 1)), 0)
        for m in range(2):
            hi, lo = split(t[:, 128 * m : 128 * m + 128])
            y2[pl.ds((k + m) * 112, 112), :] = jnp.concatenate([hi, lo], 1)
    first, n = 8, 112
    while True:
        o = halves(dot(y2[0 : SLOTS * n, :], col_band[...]), 1)
        o = o.reshape(SLOTS, n, 128) * fw[:, first : first + n, :]
        if n == PATCH:
            break
        hi, lo = split(o)
        both = jnp.concatenate([hi, lo], 1)
        m = n - 16
        band_hi, band_lo = bands[0:m, 0:n], bands[112 : 112 + m, 0:n]
        lhs = jnp.concatenate(
            [jnp.concatenate([band_hi, band_hi], 1), jnp.concatenate([band_lo, band_lo], 1)], 0
        )
        for k in range(0, SLOTS, 2):
            t = halves(dot(lhs, jnp.concatenate([both[k], both[k + 1]], 1)), 0)
            for i in range(2):
                hi, lo = split(t[:, 128 * i : 128 * i + 128])
                y2[pl.ds((k + i) * m, m), :] = jnp.concatenate([hi, lo], 1)
        first, n = first + 8, m

    def lane_transform(x):
        hi, lo = split(x)
        return split(halves(dot(jnp.concatenate([hi, lo], 1), lane_fwd[...]), 1))

    ker_hi, ker_lo = lane_transform(o.reshape(SLOTS * PATCH, 128))
    for k in range(SLOTS):
        rows = pl.ds(win_row[0, 0, k], PATCH)
        z[pl.ds(k * PATCH, PATCH), :] = window(pa[rows, :], pb[rows, :], win_col[0, 0, k] - 32)
    win_hi, win_lo = lane_transform(z[...])
    left_half = lax.broadcasted_iota(jnp.int32, (PATCH, 128), 1) < 64
    sign = jnp.where(left_half, -1.0, 1.0)

    def pair(t):
        a, b = t[:64], pltpu.roll(t[64:], 64, 1) * sign
        return a + b, a - b

    def times(a, b):
        ar, br = pltpu.roll(a, 64, 1), pltpu.roll(b, 64, 1)
        return jnp.where(left_half, a, ar) * b + jnp.where(left_half, -ar, a) * br

    def spectrum(k):
        s = slice(PATCH * k, PATCH * k + PATCH)
        w = jnp.concatenate(
            [jnp.concatenate([ker_hi[s], win_hi[s]], 1), jnp.concatenate([ker_lo[s], win_lo[s]], 1)], 0
        )
        t = halves(dot(row_fwd[...], w), 0)
        k1, k2 = pair(t[:, :128])
        w1, w2 = pair(t[:, 128:])
        p1, p2 = times(k1, w1), times(k2, w2)
        return jnp.concatenate([(p1 + p2) * 0.5, pltpu.roll((p1 - p2) * (0.5 * sign), 64, 1)], 0)

    oa[...] = jnp.zeros_like(oa)
    ob[...] = jnp.zeros_like(ob)
    lane128 = lax.broadcasted_iota(jnp.int32, (128, 128), 1)
    for k in range(0, SLOTS, 2):
        hi, lo = split(jnp.concatenate([spectrum(k), spectrum(k + 1)], 0))
        e = halves(dot(jnp.concatenate([hi, lo], 1), lane_inv[...]), 1)
        hi, lo = split(e)
        w = jnp.concatenate(
            [jnp.concatenate([hi[:128], lo[:128]], 0), jnp.concatenate([hi[128:], lo[128:]], 0)], 1
        )
        t = halves(dot(row_inv[...], w), 0)
        for m in range(2):
            kk = k + m
            col = win_col[0, 0, kk]
            live = jnp.where(kk < live_count[0, 0], 1.0, 0.0)
            patch = pltpu.roll(t[:, 128 * m : 128 * m + 128] * live, col, 1)
            rows = pl.ds(win_row[0, 0, kk], 128)
            oa[rows, :] += jnp.where(lane128 >= col, patch, 0.0)
            ob[rows, :] += jnp.where(lane128 < col, patch, 0.0)


def shape(rows, dtype=F32, cols=LANES):
    return jax.ShapeDtypeStruct((rows, cols), dtype)


def ring(x, axis, by):
    count = lax.axis_size(axis)
    return lax.ppermute(x, axis, [(i, (i + by) % count) for i in range(count)])


def per_device(friction, taps_row, taps_col, probe, win_row, win_col, live_count):
    params = pltpu.CompilerParams(vmem_limit_bytes=40 * 2**20)
    edges = jnp.stack(
        [lax.axis_index("mx"), lax.axis_index("my"), lax.axis_size("mx"), lax.axis_size("my")]
    ).astype(jnp.int32)
    down, up = pl.pallas_call(
        pack_rows_kernel,
        out_shape=[shape(UP + 8), shape(DOWN + 40)],
        in_specs=[SMEM] * 3 + [VMEM] * 2,
        out_specs=[VMEM] * 2,
        compiler_params=params,
    )(win_row, win_col, live_count, friction, probe)
    above = ring(down, "mx", 1)
    below = ring(up, "mx", -1)
    bands, col_band = pl.pallas_call(
        bands_kernel,
        out_shape=[shape(224, BF), shape(256, BF, 256)],
        in_specs=[SMEM] * 2,
        out_specs=[VMEM] * 2,
        compiler_params=params,
    )(taps_row, taps_col)
    fa, pa, right, left = pl.pallas_call(
        pack_cols_kernel,
        out_shape=[shape(EXT_F), shape(EXT_P), shape(112), shape(272)],
        in_specs=[SMEM] * 4 + [VMEM] * 4,
        out_specs=[VMEM] * 4,
        compiler_params=params,
    )(edges, win_row, win_col, live_count, friction, probe, above, below)
    from_left = ring(right, "my", 1)
    from_right = ring(left, "my", -1)
    tables = [jnp.asarray(t) for t in transform_tables()]
    oa, ob = pl.pallas_call(
        core_kernel,
        out_shape=[shape(OUT_R)] * 2,
        in_specs=[SMEM] * 4 + [VMEM] * 12,
        out_specs=[VMEM] * 2,
        scratch_shapes=[
            pltpu.VMEM((EXT_F, LANES), F32),
            pltpu.VMEM((EXT_P, LANES), F32),
            pltpu.VMEM((SLOTS, 128, LANES), F32),
            pltpu.VMEM((SLOTS * 112, 256), BF),
            pltpu.VMEM((SLOTS * PATCH, LANES), F32),
        ],
        compiler_params=params,
    )(
        edges, win_row, win_col, live_count, fa, pa, above, below, from_left, from_right, bands, col_band, *tables
    )
    spill = ring(ob, "my", 1)
    total = oa + jnp.where(lax.axis_index("my") > 0, spill, 0.0)
    lower = ring(total[TILE_R:], "mx", 1)
    lower = jnp.where(lax.axis_index("mx") > 0, lower, 0.0)
    return total[:TILE_R] + jnp.pad(lower, ((0, TILE_R - lower.shape[0]), (0, 0)))


def solution(mesh):
    placed = (
        P("mx", "my"),
        P(),
        P(),
        P("mx", "my"),
        P("mx", "my", None),
        P("mx", "my", None),
        P("mx", "my"),
    )
    return jax.shard_map(
        per_device, mesh=mesh, in_specs=placed, out_specs=P("mx", "my"), check_vma=False
    )
```

profile of v0, /device:TPU:96, one launch (start us, length us, event | category | flops | bytes accessed | tf_op | source)
XLA Modules:
  0.0 46.4 jit_solution(16960841264369012922)
XLA Ops:
  0.0 0.0 copy-start.9
  0.0 0.0 copy-start.8
  0.7 0.0 copy-done.9
  0.7 0.0 copy-done.8
  0.7 0.0 copy-start
  0.7 0.9 %copy-done = f32[256,128]{1,0:T(8,128)S(1)} copy-done((f32[256,128]{1,0:T(8,128)S(1)}, f32[256,128]{1,0:T(8,128)}, u32[]{:S(2)}) %copy-start) | copy-done | bytes 131096
  1.6 0.0 copy-start.2
  1.6 0.9 %copy-done.2 = f32[256,128]{1,0:T(8,128)S(1)} copy-done((f32[256,128]{1,0:T(8,128)S(1)}, f32[256,128]{1,0:T(8,128)}, u32[]{:S(2)}) %copy-start.2) | copy-done | bytes 131096
  2.5 0.0 copy-start.1
  2.5 0.0 copy-start.3
  2.5 0.6 %shard_map.109 = (f32[40,128]{1,0:T(8,128)S(1)}, f32[104,128]{1,0:T(8,128)S(1)}) custom-call(s32[1,1,16]{2,1,0:T(1,128)S(1)} %copy-done.8, s32[1,1,16]{2,1,0:T(1,128)S(1)} %copy-done.9, s32[1,1]{1,0:T(1,128)S(6)} %copy.12.live_count, f32[256,128]{1,0:T(8,128)S(1)} %copy-done, f32[256,128]{1,0:T(8,128)S(1)} %copy-done.2), custom_call_target="tpu_custom_call" | custom-call | tf_op jit(solution)/shard_map/pallas_call | solution.py:288
  3.1 3.2 %collective-permute-start = (f32[40,128]{1,0:T(8,128)S(1)}, f32[40,128]{1,0:T(8,128)S(1)}, u32[]{:S(2)}, u32[]{:S(2)}) collective-permute-start(f32[40,128]{1,0:T(8,128)S(1)} %get-tuple-element.15), channel_id=1, source_target_pairs={{0,32},{32,64},{64,96},{96,128},{128,160},{160,192},{192,224},{224... | collective-permute-start | bytes 61448 | tf_op jit(solution)/shard_map/ppermute | solution.py:280
  6.3 0.0 collective-permute-start.1
  6.3 0.1 pad_add_fusion.edges
  6.4 0.0 copy-start.4
  6.4 0.0 copy-start.5
  6.4 0.0 copy-start.7
  6.4 1.4 %collective-permute-done.above = f32[40,128]{1,0:T(8,128)S(1)} collective-permute-done((f32[40,128]{1,0:T(8,128)S(1)}, f32[40,128]{1,0:T(8,128)S(1)}, u32[]{:S(2)}, u32[]{:S(2)}) %collective-permute-start) | collective-permute-done | bytes 20512 | tf_op jit(solution)/shard_map/ppermute | solution.py:280
  7.8 3.9 %collective-permute-done.1.below = f32[104,128]{1,0:T(8,128)S(1)} collective-permute-done((f32[104,128]{1,0:T(8,128)S(1)}, f32[104,128]{1,0:T(8,128)S(1)}, u32[]{:S(2)}, u32[]{:S(2)}) %collective-permute-start.1) | collective-permute-done | bytes 53280 | tf_op jit(solution)/shard_map/ppermute | solution.py:280
  11.7 0.0 copy-done.1
  11.7 0.0 copy-done.3
  11.7 0.7 %shard_map.110 = (f32[352,128]{1,0:T(8,128)S(1)}, f32[288,128]{1,0:T(8,128)S(1)}, f32[112,128]{1,0:T(8,128)S(1)}, f32[272,128]{1,0:T(8,128)S(1)}) custom-call(s32[4]{0:T(128)S(1)} %pad_add_fusion.edges, s32[1,1,16]{2,1,0:T(1,128)S(1)} %copy-done.8, s32[1,1,16]{2,1,0:T(1,128)S(1)} %copy-done.9, s32[1,1]{1,0:T(1,128)S(6)} %copy.12.live_count, ...), custom_call_target="tpu_custom_call" | custom-call | tf_op jit(solution)/shard_map/pallas_call | solution.py:304
  12.4 0.0 copy-start.10
  12.4 0.0 copy-start.11
  12.4 3.3 %collective-permute-start.3 = (f32[272,128]{1,0:T(8,128)S(1)}, f32[272,128]{1,0:T(8,128)S(1)}, u32[]{:S(2)}, u32[]{:S(2)}) collective-permute-start(f32[272,128]{1,0:T(8,128)S(1)} %get-tuple-element.20), channel_id=1, source_target_pairs={{0,31},{1,0},{2,1},{3,2},{4,3},{5,4},{6,5},{7,6},{8,7},{9,8},{10,9... | collective-permute-start | bytes 417800 | tf_op jit(solution)/shard_map/ppermute | solution.py:280
  15.7 0.0 collective-permute-start.2
  15.7 0.0 copy-done.10
  15.7 0.0 copy-done.11
  15.7 0.7 %shard_map.111 = (bf16[224,128]{1,0:T(8,128)(2,1)S(1)}, bf16[256,256]{1,0:T(8,128)(2,1)S(1)}) custom-call(f32[17]{0:T(128)S(1)} %copy-done.10, f32[17]{0:T(128)S(1)} %copy-done.11), custom_call_target="tpu_custom_call" | custom-call | tf_op jit(solution)/shard_map/pallas_call | solution.py:297
  16.4 6.2 %collective-permute-done.2.from_left = f32[112,128]{1,0:T(8,128)S(1)} collective-permute-done((f32[112,128]{1,0:T(8,128)S(1)}, f32[112,128]{1,0:T(8,128)S(1)}, u32[]{:S(2)}, u32[]{:S(2)}) %collective-permute-start.2) | collective-permute-done | bytes 57376 | tf_op jit(solution)/shard_map/ppermute | solution.py:280
  22.6 0.0 collective-permute-done.3.from_right
  22.6 0.0 copy-done.4
  22.6 0.0 copy-done.5
  22.6 0.0 copy-done.7
  22.6 0.0 copy-start.6
  22.7 0.9 %copy-done.6 = bf16[256,256]{1,0:T(8,128)(2,1)S(1)} copy-done((bf16[256,256]{1,0:T(8,128)(2,1)S(1)}, bf16[256,256]{1,0:T(8,128)(2,1)}, u32[]{:S(2)}) %copy-start.6) | copy-done | bytes 131096
  23.6 9.7 %shard_map.112 = (f32[352,128]{1,0:T(8,128)S(1)}, f32[352,128]{1,0:T(8,128)S(1)}) custom-call(s32[4]{0:T(128)S(1)} %pad_add_fusion.edges, s32[1,1,16]{2,1,0:T(1,128)S(1)} %copy-done.8, s32[1,1,16]{2,1,0:T(1,128)S(1)} %copy-done.9, s32[1,1]{1,0:T(1,128)S(6)} %copy.12.live_count, f32[352,128]{1,0:T(8,128)S(1)} %get-tuple-element.17.fa, ...), custom_call_target="tpu_custom_call" | custom-call | tf_op jit(solution)/shard_map/pallas_call | solution.py:314
  33.3 0.1 collective-permute-start.4
  33.3 8.2 %collective-permute-done.4 = f32[352,128]{1,0:T(8,128)S(1)} collective-permute-done((f32[352,128]{1,0:T(8,128)S(1)}, f32[352,128]{1,0:T(8,128)S(1)}, u32[]{:S(2)}, u32[]{:S(2)}) %collective-permute-start.4) | collective-permute-done | bytes 180256 | tf_op jit(solution)/shard_map/ppermute | solution.py:280
  41.6 0.1 collective-permute-start.5
  41.7 4.1 %collective-permute-done.5 = f32[96,128]{1,0:T(8,128)S(1)} collective-permute-done((f32[96,128]{1,0:T(8,128)S(1)}, f32[96,128]{1,0:T(8,128)S(1)}, u32[]{:S(2)}, u32[]{:S(2)}) %collective-permute-start.5) | collective-permute-done | bytes 49184 | tf_op jit(solution)/shard_map/ppermute | solution.py:280
  45.8 0.7 %slice_add_fusion = f32[256,128]{1,0:T(8,128)} fusion(f32[352,128]{1,0:T(8,128)S(1)} %select_add_fusion, f32[96,128]{1,0:T(8,128)S(1)} %broadcast_select_fusion), kind=kLoop, calls=%fused_computation.1 | loop fusion | flops 32768 | bytes 311296 | tf_op jit(solution)/shard_map/add | solution.py:334
  (3 shorter events, 0.0 us)
Async XLA Ops:
  0.0 0.7 %copy-start.9 = (s32[1,1,16]{2,1,0:T(1,128)S(1)}, s32[1,1,16]{2,1,0:T(1,128)}, u32[]{:S(2)}) copy-start(s32[1,1,16]{2,1,0:T(1,128)} %win_col.5) | copy-start | bytes 196
  0.0 0.7 %copy-start.8 = (s32[1,1,16]{2,1,0:T(1,128)S(1)}, s32[1,1,16]{2,1,0:T(1,128)}, u32[]{:S(2)}) copy-start(s32[1,1,16]{2,1,0:T(1,128)} %win_row.5) | copy-start | bytes 196
  0.7 0.9 %copy-start = (f32[256,128]{1,0:T(8,128)S(1)}, f32[256,128]{1,0:T(8,128)}, u32[]{:S(2)}) copy-start(f32[256,128]{1,0:T(8,128)} %friction.3) | copy-start | bytes 393220
  1.6 0.9 %copy-start.2 = (f32[256,128]{1,0:T(8,128)S(1)}, f32[256,128]{1,0:T(8,128)}, u32[]{:S(2)}) copy-start(f32[256,128]{1,0:T(8,128)} %probe.3) | copy-start | bytes 393220
  2.5 9.1 %copy-start.1 = (f32[256,128]{1,0:T(8,128)S(1)}, f32[256,128]{1,0:T(8,128)}, u32[]{:S(2)}) copy-start(f32[256,128]{1,0:T(8,128)} %friction.3) | copy-start | bytes 393220
  2.5 9.1 %copy-start.3 = (f32[256,128]{1,0:T(8,128)S(1)}, f32[256,128]{1,0:T(8,128)}, u32[]{:S(2)}) copy-start(f32[256,128]{1,0:T(8,128)} %probe.3) | copy-start | bytes 393220
  3.1 4.7 %collective-permute-start = (f32[40,128]{1,0:T(8,128)S(1)}, f32[40,128]{1,0:T(8,128)S(1)}, u32[]{:S(2)}, u32[]{:S(2)}) collective-permute-start(f32[40,128]{1,0:T(8,128)S(1)} %get-tuple-element.15), channel_id=1, source_target_pairs={{0,32},{32,64},{64,96},{96,128},{128,160},{160,192},{192,224},{224... | collective-permute-start | bytes 61448 | tf_op jit(solution)/shard_map/ppermute | solution.py:280
  6.3 5.3 %collective-permute-start.1 = (f32[104,128]{1,0:T(8,128)S(1)}, f32[104,128]{1,0:T(8,128)S(1)}, u32[]{:S(2)}, u32[]{:S(2)}) collective-permute-start(f32[104,128]{1,0:T(8,128)S(1)} %get-tuple-element.16), channel_id=1, source_target_pairs={{0,224},{32,0},{64,32},{96,64},{128,96},{160,128},{192,160},{224,1... | collective-permute-start | bytes 159752 | tf_op jit(solution)/shard_map/ppermute | solution.py:280
  6.4 16.2 %copy-start.4 = (bf16[256,256]{1,0:T(8,128)(2,1)S(1)}, bf16[256,256]{1,0:T(8,128)(2,1)}, u32[]{:S(2)}) copy-start(bf16[256,256]{1,0:T(8,128)(2,1)} %constant.29.clone.row_inv) | copy-start | bytes 393220
  6.4 16.2 %copy-start.5 = (bf16[256,256]{1,0:T(8,128)(2,1)S(1)}, bf16[256,256]{1,0:T(8,128)(2,1)}, u32[]{:S(2)}) copy-start(bf16[256,256]{1,0:T(8,128)(2,1)} %constant.28.clone.lane_inv) | copy-start | bytes 393220
  6.4 16.2 %copy-start.7 = (bf16[256,128]{1,0:T(8,128)(2,1)S(1)}, bf16[256,128]{1,0:T(8,128)(2,1)}, u32[]{:S(2)}) copy-start(bf16[256,128]{1,0:T(8,128)(2,1)} %constant.27.clone.row_fwd) | copy-start | bytes 196612
  12.4 3.3 %copy-start.10 = (f32[17]{0:T(128)S(1)}, f32[17]{0:T(128)}, u32[]{:S(2)}) copy-start(f32[17]{0:T(128)} %taps_row.1) | copy-start | bytes 208
  12.4 3.3 %copy-start.11 = (f32[17]{0:T(128)S(1)}, f32[17]{0:T(128)}, u32[]{:S(2)}) copy-start(f32[17]{0:T(128)} %taps_col.1) | copy-start | bytes 208
  12.4 10.2 %collective-permute-start.3 = (f32[272,128]{1,0:T(8,128)S(1)}, f32[272,128]{1,0:T(8,128)S(1)}, u32[]{:S(2)}, u32[]{:S(2)}) collective-permute-start(f32[272,128]{1,0:T(8,128)S(1)} %get-tuple-element.20), channel_id=1, source_target_pairs={{0,31},{1,0},{2,1},{3,2},{4,3},{5,4},{6,5},{7,6},{8,7},{9,8},{10,9... | collective-permute-start | bytes 417800 | tf_op jit(solution)/shard_map/ppermute | solution.py:280
  15.7 6.9 %collective-permute-start.2 = (f32[112,128]{1,0:T(8,128)S(1)}, f32[112,128]{1,0:T(8,128)S(1)}, u32[]{:S(2)}, u32[]{:S(2)}) collective-permute-start(f32[112,128]{1,0:T(8,128)S(1)} %get-tuple-element.19), channel_id=1, source_target_pairs={{0,1},{1,2},{2,3},{3,4},{4,5},{5,6},{6,7},{7,8},{8,9},{9,10},{10,1... | collective-permute-start | bytes 172040 | tf_op jit(solution)/shard_map/ppermute | solution.py:280
  22.6 0.9 %copy-start.6 = (bf16[256,256]{1,0:T(8,128)(2,1)S(1)}, bf16[256,256]{1,0:T(8,128)(2,1)}, u32[]{:S(2)}) copy-start(bf16[256,256]{1,0:T(8,128)(2,1)} %constant.26.clone.lane_fwd) | copy-start | bytes 393220
  33.3 8.3 %collective-permute-start.4 = (f32[352,128]{1,0:T(8,128)S(1)}, f32[352,128]{1,0:T(8,128)S(1)}, u32[]{:S(2)}, u32[]{:S(2)}) collective-permute-start(f32[352,128]{1,0:T(8,128)S(1)} %get-tuple-element.24), channel_id=1, source_target_pairs={{0,1},{1,2},{2,3},{3,4},{4,5},{5,6},{6,7},{7,8},{8,9},{9,10},{10,1... | collective-permute-start | bytes 540680 | tf_op jit(solution)/shard_map/ppermute | solution.py:280
  41.6 4.2 %collective-permute-start.5 = (f32[96,128]{1,0:T(8,128)S(1)}, f32[96,128]{1,0:T(8,128)S(1)}, u32[]{:S(2)}, u32[]{:S(2)}) collective-permute-start(f32[96,128]{1,0:T(8,128)S(1)} %slice.9), channel_id=1, source_target_pairs={{0,32},{32,64},{64,96},{96,128},{128,160},{160,192},{192,224},{224... | collective-permute-start | bytes 147464 | tf_op jit(solution)/shard_map/ppermute | solution.py:280
where the time goes:
time: 46.6 us; the launch traced here: 46.4 us
  waiting for transfers between devices  23.7 us (51%)
  Pallas kernels  11.7 us (25%)
  starting transfers between devices  6.67 us (14%)
  local copies, waits for them, and re-layouts  2.74 us (6%)
  between operations  0.82 us (2%)
  other arithmetic  0.77 us (2%)
    ppermute x6, waiting for transfers between devices, ring(): return lax.ppermute(x, axis, [(i, (i + by) % count) for i in range(count)])  23.7 us
    pallas_call x1, Pallas kernels, per_device(): pl.pallas_call(core_kernel, out_shape=[shape(OUT_R)] * 2, in_specs=[SMEM]...  9.69 us
    ppermute x6, starting transfers between devices, ring(): return lax.ppermute(x, axis, [(i, (i + by) % count) for i in range(count)])  6.67 us
    unnamed x24, local copies, waits for them, and re-layouts  2.74 us
  transfers between devices with their start and end apart: 6, of which 5 were waited for; matrix products, arithmetic and copies ran while one was open for 0% of the time, Pallas kernels for 2%

commit v1 on v0

--- a/solution.py
+++ b/solution.py
@@ -22,6 +22,7 @@
 F32 = jnp.float32
 VMEM = pl.BlockSpec(memory_space=pltpu.VMEM)
 SMEM = pl.BlockSpec(memory_space=pltpu.SMEM)
+ANY = pl.BlockSpec(memory_space=pltpu.HBM)
 
 
 def split(x):
@@ -59,10 +60,12 @@
     lane_inv = np.block([[hi, lo], [hi, lo]])
     hi, lo = np_split(inverse.T)
     row_inv = np.block([[hi, hi], [lo, lo]])
-    return lane_fwd, row_fwd, lane_inv, row_inv
-
-
-def bands_kernel(taps_row, taps_col, row_out, col_out):
+    return np.concatenate([lane_fwd, lane_inv, row_inv, row_fwd], 1)
+
+
+def bands_kernel(taps_row, taps_col, tables_in, row_out, col_out, tables, sem):
+    table_copy = pltpu.make_async_copy(tables_in, tables, sem)
+    table_copy.start()
     gap = lax.broadcasted_iota(jnp.int32, (112, 128), 1) - lax.broadcasted_iota(jnp.int32, (112, 128), 0)
     band = jnp.zeros((112, 128), F32)
     for t in range(17):
@@ -77,43 +80,69 @@
     hi, lo = split(band)
     pair = jnp.concatenate([hi, lo], 1)
     col_out[...] = jnp.concatenate([pair, pair], 0)
-
-
-def info_block(win_row, win_col, live_count):
-    sub = lax.broadcasted_iota(jnp.int32, (8, LANES), 0)
-    lane = lax.broadcasted_iota(jnp.int32, (8, LANES), 1)
-    block = jnp.full((8, LANES), DEAD, F32)
-    live = live_count[0, 0]
-    for k in range(SLOTS):
-        half, m = (k % 4) // 2, 2 * (k // 4) + k % 2
-        row = jnp.where(k < live, win_row[0, 0, k].astype(F32), DEAD)
-        block = jnp.where((sub == half) & (lane == m), row, block)
-        block = jnp.where((sub == half + 2) & (lane == m), win_col[0, 0, k].astype(F32), block)
-    return block
-
-
-def pack_rows_kernel(win_row, win_col, live_count, friction, probe, down, up):
-    info = info_block(win_row, win_col, live_count)
-    down[0:UP, :] = friction[TILE_R - UP : TILE_R, :]
-    down[UP : UP + 8, :] = info
-    up[0:DOWN, :] = friction[0:DOWN, :]
-    up[DOWN : DOWN + 32, :] = probe[0:32, :]
-    up[DOWN + 32 : DOWN + 40, :] = info
-
-
-def pack_cols_kernel(edges, win_row, win_col, live_count, friction, probe, above, below, fa, pa, right, left):
-    top, bottom = edges[0] == 0, edges[0] == edges[2] - 1
-    info = info_block(win_row, win_col, live_count)
-    fa[0:UP, :] = jnp.where(top, 0.0, above[0:UP, :])
+    table_copy.wait()
+
+
+def own_index(axis):
+    return lax.axis_index(axis), lax.axis_size(axis)
+
+
+def pack_rows_kernel(win_row, win_col, live_count, friction, probe, even_out, odd_out, rows, cols, count, sems):
+    def fetch(down, up):
+        return [
+            pltpu.make_async_copy(friction.at[pl.ds(TILE_R - UP, UP)], down.at[pl.ds(0, UP)], sems.at[3]),
+            pltpu.make_async_copy(friction.at[pl.ds(0, DOWN)], up.at[pl.ds(0, DOWN)], sems.at[4]),
+            pltpu.make_async_copy(probe.at[pl.ds(0, 32)], up.at[pl.ds(DOWN, 32)], sems.at[5]),
+        ]
+
+    is_even = lax.rem(lax.axis_index("mx"), 2) == 0
+
+    @pl.when(is_even)
+    def _():
+        for copy in fetch(even_out, odd_out):
+            copy.start()
+
+    @pl.when(jnp.logical_not(is_even))
+    def _():
+        for copy in fetch(odd_out, even_out):
+            copy.start()
+
+    copies = [
+        pltpu.make_async_copy(win_row.at[0], rows, sems.at[0]),
+        pltpu.make_async_copy(win_col.at[0], cols, sems.at[1]),
+        pltpu.make_async_copy(live_count, count, sems.at[2]),
+    ]
+    for copy in copies:
+        copy.start()
+    for copy in copies:
+        copy.wait()
+    lane = lax.broadcasted_iota(jnp.int32, (1, SLOTS), 1)
+    live = lane < count[...]
+    row = jnp.where(live, rows[...].astype(F32), DEAD)
+    col = cols[...].astype(F32)
+    wide = jnp.concatenate([jnp.concatenate([x, jnp.zeros((1, LANES - SLOTS), F32)], 1) for x in (row, col)], 0)
+    turned = pltpu.roll(wide, LANES - 2, 1)
+    info = jnp.concatenate([wide[0:1], turned[0:1], wide[1:2], turned[1:2], jnp.zeros((4, LANES), F32)], 0)
+    even_out[96:104, :] = info
+    odd_out[96:104, :] = info
+    for copy in fetch(even_out, odd_out):
+        copy.wait()
+
+
+def pack_cols_kernel(friction, probe, mine, row_even, row_odd, fa, pa, infos, even_out, odd_out):
+    at, count = own_index("mx")
+    top, bottom = at == 0, at == count - 1
+    is_even = lax.rem(at, 2) == 0
+    above = jnp.where(is_even, row_odd[...], row_even[...])
+    below = jnp.where(is_even, row_even[...], row_odd[...])
+    fa[0:UP, :] = jnp.where(top, 0.0, above[0:UP])
     fa[UP : UP + TILE_R, :] = friction[...]
-    fa[UP + TILE_R : EXT_F, :] = jnp.where(bottom, 0.0, below[0:DOWN, :])
+    fa[UP + TILE_R : EXT_F, :] = jnp.where(bottom, 0.0, below[0:DOWN])
     pa[0:TILE_R, :] = probe[...]
-    pa[TILE_R:EXT_P, :] = jnp.where(bottom, 0.0, below[DOWN : DOWN + 32, :])
-    infos = (
-        info,
-        jnp.where(top, DEAD, above[UP : UP + 8, :]),
-        jnp.where(bottom, DEAD, below[DOWN + 32 : DOWN + 40, :]),
-    )
+    pa[TILE_R:EXT_P, :] = jnp.where(bottom, 0.0, below[DOWN : DOWN + 32])
+    infos[0:8, :] = mine[96:104, :]
+    infos[8:16, :] = jnp.where(top, DEAD, above[96:104])
+    infos[16:24, :] = jnp.where(bottom, DEAD, below[96:104])
 
     def packed(ref, rows, width, start):
         count = LANES // width
@@ -125,12 +154,22 @@
             total = jnp.where(lane == i, piece, total)
         return total
 
-    right[0:88, :] = packed(fa, EXT_F, 32, 96)
-    left[0:176, :] = packed(fa, EXT_F, 64, 0)
-    left[176:248, :] = packed(pa, EXT_P, 32, 0)
-    for n, block in enumerate(infos):
-        right[88 + 8 * n : 96 + 8 * n, :] = block
-        left[248 + 8 * n : 256 + 8 * n, :] = block
+    def fill(right, left):
+        right[0:88, :] = packed(fa, EXT_F, 32, 96)
+        left[0:176, :] = packed(fa, EXT_F, 64, 0)
+        left[176:248, :] = packed(pa, EXT_P, 32, 0)
+        right[248:272, :] = infos[...]
+        left[248:272, :] = infos[...]
+
+    is_even = lax.rem(lax.axis_index("my"), 2) == 0
+
+    @pl.when(is_even)
+    def _():
+        fill(even_out, odd_out)
+
+    @pl.when(jnp.logical_not(is_even))
+    def _():
+        fill(odd_out, even_out)
 
 
 def window(a, b, start):
@@ -140,11 +179,21 @@
 
 
 def core_kernel(
-    edges, win_row, win_col, live_count, fa, pa, above, below, from_left, from_right, bands, col_band,
-    lane_fwd, row_fwd, lane_inv, row_inv, oa, ob, fb, pb, fw, y2, z,
+    win_row_in, win_col_in, live_in, fa, pa, infos, even_in, odd_in, bands, col_band, tables,
+    oa, ob, fb, pb, fw, y2, z, win_row, win_col, live_count, from_left, from_right, sems,
 ):
-    top, bottom = edges[0] == 0, edges[0] == edges[2] - 1
-    leftmost, rightmost = edges[1] == 0, edges[1] == edges[3] - 1
+    scalar_copies = [
+        pltpu.make_async_copy(win_row_in, win_row, sems.at[1]),
+        pltpu.make_async_copy(win_col_in, win_col, sems.at[2]),
+        pltpu.make_async_copy(live_in, live_count, sems.at[3]),
+    ]
+    for copy in scalar_copies:
+        copy.start()
+    at_col, col_count = own_index("my")
+    leftmost, rightmost = at_col == 0, at_col == col_count - 1
+    is_even = lax.rem(at_col, 2) == 0
+    from_left[...] = jnp.where(is_even, odd_in[...], even_in[...])
+    from_right[...] = jnp.where(is_even, even_in[...], odd_in[...])
     lane = lax.broadcasted_iota(jnp.int32, (8, LANES), 1)
     for i in range(4):
         rows = slice(88 * i, 88 * i + 88)
@@ -159,26 +208,23 @@
         lane72 = lax.broadcasted_iota(jnp.int32, (72, LANES), 1)
         near = pltpu.roll(from_right[176:248, :], (128 - 32 * i) % 128, 1)
         pb[72 * i : 72 * i + 72, :] = jnp.where((lane72 < 32) & jnp.logical_not(rightmost), near, 0.0)
-    sub = lax.broadcasted_iota(jnp.int32, (8, LANES), 0)
-    is_row = sub < 2
+    is_row = lax.broadcasted_iota(jnp.int32, (8, LANES), 0) < 2
     cand = jnp.full((8, LANES), DEAD, F32)
     tile = 0
-    for dc, mine in ((0, None), (-1, from_left), (1, from_right)):
+    for dc in (0, -1, 1):
         for n, dr in enumerate((0, -1, 1)):
             if dc == 0:
-                if dr == 0:
-                    block = info_block(win_row, win_col, live_count)
-                elif dr == -1:
-                    block = jnp.where(top, DEAD, above[UP : UP + 8, :])
-                else:
-                    block = jnp.where(bottom, DEAD, below[DOWN + 32 : DOWN + 40, :])
+                block = infos[8 * n : 8 * n + 8, :]
             elif dc == -1:
-                block = jnp.where(leftmost, DEAD, from_left[88 + 8 * n : 96 + 8 * n, :])
+                block = jnp.where(leftmost, DEAD, from_left[248 + 8 * n : 256 + 8 * n, :])
             else:
                 block = jnp.where(rightmost, DEAD, from_right[248 + 8 * n : 256 + 8 * n, :])
             block = block + jnp.where(is_row, float(TILE_R * dr), float(LANES * dc))
-            cand = jnp.where(lane // 8 == tile, pltpu.roll(block, 8 * tile, 1), cand)
+            here = (lane // 16 == tile // 2) & (lax.rem(lane, 4) // 2 == tile % 2)
+            cand = jnp.where(here, pltpu.roll(block, 16 * (tile // 2) + 2 * (tile % 2), 1), cand)
             tile += 1
+    for copy in scalar_copies:
+        copy.wait()
     for k in range(SLOTS):
         rows = pl.ds(win_row[0, 0, k], 128)
         fw[k] = window(fa[rows, :], fb[rows, :], win_col[0, 0, k] - 32)
@@ -221,7 +267,7 @@
 
     def lane_transform(x):
         hi, lo = split(x)
-        return split(halves(dot(jnp.concatenate([hi, lo], 1), lane_fwd[...]), 1))
+        return split(halves(dot(jnp.concatenate([hi, lo], 1), tables[:, 0:256]), 1))
 
     ker_hi, ker_lo = lane_transform(o.reshape(SLOTS * PATCH, 128))
     for k in range(SLOTS):
@@ -244,7 +290,7 @@
         w = jnp.concatenate(
             [jnp.concatenate([ker_hi[s], win_hi[s]], 1), jnp.concatenate([ker_lo[s], win_lo[s]], 1)], 0
         )
-        t = halves(dot(row_fwd[...], w), 0)
+        t = halves(dot(tables[:, 768:896], w), 0)
         k1, k2 = pair(t[:, :128])
         w1, w2 = pair(t[:, 128:])
         p1, p2 = times(k1, w1), times(k2, w2)
@@ -255,12 +301,12 @@
     lane128 = lax.broadcasted_iota(jnp.int32, (128, 128), 1)
     for k in range(0, SLOTS, 2):
         hi, lo = split(jnp.concatenate([spectrum(k), spectrum(k + 1)], 0))
-        e = halves(dot(jnp.concatenate([hi, lo], 1), lane_inv[...]), 1)
+        e = halves(dot(jnp.concatenate([hi, lo], 1), tables[:, 256:512]), 1)
         hi, lo = split(e)
         w = jnp.concatenate(
             [jnp.concatenate([hi[:128], lo[:128]], 0), jnp.concatenate([hi[128:], lo[128:]], 0)], 1
         )
-        t = halves(dot(row_inv[...], w), 0)
+        t = halves(dot(tables[:, 512:768], w), 0)
         for m in range(2):
             kk = k + m
             col = win_col[0, 0, kk]
@@ -280,41 +326,32 @@
     return lax.ppermute(x, axis, [(i, (i + by) % count) for i in range(count)])
 
 
-def per_device(friction, taps_row, taps_col, probe, win_row, win_col, live_count):
-    params = pltpu.CompilerParams(vmem_limit_bytes=40 * 2**20)
-    edges = jnp.stack(
-        [lax.axis_index("mx"), lax.axis_index("my"), lax.axis_size("mx"), lax.axis_size("my")]
-    ).astype(jnp.int32)
-    down, up = pl.pallas_call(
-        pack_rows_kernel,
-        out_shape=[shape(UP + 8), shape(DOWN + 40)],
-        in_specs=[SMEM] * 3 + [VMEM] * 2,
-        out_specs=[VMEM] * 2,
-        compiler_params=params,
-    )(win_row, win_col, live_count, friction, probe)
-    above = ring(down, "mx", 1)
-    below = ring(up, "mx", -1)
-    bands, col_band = pl.pallas_call(
-        bands_kernel,
-        out_shape=[shape(224, BF), shape(256, BF, 256)],
-        in_specs=[SMEM] * 2,
-        out_specs=[VMEM] * 2,
-        compiler_params=params,
-    )(taps_row, taps_col)
-    fa, pa, right, left = pl.pallas_call(
-        pack_cols_kernel,
-        out_shape=[shape(EXT_F), shape(EXT_P), shape(112), shape(272)],
-        in_specs=[SMEM] * 4 + [VMEM] * 4,
-        out_specs=[VMEM] * 4,
-        compiler_params=params,
-    )(edges, win_row, win_col, live_count, friction, probe, above, below)
-    from_left = ring(right, "my", 1)
-    from_right = ring(left, "my", -1)
-    tables = [jnp.asarray(t) for t in transform_tables()]
-    oa, ob = pl.pallas_call(
+def swap(x, axis, odd):
+    rows, cols = lax.axis_size("mx"), lax.axis_size("my")
+    pairs = []
+    for i in range(rows):
+        for j in range(cols):
+            if axis == "my":
+                k = ((j + 1) ^ 1) - 1 if odd else j ^ 1
+                to = (i, k) if 0 <= k < cols else (i ^ 1, j)
+            else:
+                k = ((i + 1) ^ 1) - 1 if odd else i ^ 1
+                to = (k, j) if 0 <= k < rows else (i, j ^ 1)
+            pairs.append((i * cols + j, to[0] * cols + to[1]))
+    return lax.ppermute(x, ("mx", "my"), pairs)
+
+
+def diagonal(x):
+    rows, cols = lax.axis_size("mx"), lax.axis_size("my")
+    pairs = [(i * cols + j, (i + 1) % rows * cols + (j + 1) % cols) for i in range(rows) for j in range(cols)]
+    return lax.ppermute(x, ("mx", "my"), pairs)
+
+
+def core_call(win_row, win_col, live_count, fa, pa, infos, even_in, odd_in, bands, col_band, tables):
+    return pl.pallas_call(
         core_kernel,
         out_shape=[shape(OUT_R)] * 2,
-        in_specs=[SMEM] * 4 + [VMEM] * 12,
+        in_specs=[ANY] * 3 + [VMEM] * 8,
         out_specs=[VMEM] * 2,
         scratch_shapes=[
             pltpu.VMEM((EXT_F, LANES), F32),
@@ -322,16 +359,64 @@
             pltpu.VMEM((SLOTS, 128, LANES), F32),
             pltpu.VMEM((SLOTS * 112, 256), BF),
             pltpu.VMEM((SLOTS * PATCH, LANES), F32),
+            pltpu.SMEM((1, 1, SLOTS), jnp.int32),
+            pltpu.SMEM((1, 1, SLOTS), jnp.int32),
+            pltpu.SMEM((1, 1), jnp.int32),
+            pltpu.VMEM((272, LANES), F32),
+            pltpu.VMEM((272, LANES), F32),
+            pltpu.SemaphoreType.DMA((4,)),
         ],
+        compiler_params=pltpu.CompilerParams(vmem_limit_bytes=40 * 2**20),
+    )(
+        win_row, win_col, live_count, fa, pa, infos, even_in, odd_in, bands, col_band, tables,
+    )
+
+
+def per_device(friction, taps_row, taps_col, probe, win_row, win_col, live_count):
+    params = pltpu.CompilerParams(vmem_limit_bytes=40 * 2**20)
+    row_even_out, row_odd_out = pl.pallas_call(
+        pack_rows_kernel,
+        out_shape=[shape(104), shape(104)],
+        in_specs=[ANY] * 5,
+        out_specs=[VMEM] * 2,
+        scratch_shapes=[
+            pltpu.VMEM((1, SLOTS), jnp.int32),
+            pltpu.VMEM((1, SLOTS), jnp.int32),
+            pltpu.VMEM((1, 1), jnp.int32),
+            pltpu.SemaphoreType.DMA((6,)),
+        ],
+        compiler_params=pltpu.CompilerParams(vmem_limit_bytes=40 * 2**20),
+    )(win_row, win_col, live_count, friction, probe)
+    row_odd = swap(row_odd_out, "mx", True)
+    row_even = swap(row_even_out, "mx", False)
+    bands, col_band, tables = pl.pallas_call(
+        bands_kernel,
+        out_shape=[shape(224, BF), shape(256, BF, 256), shape(256, BF, 896)],
+        in_specs=[SMEM] * 2 + [ANY],
+        out_specs=[VMEM] * 3,
+        scratch_shapes=[pltpu.SemaphoreType.DMA],
         compiler_params=params,
-    )(
-        edges, win_row, win_col, live_count, fa, pa, above, below, from_left, from_right, bands, col_band, *tables
+    )(taps_row, taps_col, jnp.asarray(transform_tables()))
+    fa, pa, infos, even_out, odd_out = pl.pallas_call(
+        pack_cols_kernel,
+        out_shape=[shape(EXT_F), shape(EXT_P), shape(24), shape(272), shape(272)],
+        in_specs=[VMEM] * 5,
+        out_specs=[VMEM] * 5,
+        compiler_params=params,
+    )(friction, probe, row_even_out, row_even, row_odd)
+    odd_in = swap(odd_out, "my", True)
+    even_in = swap(even_out, "my", False)
+    oa, ob = core_call(
+        win_row, win_col, live_count, fa, pa, infos, even_in, odd_in, bands, col_band, tables
     )
-    spill = ring(ob, "my", 1)
-    total = oa + jnp.where(lax.axis_index("my") > 0, spill, 0.0)
-    lower = ring(total[TILE_R:], "mx", 1)
-    lower = jnp.where(lax.axis_index("mx") > 0, lower, 0.0)
-    return total[:TILE_R] + jnp.pad(lower, ((0, TILE_R - lower.shape[0]), (0, 0)))
+    side, side_low, own, own_low = ob[:TILE_R], ob[TILE_R:], oa[:TILE_R], oa[TILE_R:]
+    corner = diagonal(side_low)
+    spill = ring(side, "my", 1)
+    lower = ring(own_low, "mx", 1)
+    inner_row, inner_col = lax.axis_index("mx") > 0, lax.axis_index("my") > 0
+    result = own + jnp.where(inner_col, spill, 0.0)
+    low = jnp.where(inner_row, lower, 0.0) + jnp.where(inner_row & inner_col, corner, 0.0)
+    return result + jnp.pad(low, ((0, TILE_R - low.shape[0]), (0, 0)))
 
 
 def solution(mesh):

time: 46.6 us -> 38.1 us (0.82)
  the two profiles are of different devices: /device:TPU:96 before, /device:TPU:68 now
where the time goes in v1:
time: 38.1 us; the launch traced here: 37.9 us
  waiting for transfers between devices  12.6 us (33%)
  Pallas kernels  11.2 us (29%)
  starting transfers between devices  9.73 us (26%)
  local copies, waits for them, and re-layouts  2.87 us (8%)
  between operations  0.8 us (2%)
  other arithmetic  0.69 us (2%)
    pallas_call x1, Pallas kernels, core_call(): pl.pallas_call(core_kernel, out_shape=[shape(OUT_R)] * 2, in_specs=[ANY]...  9.77 us
    ppermute x4, waiting for transfers between devices, swap(): return lax.ppermute(x, ('mx', 'my'), pairs)  5.69 us
    ppermute x4, starting transfers between devices, swap(): return lax.ppermute(x, ('mx', 'my'), pairs)  5.18 us
    ppermute x1, waiting for transfers between devices, diagonal(): return lax.ppermute(x, ('mx', 'my'), pairs)  4.42 us
    ppermute x2, starting transfers between devices, ring(): return lax.ppermute(x, axis, [(i, (i + by) % count) for i in range(count)])  3.69 us
    unnamed x18, local copies, waits for them, and re-layouts  2.85 us
    ppermute x2, waiting for transfers between devices, ring(): return lax.ppermute(x, axis, [(i, (i + by) % count) for i in range(count)])  2.47 us
    pallas_call x1, Pallas kernels, per_device(): pl.pallas_call(bands_kernel, out_shape=[shape(224, BF), shape(256, BF, 25...  0.99 us
  transfers between devices with their start and end apart: 7, of which 5 were waited for; matrix products, arithmetic and copies ran while one was open for 0% of the time, Pallas kernels for 3%

profile of v1, /device:TPU:68, one launch (start us, length us, event | category | flops | bytes accessed | tf_op | source)
XLA Modules:
  0.0 37.9 jit_solution(16869535491889679888)
XLA Ops:
  0.0 0.0 copy-start.5
  0.0 0.0 copy-start.6
  0.7 0.0 copy-done.5
  0.7 0.0 copy-done.6
  0.7 0.0 copy-start
  0.7 0.9 %copy-done = f32[256,128]{1,0:T(8,128)S(1)} copy-done((f32[256,128]{1,0:T(8,128)S(1)}, f32[256,128]{1,0:T(8,128)}, u32[]{:S(2)}) %copy-start) | copy-done | bytes 131096
  1.6 0.0 copy-start.2
  1.6 0.9 %copy-done.2 = f32[256,128]{1,0:T(8,128)S(1)} copy-done((f32[256,128]{1,0:T(8,128)S(1)}, f32[256,128]{1,0:T(8,128)}, u32[]{:S(2)}) %copy-start.2) | copy-done | bytes 131096
  2.5 0.0 copy-start.1
  2.5 0.0 copy-start.3
  2.5 0.3 shard_map.82
  2.8 2.0 %collective-permute-start = (f32[104,128]{1,0:T(8,128)S(1)}, f32[104,128]{1,0:T(8,128)S(1)}, u32[]{:S(2)}, u32[]{:S(2)}) collective-permute-start(f32[104,128]{1,0:T(8,128)S(1)} %get-tuple-element.17.mine), channel_id=1, source_target_pairs={{0,32},{1,33},{2,34},{3,35},{4,36},{5,37},{6,38},{7,39},{8,40},{9,... | collective-permute-start | bytes 159752 | tf_op jit(solution)/shard_map/ppermute | solution.py:341
  4.8 0.0 collective-permute-start.1
  4.8 2.2 %collective-permute-done.row_even = f32[104,128]{1,0:T(8,128)S(1)} collective-permute-done((f32[104,128]{1,0:T(8,128)S(1)}, f32[104,128]{1,0:T(8,128)S(1)}, u32[]{:S(2)}, u32[]{:S(2)}) %collective-permute-start) | collective-permute-done | bytes 53280 | tf_op jit(solution)/shard_map/ppermute | solution.py:341
  7.0 1.9 %collective-permute-done.1.row_odd = f32[104,128]{1,0:T(8,128)S(1)} collective-permute-done((f32[104,128]{1,0:T(8,128)S(1)}, f32[104,128]{1,0:T(8,128)S(1)}, u32[]{:S(2)}, u32[]{:S(2)}) %collective-permute-start.1) | collective-permute-done | bytes 53280 | tf_op jit(solution)/shard_map/ppermute | solution.py:341
  8.9 0.0 copy-done.1
  8.9 0.0 copy-done.3
  9.0 0.2 shard_map.83
  9.1 0.0 copy-start.7
  9.2 0.0 copy-start.8
  9.2 0.1 collective-permute-start.2
  9.3 3.1 %collective-permute-start.3 = (f32[272,128]{1,0:T(8,128)S(1)}, f32[272,128]{1,0:T(8,128)S(1)}, u32[]{:S(2)}, u32[]{:S(2)}) collective-permute-start(f32[272,128]{1,0:T(8,128)S(1)} %get-tuple-element.23), channel_id=1, source_target_pairs={{0,32},{1,2},{2,1},{3,4},{4,3},{5,6},{6,5},{7,8},{8,7},{9,10},{10,... | collective-permute-start | bytes 417800 | tf_op jit(solution)/shard_map/ppermute | solution.py:341
  12.4 0.0 copy-done.7
  12.4 0.0 copy-done.8
  12.4 0.0 copy-start.4
  12.4 1.0 %copy-done.4 = bf16[256,896]{1,0:T(8,128)(2,1)S(1)} copy-done((bf16[256,896]{1,0:T(8,128)(2,1)S(1)}, bf16[256,896]{1,0:T(8,128)(2,1)}, u32[]{:S(2)}) %copy-start.4) | copy-done | bytes 458776
  13.4 1.0 %shard_map.84 = (bf16[224,128]{1,0:T(8,128)(2,1)S(1)}, bf16[256,256]{1,0:T(8,128)(2,1)S(1)}, bf16[256,896]{1,0:T(8,128)(2,1)S(1)}) custom-call(f32[17]{0:T(128)S(1)} %copy-done.7, f32[17]{0:T(128)S(1)} %copy-done.8, bf16[256,896]{1,0:T(8,128)(2,1)S(1)} %copy-done.4), custom_call_target="tpu_custom_call" | custom-call | tf_op jit(solution)/shard_map/pallas_call | solution.py:392
  14.4 0.0 collective-permute-done.2.even_in
  14.4 1.6 %collective-permute-done.3.odd_in = f32[272,128]{1,0:T(8,128)S(1)} collective-permute-done((f32[272,128]{1,0:T(8,128)S(1)}, f32[272,128]{1,0:T(8,128)S(1)}, u32[]{:S(2)}, u32[]{:S(2)}) %collective-permute-start.3) | collective-permute-done | bytes 139296 | tf_op jit(solution)/shard_map/ppermute | solution.py:341
  15.9 9.8 %shard_map.85 = (f32[352,128]{1,0:T(8,128)S(1)}, f32[352,128]{1,0:T(8,128)S(1)}) custom-call(s32[1,1,16]{2,1,0:T(1,128)S(1)} %copy-done.5, s32[1,1,16]{2,1,0:T(1,128)S(1)} %copy-done.6, s32[1,1]{1,0:T(1,128)S(6)} %copy.9.live_count.live_in, f32[352,128]{1,0:T(8,128)S(1)} %get-tuple-element.19.fa, f32[288,128]{1,0:T(8,128)S(1)} %get-tuple-element.20.pa, ...), custom_call_target="tpu_custom_call" | custom-call | tf_op jit(solution)/shard_map/pallas_call | solution.py:351
  25.7 2.2 %collective-permute-start.5 = (f32[96,128]{1,0:T(8,128)S(1)}, f32[96,128]{1,0:T(8,128)S(1)}, u32[]{:S(2)}, u32[]{:S(2)}) collective-permute-start(f32[96,128]{1,0:T(8,128)S(1)} %slice.14), channel_id=1, source_target_pairs={{0,32},{32,64},{64,96},{96,128},{128,160},{160,192},{192,224},{224... | collective-permute-start | bytes 147464 | tf_op jit(solution)/shard_map/ppermute | solution.py:326
  27.9 0.9 %collective-permute-start.6 = (f32[96,128]{1,0:T(8,128)S(1)}, f32[96,128]{1,0:T(8,128)S(1)}, u32[]{:S(2)}, u32[]{:S(2)}) collective-permute-start(f32[96,128]{1,0:T(8,128)S(1)} %slice.15), channel_id=1, source_target_pairs={{0,33},{1,34},{2,35},{3,36},{4,37},{5,38},{6,39},{7,40},{8,41},{9,... | collective-permute-start | bytes 147464 | tf_op jit(solution)/shard_map/ppermute | solution.py:347
  28.8 1.5 %collective-permute-start.4 = (f32[256,128]{1,0:T(8,128)S(1)}, f32[256,128]{1,0:T(8,128)S(1)}, u32[]{:S(2)}, u32[]{:S(2)}) collective-permute-start(f32[256,128]{1,0:T(8,128)S(1)} %slice.13), channel_id=1, source_target_pairs={{0,1},{1,2},{2,3},{3,4},{4,5},{5,6},{6,7},{7,8},{8,9},{9,10},{10,1... | collective-permute-start | bytes 393224 | tf_op jit(solution)/shard_map/ppermute | solution.py:326
  30.3 0.0 collective-permute-done.5
  30.3 4.4 %collective-permute-done.6 = f32[96,128]{1,0:T(8,128)S(1)} collective-permute-done((f32[96,128]{1,0:T(8,128)S(1)}, f32[96,128]{1,0:T(8,128)S(1)}, u32[]{:S(2)}, u32[]{:S(2)}) %collective-permute-start.6) | collective-permute-done | bytes 49184 | tf_op jit(solution)/shard_map/ppermute | solution.py:347
  34.7 2.5 %collective-permute-done.4 = f32[256,128]{1,0:T(8,128)S(1)} collective-permute-done((f32[256,128]{1,0:T(8,128)S(1)}, f32[256,128]{1,0:T(8,128)S(1)}, u32[]{:S(2)}, u32[]{:S(2)}) %collective-permute-start.4) | collective-permute-done | bytes 131104 | tf_op jit(solution)/shard_map/ppermute | solution.py:326
  37.2 0.7 %pad_add_fusion = f32[256,128]{1,0:T(8,128)} fusion(f32[96,128]{1,0:T(8,128)S(1)} %select_add_fusion, f32[256,128]{1,0:T(8,128)S(1)} %collective-permute-done.4, f32[352,128]{1,0:T(8,128)S(1)} %get-tuple-element.27, pred[]{:T(512)S(6)} %gt.6), kind=kLoop, calls=%fused_computation | loop fusion | flops 98304 | bytes 442369 | tf_op jit(solution)/shard_map/add | solution.py:419
  (4 shorter events, 0.0 us)
Async XLA Ops:
  0.0 0.7 %copy-start.5 = (s32[1,1,16]{2,1,0:T(1,128)S(1)}, s32[1,1,16]{2,1,0:T(1,128)}, u32[]{:S(2)}) copy-start(s32[1,1,16]{2,1,0:T(1,128)} %win_row_in.1) | copy-start | bytes 196
  0.0 0.7 %copy-start.6 = (s32[1,1,16]{2,1,0:T(1,128)S(1)}, s32[1,1,16]{2,1,0:T(1,128)}, u32[]{:S(2)}) copy-start(s32[1,1,16]{2,1,0:T(1,128)} %win_col_in.1) | copy-start | bytes 196
  0.7 0.9 %copy-start = (f32[256,128]{1,0:T(8,128)S(1)}, f32[256,128]{1,0:T(8,128)}, u32[]{:S(2)}) copy-start(f32[256,128]{1,0:T(8,128)} %friction.3) | copy-start | bytes 393220
  1.6 0.9 %copy-start.2 = (f32[256,128]{1,0:T(8,128)S(1)}, f32[256,128]{1,0:T(8,128)}, u32[]{:S(2)}) copy-start(f32[256,128]{1,0:T(8,128)} %probe.3) | copy-start | bytes 393220
  2.5 6.4 %copy-start.1 = (f32[256,128]{1,0:T(8,128)S(1)}, f32[256,128]{1,0:T(8,128)}, u32[]{:S(2)}) copy-start(f32[256,128]{1,0:T(8,128)} %friction.3) | copy-start | bytes 393220
  2.5 6.4 %copy-start.3 = (f32[256,128]{1,0:T(8,128)S(1)}, f32[256,128]{1,0:T(8,128)}, u32[]{:S(2)}) copy-start(f32[256,128]{1,0:T(8,128)} %probe.3) | copy-start | bytes 393220
  2.8 4.2 %collective-permute-start = (f32[104,128]{1,0:T(8,128)S(1)}, f32[104,128]{1,0:T(8,128)S(1)}, u32[]{:S(2)}, u32[]{:S(2)}) collective-permute-start(f32[104,128]{1,0:T(8,128)S(1)} %get-tuple-element.17.mine), channel_id=1, source_target_pairs={{0,32},{1,33},{2,34},{3,35},{4,36},{5,37},{6,38},{7,39},{8,40},{9,... | collective-permute-start | bytes 159752 | tf_op jit(solution)/shard_map/ppermute | solution.py:341
  4.8 4.1 %collective-permute-start.1 = (f32[104,128]{1,0:T(8,128)S(1)}, f32[104,128]{1,0:T(8,128)S(1)}, u32[]{:S(2)}, u32[]{:S(2)}) collective-permute-start(f32[104,128]{1,0:T(8,128)S(1)} %get-tuple-element.18), channel_id=1, source_target_pairs={{0,1},{1,0},{2,3},{3,2},{4,5},{5,4},{6,7},{7,6},{8,9},{9,8},{10,11... | collective-permute-start | bytes 159752 | tf_op jit(solution)/shard_map/ppermute | solution.py:341
  9.1 3.2 %copy-start.7 = (f32[17]{0:T(128)S(1)}, f32[17]{0:T(128)}, u32[]{:S(2)}) copy-start(f32[17]{0:T(128)} %taps_row.1) | copy-start | bytes 208
  9.2 3.2 %copy-start.8 = (f32[17]{0:T(128)S(1)}, f32[17]{0:T(128)}, u32[]{:S(2)}) copy-start(f32[17]{0:T(128)} %taps_col.1) | copy-start | bytes 208
  9.2 5.2 %collective-permute-start.2 = (f32[272,128]{1,0:T(8,128)S(1)}, f32[272,128]{1,0:T(8,128)S(1)}, u32[]{:S(2)}, u32[]{:S(2)}) collective-permute-start(f32[272,128]{1,0:T(8,128)S(1)} %get-tuple-element.22), channel_id=1, source_target_pairs={{0,1},{1,0},{2,3},{3,2},{4,5},{5,4},{6,7},{7,6},{8,9},{9,8},{10,11... | collective-permute-start | bytes 417800 | tf_op jit(solution)/shard_map/ppermute | solution.py:341
  9.3 6.7 %collective-permute-start.3 = (f32[272,128]{1,0:T(8,128)S(1)}, f32[272,128]{1,0:T(8,128)S(1)}, u32[]{:S(2)}, u32[]{:S(2)}) collective-permute-start(f32[272,128]{1,0:T(8,128)S(1)} %get-tuple-element.23), channel_id=1, source_target_pairs={{0,32},{1,2},{2,1},{3,4},{4,3},{5,6},{6,5},{7,8},{8,7},{9,10},{10,... | collective-permute-start | bytes 417800 | tf_op jit(solution)/shard_map/ppermute | solution.py:341
  12.4 1.0 %copy-start.4 = (bf16[256,896]{1,0:T(8,128)(2,1)S(1)}, bf16[256,896]{1,0:T(8,128)(2,1)}, u32[]{:S(2)}) copy-start(bf16[256,896]{1,0:T(8,128)(2,1)} %constant.16.clone.tables_in) | copy-start | bytes 1376260
  25.7 4.6 %collective-permute-start.5 = (f32[96,128]{1,0:T(8,128)S(1)}, f32[96,128]{1,0:T(8,128)S(1)}, u32[]{:S(2)}, u32[]{:S(2)}) collective-permute-start(f32[96,128]{1,0:T(8,128)S(1)} %slice.14), channel_id=1, source_target_pairs={{0,32},{32,64},{64,96},{96,128},{128,160},{160,192},{192,224},{224... | collective-permute-start | bytes 147464 | tf_op jit(solution)/shard_map/ppermute | solution.py:326
  27.9 6.8 %collective-permute-start.6 = (f32[96,128]{1,0:T(8,128)S(1)}, f32[96,128]{1,0:T(8,128)S(1)}, u32[]{:S(2)}, u32[]{:S(2)}) collective-permute-start(f32[96,128]{1,0:T(8,128)S(1)} %slice.15), channel_id=1, source_target_pairs={{0,33},{1,34},{2,35},{3,36},{4,37},{5,38},{6,39},{7,40},{8,41},{9,... | collective-permute-start | bytes 147464 | tf_op jit(solution)/shard_map/ppermute | solution.py:347
  28.8 8.4 %collective-permute-start.4 = (f32[256,128]{1,0:T(8,128)S(1)}, f32[256,128]{1,0:T(8,128)S(1)}, u32[]{:S(2)}, u32[]{:S(2)}) collective-permute-start(f32[256,128]{1,0:T(8,128)S(1)} %slice.13), channel_id=1, source_target_pairs={{0,1},{1,2},{2,3},{3,4},{4,5},{5,6},{6,7},{7,8},{8,9},{9,10},{10,1... | collective-permute-start | bytes 393224 | tf_op jit(solution)/shard_map/ppermute | solution.py:326

commit v2 on v1

--- a/solution.py
+++ b/solution.py
@@ -52,11 +52,12 @@
     wide[32:96] = forward
     full = np.outer(theta, np.arange(128))
     inverse = np.concatenate([np.cos(full), np.sin(full)], 0) / 64
+    lane_half = inverse / 2
     hi, lo = np_split(wide)
     lane_fwd = np.block([[hi, lo], [hi, lo]])
     hi, lo = np_split(forward.T)
     row_fwd = np.block([[hi, hi], [lo, lo]])
-    hi, lo = np_split(inverse)
+    hi, lo = np_split(lane_half)
     lane_inv = np.block([[hi, lo], [hi, lo]])
     hi, lo = np_split(inverse.T)
     row_inv = np.block([[hi, hi], [lo, lo]])
@@ -180,7 +181,7 @@
 
 def core_kernel(
     win_row_in, win_col_in, live_in, fa, pa, infos, even_in, odd_in, bands, col_band, tables,
-    oa, ob, fb, pb, fw, y2, z, win_row, win_col, live_count, from_left, from_right, sems,
+    oa, ob, fb, pb, fw, y2, z, comb, spec, wide, win_row, win_col, live_count, from_left, from_right, sems,
 ):
     scalar_copies = [
         pltpu.make_async_copy(win_row_in, win_row, sems.at[1]),
@@ -223,28 +224,28 @@
             here = (lane // 16 == tile // 2) & (lax.rem(lane, 4) // 2 == tile % 2)
             cand = jnp.where(here, pltpu.roll(block, 16 * (tile // 2) + 2 * (tile % 2), 1), cand)
             tile += 1
+    sub_f = lax.broadcasted_iota(jnp.int32, (128, LANES), 0).astype(F32)
+    lane_f = lax.broadcasted_iota(jnp.int32, (128, LANES), 1).astype(F32)
+    lane1 = lax.broadcasted_iota(jnp.int32, (1, LANES), 1)
+    upright = cand.T
+    columns = [jnp.broadcast_to(upright[:, 2 + h : 3 + h], (128, LANES)) for h in range(2)]
+    for k in range(SLOTS):
+        half = (k % 4) // 2
+        row0, col0 = infos[0:1, k : k + 1] - 64.0, infos[2:3, k : k + 1] - 64.0
+        p = jnp.where(lax.rem(lane1, 2) == k % 2, cand[half : half + 1] - row0, -1.0)
+        at_row = (sub_f == p).astype(F32).astype(BF)
+        at_col = jnp.where(lane_f + col0 == columns[half], 64.0, 0.0).astype(BF)
+        comb[k // 2, :, 128 * (k % 2) : 128 * (k % 2) + 128] = dot(at_row, at_col).astype(BF)
+    for k in range(0, SLOTS, 2):
+        t = halves(dot(bands[...], comb[k // 2]), 0)
+        for m in range(2):
+            hi, lo = split(t[:, 128 * m : 128 * m + 128])
+            y2[pl.ds((k + m) * 112, 112), :] = jnp.concatenate([hi, lo], 1)
     for copy in scalar_copies:
         copy.wait()
     for k in range(SLOTS):
         rows = pl.ds(win_row[0, 0, k], 128)
         fw[k] = window(fa[rows, :], fb[rows, :], win_col[0, 0, k] - 32)
-    sub_f = lax.broadcasted_iota(jnp.int32, (128, 128), 0).astype(F32)
-    lane1 = lax.broadcasted_iota(jnp.int32, (1, LANES), 1)
-    for k in range(0, SLOTS, 2):
-        combs = []
-        for kk in (k, k + 1):
-            half = (kk % 4) // 2
-            mine = lax.rem(lane1, 2) == kk % 2
-            p = jnp.where(mine, cand[half : half + 1] - (win_row[0, 0, kk] - 64).astype(F32), -1.0)
-            q = jnp.where(mine, cand[half + 2 : half + 3] - (win_col[0, 0, kk] - 64).astype(F32), -1.0)
-            at_row = (sub_f == p).astype(F32).astype(BF)
-            at_col = jnp.where(sub_f == q, 64.0, 0.0).astype(BF)
-            comb = lax.dot_general(at_row, at_col, (((1,), (1,)), ((), ())), preferred_element_type=F32)
-            combs.append(comb.astype(BF))
-        t = halves(dot(bands[...], jnp.concatenate(combs, 1)), 0)
-        for m in range(2):
-            hi, lo = split(t[:, 128 * m : 128 * m + 128])
-            y2[pl.ds((k + m) * 112, 112), :] = jnp.concatenate([hi, lo], 1)
     first, n = 8, 112
     while True:
         o = halves(dot(y2[0 : SLOTS * n, :], col_band[...]), 1)
@@ -294,19 +295,19 @@
         k1, k2 = pair(t[:, :128])
         w1, w2 = pair(t[:, 128:])
         p1, p2 = times(k1, w1), times(k2, w2)
-        return jnp.concatenate([(p1 + p2) * 0.5, pltpu.roll((p1 - p2) * (0.5 * sign), 64, 1)], 0)
-
+        return jnp.concatenate([p1 + p2, pltpu.roll((p1 - p2) * sign, 64, 1)], 0)
+
+    for k in range(SLOTS):
+        hi, lo = split(spectrum(k))
+        spec[pl.ds(k * 128, 128), :] = jnp.concatenate([hi, lo], 1)
+    for k in range(SLOTS):
+        hi, lo = split(halves(dot(spec[k * 128 : k * 128 + 128, :], tables[:, 256:512]), 1))
+        wide[k // 2, :, 128 * (k % 2) : 128 * (k % 2) + 128] = jnp.concatenate([hi, lo], 0)
     oa[...] = jnp.zeros_like(oa)
     ob[...] = jnp.zeros_like(ob)
-    lane128 = lax.broadcasted_iota(jnp.int32, (128, 128), 1)
+    lane128 = lax.broadcasted_iota(jnp.int32, (128, LANES), 1)
     for k in range(0, SLOTS, 2):
-        hi, lo = split(jnp.concatenate([spectrum(k), spectrum(k + 1)], 0))
-        e = halves(dot(jnp.concatenate([hi, lo], 1), tables[:, 256:512]), 1)
-        hi, lo = split(e)
-        w = jnp.concatenate(
-            [jnp.concatenate([hi[:128], lo[:128]], 0), jnp.concatenate([hi[128:], lo[128:]], 0)], 1
-        )
-        t = halves(dot(tables[:, 512:768], w), 0)
+        t = halves(dot(tables[:, 512:768], wide[k // 2]), 0)
         for m in range(2):
             kk = k + m
             col = win_col[0, 0, kk]
@@ -359,6 +360,9 @@
             pltpu.VMEM((SLOTS, 128, LANES), F32),
             pltpu.VMEM((SLOTS * 112, 256), BF),
             pltpu.VMEM((SLOTS * PATCH, LANES), F32),
+            pltpu.VMEM((SLOTS // 2, 128, 256), BF),
+            pltpu.VMEM((SLOTS * 128, 256), BF),
+            pltpu.VMEM((SLOTS // 2, 256, 256), BF),
             pltpu.SMEM((1, 1, SLOTS), jnp.int32),
             pltpu.SMEM((1, 1, SLOTS), jnp.int32),
             pltpu.SMEM((1, 1), jnp.int32),

time: 38.1 us -> 33.9 us (0.89)
  Pallas kernels: 11.2 us -> 7.1 us
    pallas_call x1, Pallas kernels: 9.77 us -> 5.64 us  [core_call(): pl.pallas_call(core_kernel, out_shape=[shape(OUT_R)] * 2, in_specs=[ANY]...]
where the time goes in v2:
time: 33.9 us; the launch traced here: 33.8 us
  waiting for transfers between devices  12.6 us (37%)
  starting transfers between devices  9.72 us (29%)
  Pallas kernels  7.1 us (21%)
  local copies, waits for them, and re-layouts  2.87 us (8%)
  between operations  0.8 us (2%)
  other arithmetic  0.69 us (2%)
    ppermute x4, waiting for transfers between devices, swap(): return lax.ppermute(x, ('mx', 'my'), pairs)  5.69 us
    pallas_call x1, Pallas kernels, core_call(): pl.pallas_call(core_kernel, out_shape=[shape(OUT_R)] * 2, in_specs=[ANY]...  5.64 us
    ppermute x4, starting transfers between devices, swap(): return lax.ppermute(x, ('mx', 'my'), pairs)  5.18 us
    ppermute x1, waiting for transfers between devices, diagonal(): return lax.ppermute(x, ('mx', 'my'), pairs)  4.43 us
    ppermute x2, starting transfers between devices, ring(): return lax.ppermute(x, axis, [(i, (i + by) % count) for i in range(count)])  3.67 us
    unnamed x18, local copies, waits for them, and re-layouts  2.85 us
    ppermute x2, waiting for transfers between devices, ring(): return lax.ppermute(x, axis, [(i, (i + by) % count) for i in range(count)])  2.49 us
    pallas_call x1, Pallas kernels, per_device(): pl.pallas_call(bands_kernel, out_shape=[shape(224, BF), shape(256, BF, 25...  0.99 us
  transfers between devices with their start and end apart: 7, of which 5 were waited for; matrix products, arithmetic and copies ran while one was open for 0% of the time, Pallas kernels for 3%

profile of v2, /device:TPU:68, one launch (start us, length us, event | category | flops | bytes accessed | tf_op | source)
XLA Modules:
  0.0 33.8 jit_solution(3230537087940341792)
XLA Ops:
  0.0 0.0 copy-start.5
  0.0 0.0 copy-start.6
  0.7 0.0 copy-done.5
  0.7 0.0 copy-done.6
  0.7 0.0 copy-start
  0.7 0.9 %copy-done = f32[256,128]{1,0:T(8,128)S(1)} copy-done((f32[256,128]{1,0:T(8,128)S(1)}, f32[256,128]{1,0:T(8,128)}, u32[]{:S(2)}) %copy-start) | copy-done | bytes 131096
  1.6 0.0 copy-start.2
  1.6 0.9 %copy-done.2 = f32[256,128]{1,0:T(8,128)S(1)} copy-done((f32[256,128]{1,0:T(8,128)S(1)}, f32[256,128]{1,0:T(8,128)}, u32[]{:S(2)}) %copy-start.2) | copy-done | bytes 131096
  2.5 0.0 copy-start.1
  2.5 0.0 copy-start.3
  2.5 0.3 shard_map.82
  2.8 2.0 %collective-permute-start = (f32[104,128]{1,0:T(8,128)S(1)}, f32[104,128]{1,0:T(8,128)S(1)}, u32[]{:S(2)}, u32[]{:S(2)}) collective-permute-start(f32[104,128]{1,0:T(8,128)S(1)} %get-tuple-element.17.mine), channel_id=1, source_target_pairs={{0,32},{1,33},{2,34},{3,35},{4,36},{5,37},{6,38},{7,39},{8,40},{9,... | collective-permute-start | bytes 159752 | tf_op jit(solution)/shard_map/ppermute | solution.py:342
  4.8 0.0 collective-permute-start.1
  4.8 2.2 %collective-permute-done.row_even = f32[104,128]{1,0:T(8,128)S(1)} collective-permute-done((f32[104,128]{1,0:T(8,128)S(1)}, f32[104,128]{1,0:T(8,128)S(1)}, u32[]{:S(2)}, u32[]{:S(2)}) %collective-permute-start) | collective-permute-done | bytes 53280 | tf_op jit(solution)/shard_map/ppermute | solution.py:342
  7.0 1.9 %collective-permute-done.1.row_odd = f32[104,128]{1,0:T(8,128)S(1)} collective-permute-done((f32[104,128]{1,0:T(8,128)S(1)}, f32[104,128]{1,0:T(8,128)S(1)}, u32[]{:S(2)}, u32[]{:S(2)}) %collective-permute-start.1) | collective-permute-done | bytes 53280 | tf_op jit(solution)/shard_map/ppermute | solution.py:342
  8.9 0.0 copy-done.1
  8.9 0.0 copy-done.3
  9.0 0.2 shard_map.83
  9.1 0.0 copy-start.7
  9.2 0.0 copy-start.8
  9.2 0.1 collective-permute-start.2
  9.3 3.1 %collective-permute-start.3 = (f32[272,128]{1,0:T(8,128)S(1)}, f32[272,128]{1,0:T(8,128)S(1)}, u32[]{:S(2)}, u32[]{:S(2)}) collective-permute-start(f32[272,128]{1,0:T(8,128)S(1)} %get-tuple-element.23), channel_id=1, source_target_pairs={{0,32},{1,2},{2,1},{3,4},{4,3},{5,6},{6,5},{7,8},{8,7},{9,10},{10,... | collective-permute-start | bytes 417800 | tf_op jit(solution)/shard_map/ppermute | solution.py:342
  12.4 0.0 copy-done.7
  12.4 0.0 copy-done.8
  12.4 0.0 copy-start.4
  12.4 1.0 %copy-done.4 = bf16[256,896]{1,0:T(8,128)(2,1)S(1)} copy-done((bf16[256,896]{1,0:T(8,128)(2,1)S(1)}, bf16[256,896]{1,0:T(8,128)(2,1)}, u32[]{:S(2)}) %copy-start.4) | copy-done | bytes 458776
  13.4 1.0 %shard_map.84 = (bf16[224,128]{1,0:T(8,128)(2,1)S(1)}, bf16[256,256]{1,0:T(8,128)(2,1)S(1)}, bf16[256,896]{1,0:T(8,128)(2,1)S(1)}) custom-call(f32[17]{0:T(128)S(1)} %copy-done.7, f32[17]{0:T(128)S(1)} %copy-done.8, bf16[256,896]{1,0:T(8,128)(2,1)S(1)} %copy-done.4), custom_call_target="tpu_custom_call" | custom-call | tf_op jit(solution)/shard_map/pallas_call | solution.py:396
  14.4 0.0 collective-permute-done.2.even_in
  14.4 1.6 %collective-permute-done.3.odd_in = f32[272,128]{1,0:T(8,128)S(1)} collective-permute-done((f32[272,128]{1,0:T(8,128)S(1)}, f32[272,128]{1,0:T(8,128)S(1)}, u32[]{:S(2)}, u32[]{:S(2)}) %collective-permute-start.3) | collective-permute-done | bytes 139296 | tf_op jit(solution)/shard_map/ppermute | solution.py:342
  15.9 5.6 %shard_map.85 = (f32[352,128]{1,0:T(8,128)S(1)}, f32[352,128]{1,0:T(8,128)S(1)}) custom-call(s32[1,1,16]{2,1,0:T(1,128)S(1)} %copy-done.5, s32[1,1,16]{2,1,0:T(1,128)S(1)} %copy-done.6, s32[1,1]{1,0:T(1,128)S(6)} %copy.9.live_count.live_in, f32[352,128]{1,0:T(8,128)S(1)} %get-tuple-element.19.fa, f32[288,128]{1,0:T(8,128)S(1)} %get-tuple-element.20.pa, ...), custom_call_target="tpu_custom_call" | custom-call | tf_op jit(solution)/shard_map/pallas_call | solution.py:352
  21.6 2.2 %collective-permute-start.5 = (f32[96,128]{1,0:T(8,128)S(1)}, f32[96,128]{1,0:T(8,128)S(1)}, u32[]{:S(2)}, u32[]{:S(2)}) collective-permute-start(f32[96,128]{1,0:T(8,128)S(1)} %slice.14), channel_id=1, source_target_pairs={{0,32},{32,64},{64,96},{96,128},{128,160},{160,192},{192,224},{224... | collective-permute-start | bytes 147464 | tf_op jit(solution)/shard_map/ppermute | solution.py:327
  23.8 0.9 %collective-permute-start.6 = (f32[96,128]{1,0:T(8,128)S(1)}, f32[96,128]{1,0:T(8,128)S(1)}, u32[]{:S(2)}, u32[]{:S(2)}) collective-permute-start(f32[96,128]{1,0:T(8,128)S(1)} %slice.15), channel_id=1, source_target_pairs={{0,33},{1,34},{2,35},{3,36},{4,37},{5,38},{6,39},{7,40},{8,41},{9,... | collective-permute-start | bytes 147464 | tf_op jit(solution)/shard_map/ppermute | solution.py:348
  24.7 1.5 %collective-permute-start.4 = (f32[256,128]{1,0:T(8,128)S(1)}, f32[256,128]{1,0:T(8,128)S(1)}, u32[]{:S(2)}, u32[]{:S(2)}) collective-permute-start(f32[256,128]{1,0:T(8,128)S(1)} %slice.13), channel_id=1, source_target_pairs={{0,1},{1,2},{2,3},{3,4},{4,5},{5,6},{6,7},{7,8},{8,9},{9,10},{10,1... | collective-permute-start | bytes 393224 | tf_op jit(solution)/shard_map/ppermute | solution.py:327
  26.2 0.0 collective-permute-done.5
  26.2 4.4 %collective-permute-done.6 = f32[96,128]{1,0:T(8,128)S(1)} collective-permute-done((f32[96,128]{1,0:T(8,128)S(1)}, f32[96,128]{1,0:T(8,128)S(1)}, u32[]{:S(2)}, u32[]{:S(2)}) %collective-permute-start.6) | collective-permute-done | bytes 49184 | tf_op jit(solution)/shard_map/ppermute | solution.py:348
  30.6 2.5 %collective-permute-done.4 = f32[256,128]{1,0:T(8,128)S(1)} collective-permute-done((f32[256,128]{1,0:T(8,128)S(1)}, f32[256,128]{1,0:T(8,128)S(1)}, u32[]{:S(2)}, u32[]{:S(2)}) %collective-permute-start.4) | collective-permute-done | bytes 131104 | tf_op jit(solution)/shard_map/ppermute | solution.py:327
  33.1 0.7 %pad_add_fusion = f32[256,128]{1,0:T(8,128)} fusion(f32[96,128]{1,0:T(8,128)S(1)} %select_add_fusion, f32[256,128]{1,0:T(8,128)S(1)} %collective-permute-done.4, f32[352,128]{1,0:T(8,128)S(1)} %get-tuple-element.27, pred[]{:T(512)S(6)} %gt.6), kind=kLoop, calls=%fused_computation | loop fusion | flops 98304 | bytes 442369 | tf_op jit(solution)/shard_map/add | solution.py:423
  (4 shorter events, 0.0 us)
Async XLA Ops:
  0.0 0.7 %copy-start.5 = (s32[1,1,16]{2,1,0:T(1,128)S(1)}, s32[1,1,16]{2,1,0:T(1,128)}, u32[]{:S(2)}) copy-start(s32[1,1,16]{2,1,0:T(1,128)} %win_row_in.1) | copy-start | bytes 196
  0.0 0.7 %copy-start.6 = (s32[1,1,16]{2,1,0:T(1,128)S(1)}, s32[1,1,16]{2,1,0:T(1,128)}, u32[]{:S(2)}) copy-start(s32[1,1,16]{2,1,0:T(1,128)} %win_col_in.1) | copy-start | bytes 196
  0.7 0.9 %copy-start = (f32[256,128]{1,0:T(8,128)S(1)}, f32[256,128]{1,0:T(8,128)}, u32[]{:S(2)}) copy-start(f32[256,128]{1,0:T(8,128)} %friction.3) | copy-start | bytes 393220
  1.6 0.9 %copy-start.2 = (f32[256,128]{1,0:T(8,128)S(1)}, f32[256,128]{1,0:T(8,128)}, u32[]{:S(2)}) copy-start(f32[256,128]{1,0:T(8,128)} %probe.3) | copy-start | bytes 393220
  2.5 6.4 %copy-start.1 = (f32[256,128]{1,0:T(8,128)S(1)}, f32[256,128]{1,0:T(8,128)}, u32[]{:S(2)}) copy-start(f32[256,128]{1,0:T(8,128)} %friction.3) | copy-start | bytes 393220
  2.5 6.4 %copy-start.3 = (f32[256,128]{1,0:T(8,128)S(1)}, f32[256,128]{1,0:T(8,128)}, u32[]{:S(2)}) copy-start(f32[256,128]{1,0:T(8,128)} %probe.3) | copy-start | bytes 393220
  2.8 4.2 %collective-permute-start = (f32[104,128]{1,0:T(8,128)S(1)}, f32[104,128]{1,0:T(8,128)S(1)}, u32[]{:S(2)}, u32[]{:S(2)}) collective-permute-start(f32[104,128]{1,0:T(8,128)S(1)} %get-tuple-element.17.mine), channel_id=1, source_target_pairs={{0,32},{1,33},{2,34},{3,35},{4,36},{5,37},{6,38},{7,39},{8,40},{9,... | collective-permute-start | bytes 159752 | tf_op jit(solution)/shard_map/ppermute | solution.py:342
  4.8 4.1 %collective-permute-start.1 = (f32[104,128]{1,0:T(8,128)S(1)}, f32[104,128]{1,0:T(8,128)S(1)}, u32[]{:S(2)}, u32[]{:S(2)}) collective-permute-start(f32[104,128]{1,0:T(8,128)S(1)} %get-tuple-element.18), channel_id=1, source_target_pairs={{0,1},{1,0},{2,3},{3,2},{4,5},{5,4},{6,7},{7,6},{8,9},{9,8},{10,11... | collective-permute-start | bytes 159752 | tf_op jit(solution)/shard_map/ppermute | solution.py:342
  9.1 3.2 %copy-start.7 = (f32[17]{0:T(128)S(1)}, f32[17]{0:T(128)}, u32[]{:S(2)}) copy-start(f32[17]{0:T(128)} %taps_row.1) | copy-start | bytes 208
  9.2 3.2 %copy-start.8 = (f32[17]{0:T(128)S(1)}, f32[17]{0:T(128)}, u32[]{:S(2)}) copy-start(f32[17]{0:T(128)} %taps_col.1) | copy-start | bytes 208
  9.2 5.2 %collective-permute-start.2 = (f32[272,128]{1,0:T(8,128)S(1)}, f32[272,128]{1,0:T(8,128)S(1)}, u32[]{:S(2)}, u32[]{:S(2)}) collective-permute-start(f32[272,128]{1,0:T(8,128)S(1)} %get-tuple-element.22), channel_id=1, source_target_pairs={{0,1},{1,0},{2,3},{3,2},{4,5},{5,4},{6,7},{7,6},{8,9},{9,8},{10,11... | collective-permute-start | bytes 417800 | tf_op jit(solution)/shard_map/ppermute | solution.py:342
  9.3 6.7 %collective-permute-start.3 = (f32[272,128]{1,0:T(8,128)S(1)}, f32[272,128]{1,0:T(8,128)S(1)}, u32[]{:S(2)}, u32[]{:S(2)}) collective-permute-start(f32[272,128]{1,0:T(8,128)S(1)} %get-tuple-element.23), channel_id=1, source_target_pairs={{0,32},{1,2},{2,1},{3,4},{4,3},{5,6},{6,5},{7,8},{8,7},{9,10},{10,... | collective-permute-start | bytes 417800 | tf_op jit(solution)/shard_map/ppermute | solution.py:342
  12.4 1.0 %copy-start.4 = (bf16[256,896]{1,0:T(8,128)(2,1)S(1)}, bf16[256,896]{1,0:T(8,128)(2,1)}, u32[]{:S(2)}) copy-start(bf16[256,896]{1,0:T(8,128)(2,1)} %constant.16.clone.tables_in) | copy-start | bytes 1376260
  21.6 4.6 %collective-permute-start.5 = (f32[96,128]{1,0:T(8,128)S(1)}, f32[96,128]{1,0:T(8,128)S(1)}, u32[]{:S(2)}, u32[]{:S(2)}) collective-permute-start(f32[96,128]{1,0:T(8,128)S(1)} %slice.14), channel_id=1, source_target_pairs={{0,32},{32,64},{64,96},{96,128},{128,160},{160,192},{192,224},{224... | collective-permute-start | bytes 147464 | tf_op jit(solution)/shard_map/ppermute | solution.py:327
  23.8 6.8 %collective-permute-start.6 = (f32[96,128]{1,0:T(8,128)S(1)}, f32[96,128]{1,0:T(8,128)S(1)}, u32[]{:S(2)}, u32[]{:S(2)}) collective-permute-start(f32[96,128]{1,0:T(8,128)S(1)} %slice.15), channel_id=1, source_target_pairs={{0,33},{1,34},{2,35},{3,36},{4,37},{5,38},{6,39},{7,40},{8,41},{9,... | collective-permute-start | bytes 147464 | tf_op jit(solution)/shard_map/ppermute | solution.py:348
  24.7 8.4 %collective-permute-start.4 = (f32[256,128]{1,0:T(8,128)S(1)}, f32[256,128]{1,0:T(8,128)S(1)}, u32[]{:S(2)}, u32[]{:S(2)}) collective-permute-start(f32[256,128]{1,0:T(8,128)S(1)} %slice.13), channel_id=1, source_target_pairs={{0,1},{1,2},{2,3},{3,4},{4,5},{5,6},{6,7},{7,8},{8,9},{9,10},{10,1... | collective-permute-start | bytes 393224 | tf_op jit(solution)/shard_map/ppermute | solution.py:327

commit v3 on v2

--- a/solution.py
+++ b/solution.py
@@ -130,16 +130,25 @@
         copy.wait()
 
 
-def pack_cols_kernel(friction, probe, mine, row_even, row_odd, fa, pa, infos, even_out, odd_out):
+def fetch_kernel(friction, probe, fa, pa, sems):
+    copies = [
+        pltpu.make_async_copy(friction, fa.at[pl.ds(UP, TILE_R)], sems.at[0]),
+        pltpu.make_async_copy(probe, pa.at[pl.ds(0, TILE_R)], sems.at[1]),
+    ]
+    for copy in copies:
+        copy.start()
+    for copy in copies:
+        copy.wait()
+
+
+def pack_cols_kernel(fa_in, pa_in, mine, row_even, row_odd, fa, pa, infos, even_out, odd_out):
     at, count = own_index("mx")
     top, bottom = at == 0, at == count - 1
     is_even = lax.rem(at, 2) == 0
     above = jnp.where(is_even, row_odd[...], row_even[...])
     below = jnp.where(is_even, row_even[...], row_odd[...])
     fa[0:UP, :] = jnp.where(top, 0.0, above[0:UP])
-    fa[UP : UP + TILE_R, :] = friction[...]
     fa[UP + TILE_R : EXT_F, :] = jnp.where(bottom, 0.0, below[0:DOWN])
-    pa[0:TILE_R, :] = probe[...]
     pa[TILE_R:EXT_P, :] = jnp.where(bottom, 0.0, below[DOWN : DOWN + 32])
     infos[0:8, :] = mine[96:104, :]
     infos[8:16, :] = jnp.where(top, DEAD, above[96:104])
@@ -389,10 +398,18 @@
             pltpu.VMEM((1, 1), jnp.int32),
             pltpu.SemaphoreType.DMA((6,)),
         ],
-        compiler_params=pltpu.CompilerParams(vmem_limit_bytes=40 * 2**20),
+        compiler_params=pltpu.CompilerParams(vmem_limit_bytes=55040 * 2**10),
     )(win_row, win_col, live_count, friction, probe)
     row_odd = swap(row_odd_out, "mx", True)
     row_even = swap(row_even_out, "mx", False)
+    fa, pa = pl.pallas_call(
+        fetch_kernel,
+        out_shape=[shape(EXT_F), shape(EXT_P)],
+        in_specs=[ANY] * 2,
+        out_specs=[VMEM] * 2,
+        scratch_shapes=[pltpu.SemaphoreType.DMA((2,))],
+        compiler_params=params,
+    )(friction, probe)
     bands, col_band, tables = pl.pallas_call(
         bands_kernel,
         out_shape=[shape(224, BF), shape(256, BF, 256), shape(256, BF, 896)],
@@ -406,20 +423,22 @@
         out_shape=[shape(EXT_F), shape(EXT_P), shape(24), shape(272), shape(272)],
         in_specs=[VMEM] * 5,
         out_specs=[VMEM] * 5,
+        input_output_aliases={0: 0, 1: 1},
         compiler_params=params,
-    )(friction, probe, row_even_out, row_even, row_odd)
+    )(fa, pa, row_even_out, row_even, row_odd)
     odd_in = swap(odd_out, "my", True)
     even_in = swap(even_out, "my", False)
     oa, ob = core_call(
         win_row, win_col, live_count, fa, pa, infos, even_in, odd_in, bands, col_band, tables
     )
     side, side_low, own, own_low = ob[:TILE_R], ob[TILE_R:], oa[:TILE_R], oa[TILE_R:]
+    spill = ring(side, "my", 1)
     corner = diagonal(side_low)
-    spill = ring(side, "my", 1)
     lower = ring(own_low, "mx", 1)
     inner_row, inner_col = lax.axis_index("mx") > 0, lax.axis_index("my") > 0
-    result = own + jnp.where(inner_col, spill, 0.0)
-    low = jnp.where(inner_row, lower, 0.0) + jnp.where(inner_row & inner_col, corner, 0.0)
+    result = lax.optimization_barrier(own + jnp.where(inner_col, spill, 0.0))
+    result = lax.optimization_barrier(result.at[:96].add(jnp.where(inner_row & inner_col, corner, 0.0)))
+    low = jnp.where(inner_row, lower, 0.0)
     return result + jnp.pad(low, ((0, TILE_R - low.shape[0]), (0, 0)))
 
 

time: 33.9 us -> 32 us (0.944)
  the two profiles are of different devices: /device:TPU:68 before, /device:TPU:100 now
where the time goes in v3:
time: 32 us; the launch traced here: 31.8 us
  waiting for transfers between devices  11.2 us (35%)
  starting transfers between devices  10.9 us (34%)
  Pallas kernels  8.07 us (25%)
  between operations  0.86 us (3%)
  other arithmetic  0.71 us (2%)
    ppermute x4, starting transfers between devices, swap(): return lax.ppermute(x, ('mx', 'my'), pairs)  7.41 us
    ppermute x2, waiting for transfers between devices, ring(): return lax.ppermute(x, axis, [(i, (i + by) % count) for i in range(count)])  6.92 us
    pallas_call x1, Pallas kernels, core_call(): pl.pallas_call(core_kernel, out_shape=[shape(OUT_R)] * 2, in_specs=[ANY]...  5.66 us
    ppermute x4, waiting for transfers between devices, swap(): return lax.ppermute(x, ('mx', 'my'), pairs)  4.32 us
    ppermute x2, starting transfers between devices, ring(): return lax.ppermute(x, axis, [(i, (i + by) % count) for i in range(count)])  3.41 us
    pallas_call x1, Pallas kernels, per_device(): pl.pallas_call(bands_kernel, out_shape=[shape(224, BF), shape(256, BF, 25...  0.99 us
    pallas_call x1, Pallas kernels, per_device(): pl.pallas_call(pack_rows_kernel, out_shape=[shape(104), shape(104)], in_s...  0.91 us
    add x1, other arithmetic, per_device(): return result + jnp.pad(low, ((0, TILE_R - low.shape[0]), (0, 0)))  0.67 us
  transfers between devices with their start and end apart: 7, of which 4 were waited for; matrix products, arithmetic and copies ran while one was open for 0% of the time, Pallas kernels for 4%

profile of v3, /device:TPU:100, one launch (start us, length us, event | category | flops | bytes accessed | tf_op | source)
XLA Modules:
  0.0 31.8 jit_solution(3067738833985710748)
XLA Ops:
  0.0 0.0 copy-start.3
  0.0 0.0 copy-start.4
  0.7 0.0 copy-done.3
  0.7 0.0 copy-done.4
  0.7 0.0 copy-start
  0.7 0.0 copy-start.1
  0.7 0.0 copy-start.2
  0.7 0.9 %shard_map.83 = (f32[104,128]{1,0:T(8,128)S(1)}, f32[104,128]{1,0:T(8,128)S(1)}) custom-call(s32[1,1,16]{2,1,0:T(1,128)S(1)} %copy-done.3, s32[1,1,16]{2,1,0:T(1,128)S(1)} %copy-done.4, s32[1,1]{1,0:T(1,128)S(6)} %copy.14.live_count.live_in, f32[256,128]{1,0:T(8,128)} %friction.3, f32[256,128]{1,0:T(8,128)} %probe.3), custom_call_target="tpu_custom_call" | custom-call | tf_op jit(solution)/shard_map/pallas_call | solution.py:390
  1.7 0.2 collective-permute-start
  1.8 4.0 %collective-permute-start.1 = (f32[104,128]{1,0:T(8,128)S(1)}, f32[104,128]{1,0:T(8,128)S(1)}, u32[]{:S(2)}, u32[]{:S(2)}) collective-permute-start(f32[104,128]{1,0:T(8,128)S(1)} %get-tuple-element.34), channel_id=1, source_target_pairs={{0,1},{1,0},{2,3},{3,2},{4,5},{5,4},{6,7},{7,6},{8,9},{9,8},{10,11... | collective-permute-start | bytes 159752 | tf_op jit(solution)/shard_map/ppermute | solution.py:351
  5.9 0.0 copy-done
  5.9 0.0 copy-done.1
  5.9 0.3 %shard_map.82 = (f32[352,128]{1,0:T(8,128)S(1)}, f32[288,128]{1,0:T(8,128)S(1)}) custom-call(f32[256,128]{1,0:T(8,128)S(1)} %copy-done, f32[256,128]{1,0:T(8,128)S(1)} %copy-done.1), custom_call_target="tpu_custom_call" | custom-call | tf_op jit(solution)/shard_map/pallas_call | solution.py:405
  6.2 0.0 collective-permute-done.row_even
  6.3 1.7 %collective-permute-done.1.row_odd = f32[104,128]{1,0:T(8,128)S(1)} collective-permute-done((f32[104,128]{1,0:T(8,128)S(1)}, f32[104,128]{1,0:T(8,128)S(1)}, u32[]{:S(2)}, u32[]{:S(2)}) %collective-permute-start.1) | collective-permute-done | bytes 53280 | tf_op jit(solution)/shard_map/ppermute | solution.py:351
  8.0 0.2 shard_map.84
  8.2 0.0 copy-start.5
  8.2 0.0 copy-start.6
  8.2 0.1 collective-permute-start.2
  8.3 3.1 %collective-permute-start.3 = (f32[272,128]{1,0:T(8,128)S(1)}, f32[272,128]{1,0:T(8,128)S(1)}, u32[]{:S(2)}, u32[]{:S(2)}) collective-permute-start(f32[272,128]{1,0:T(8,128)S(1)} %get-tuple-element.39), channel_id=1, source_target_pairs={{0,32},{1,2},{2,1},{3,4},{4,3},{5,6},{6,5},{7,8},{8,7},{9,10},{10,... | collective-permute-start | bytes 417800 | tf_op jit(solution)/shard_map/ppermute | solution.py:351
  11.4 0.0 copy-done.2
  11.4 0.0 copy-done.5
  11.4 0.0 copy-done.6
  11.4 1.0 %shard_map.85 = (bf16[224,128]{1,0:T(8,128)(2,1)S(1)}, bf16[256,256]{1,0:T(8,128)(2,1)S(1)}, bf16[256,896]{1,0:T(8,128)(2,1)S(1)}) custom-call(f32[17]{0:T(128)S(1)} %copy-done.5, f32[17]{0:T(128)S(1)} %copy-done.6, bf16[256,896]{1,0:T(8,128)(2,1)S(1)} %copy-done.2), custom_call_target="tpu_custom_call" | custom-call | tf_op jit(solution)/shard_map/pallas_call | solution.py:413
  12.4 0.0 collective-permute-done.2.even_in
  12.4 2.6 %collective-permute-done.3.odd_in = f32[272,128]{1,0:T(8,128)S(1)} collective-permute-done((f32[272,128]{1,0:T(8,128)S(1)}, f32[272,128]{1,0:T(8,128)S(1)}, u32[]{:S(2)}, u32[]{:S(2)}) %collective-permute-start.3) | collective-permute-done | bytes 139296 | tf_op jit(solution)/shard_map/ppermute | solution.py:351
  15.0 5.7 %shard_map.86 = (f32[352,128]{1,0:T(8,128)S(1)}, f32[352,128]{1,0:T(8,128)S(1)}) custom-call(s32[1,1,16]{2,1,0:T(1,128)S(1)} %copy-done.3, s32[1,1,16]{2,1,0:T(1,128)S(1)} %copy-done.4, s32[1,1]{1,0:T(1,128)S(6)} %copy.14.live_count.live_in, f32[352,128]{1,0:T(8,128)S(1)} %get-tuple-element.35.fa, f32[288,128]{1,0:T(8,128)S(1)} %get-tuple-element.36.pa, ...), custom_call_target="tpu_custom_call" | custom-call | tf_op jit(solution)/shard_map/pallas_call | solution.py:361
  20.7 3.3 %collective-permute-start.6 = (f32[96,128]{1,0:T(8,128)S(1)}, f32[96,128]{1,0:T(8,128)S(1)}, u32[]{:S(2)}, u32[]{:S(2)}) collective-permute-start(f32[96,128]{1,0:T(8,128)S(1)} %slice.35), channel_id=1, source_target_pairs={{0,32},{32,64},{64,96},{96,128},{128,160},{160,192},{192,224},{224... | collective-permute-start | bytes 147464 | tf_op jit(solution)/shard_map/ppermute | solution.py:336
  24.0 0.1 collective-permute-start.4
  24.1 0.1 collective-permute-start.5
  24.2 1.5 %collective-permute-done.6 = f32[96,128]{1,0:T(8,128)S(1)} collective-permute-done((f32[96,128]{1,0:T(8,128)S(1)}, f32[96,128]{1,0:T(8,128)S(1)}, u32[]{:S(2)}, u32[]{:S(2)}) %collective-permute-start.6) | collective-permute-done | bytes 49184 | tf_op jit(solution)/shard_map/ppermute | solution.py:336
  25.7 5.4 %collective-permute-done.4 = f32[256,128]{1,0:T(8,128)S(1)} collective-permute-done((f32[256,128]{1,0:T(8,128)S(1)}, f32[256,128]{1,0:T(8,128)S(1)}, u32[]{:S(2)}, u32[]{:S(2)}) %collective-permute-start.4) | collective-permute-done | bytes 131104 | tf_op jit(solution)/shard_map/ppermute | solution.py:336
  31.1 0.0 collective-permute-done.5
  31.2 0.7 %pad_add_fusion = f32[256,128]{1,0:T(8,128)} fusion(f32[256,128]{1,0:T(8,128)S(1)} %fusion, f32[96,128]{1,0:T(8,128)S(1)} %broadcast_select_fusion), kind=kLoop, calls=%fused_computation | loop fusion | flops 32768 | bytes 311296 | tf_op jit(solution)/shard_map/add | solution.py:442
  (6 shorter events, 0.1 us)
Async XLA Ops:
  0.0 0.7 %copy-start.3 = (s32[1,1,16]{2,1,0:T(1,128)S(1)}, s32[1,1,16]{2,1,0:T(1,128)}, u32[]{:S(2)}) copy-start(s32[1,1,16]{2,1,0:T(1,128)} %win_row_in.1) | copy-start | bytes 196
  0.0 0.7 %copy-start.4 = (s32[1,1,16]{2,1,0:T(1,128)S(1)}, s32[1,1,16]{2,1,0:T(1,128)}, u32[]{:S(2)}) copy-start(s32[1,1,16]{2,1,0:T(1,128)} %win_col_in.1) | copy-start | bytes 196
  0.7 5.2 %copy-start = (f32[256,128]{1,0:T(8,128)S(1)}, f32[256,128]{1,0:T(8,128)}, u32[]{:S(2)}) copy-start(f32[256,128]{1,0:T(8,128)} %friction.3) | copy-start | bytes 393220
  0.7 5.2 %copy-start.1 = (f32[256,128]{1,0:T(8,128)S(1)}, f32[256,128]{1,0:T(8,128)}, u32[]{:S(2)}) copy-start(f32[256,128]{1,0:T(8,128)} %probe.3) | copy-start | bytes 393220
  0.7 10.7 %copy-start.2 = (bf16[256,896]{1,0:T(8,128)(2,1)S(1)}, bf16[256,896]{1,0:T(8,128)(2,1)}, u32[]{:S(2)}) copy-start(bf16[256,896]{1,0:T(8,128)(2,1)} %constant.43.clone.tables_in) | copy-start | bytes 1376260
  1.7 4.6 %collective-permute-start = (f32[104,128]{1,0:T(8,128)S(1)}, f32[104,128]{1,0:T(8,128)S(1)}, u32[]{:S(2)}, u32[]{:S(2)}) collective-permute-start(f32[104,128]{1,0:T(8,128)S(1)} %get-tuple-element.33.mine), channel_id=1, source_target_pairs={{0,32},{1,33},{2,34},{3,35},{4,36},{5,37},{6,38},{7,39},{8,40},{9,... | collective-permute-start | bytes 159752 | tf_op jit(solution)/shard_map/ppermute | solution.py:351
  1.8 6.2 %collective-permute-start.1 = (f32[104,128]{1,0:T(8,128)S(1)}, f32[104,128]{1,0:T(8,128)S(1)}, u32[]{:S(2)}, u32[]{:S(2)}) collective-permute-start(f32[104,128]{1,0:T(8,128)S(1)} %get-tuple-element.34), channel_id=1, source_target_pairs={{0,1},{1,0},{2,3},{3,2},{4,5},{5,4},{6,7},{7,6},{8,9},{9,8},{10,11... | collective-permute-start | bytes 159752 | tf_op jit(solution)/shard_map/ppermute | solution.py:351
  8.2 3.2 %copy-start.5 = (f32[17]{0:T(128)S(1)}, f32[17]{0:T(128)}, u32[]{:S(2)}) copy-start(f32[17]{0:T(128)} %taps_row.1) | copy-start | bytes 208
  8.2 3.2 %copy-start.6 = (f32[17]{0:T(128)S(1)}, f32[17]{0:T(128)}, u32[]{:S(2)}) copy-start(f32[17]{0:T(128)} %taps_col.1) | copy-start | bytes 208
  8.2 4.2 %collective-permute-start.2 = (f32[272,128]{1,0:T(8,128)S(1)}, f32[272,128]{1,0:T(8,128)S(1)}, u32[]{:S(2)}, u32[]{:S(2)}) collective-permute-start(f32[272,128]{1,0:T(8,128)S(1)} %get-tuple-element.38), channel_id=1, source_target_pairs={{0,1},{1,0},{2,3},{3,2},{4,5},{5,4},{6,7},{7,6},{8,9},{9,8},{10,11... | collective-permute-start | bytes 417800 | tf_op jit(solution)/shard_map/ppermute | solution.py:351
  8.3 6.7 %collective-permute-start.3 = (f32[272,128]{1,0:T(8,128)S(1)}, f32[272,128]{1,0:T(8,128)S(1)}, u32[]{:S(2)}, u32[]{:S(2)}) collective-permute-start(f32[272,128]{1,0:T(8,128)S(1)} %get-tuple-element.39), channel_id=1, source_target_pairs={{0,32},{1,2},{2,1},{3,4},{4,3},{5,6},{6,5},{7,8},{8,7},{9,10},{10,... | collective-permute-start | bytes 417800 | tf_op jit(solution)/shard_map/ppermute | solution.py:351
  20.7 5.1 %collective-permute-start.6 = (f32[96,128]{1,0:T(8,128)S(1)}, f32[96,128]{1,0:T(8,128)S(1)}, u32[]{:S(2)}, u32[]{:S(2)}) collective-permute-start(f32[96,128]{1,0:T(8,128)S(1)} %slice.35), channel_id=1, source_target_pairs={{0,32},{32,64},{64,96},{96,128},{128,160},{160,192},{192,224},{224... | collective-permute-start | bytes 147464 | tf_op jit(solution)/shard_map/ppermute | solution.py:336
  24.0 7.1 %collective-permute-start.4 = (f32[256,128]{1,0:T(8,128)S(1)}, f32[256,128]{1,0:T(8,128)S(1)}, u32[]{:S(2)}, u32[]{:S(2)}) collective-permute-start(f32[256,128]{1,0:T(8,128)S(1)} %slice.32), channel_id=1, source_target_pairs={{0,1},{1,2},{2,3},{3,4},{4,5},{5,6},{6,7},{7,8},{8,9},{9,10},{10,1... | collective-permute-start | bytes 393224 | tf_op jit(solution)/shard_map/ppermute | solution.py:336
  24.1 7.0 %collective-permute-start.5 = (f32[96,128]{1,0:T(8,128)S(1)}, f32[96,128]{1,0:T(8,128)S(1)}, u32[]{:S(2)}, u32[]{:S(2)}) collective-permute-start(f32[96,128]{1,0:T(8,128)S(1)} %slice.34), channel_id=1, source_target_pairs={{0,33},{1,34},{2,35},{3,36},{4,37},{5,38},{6,39},{7,40},{8,41},{9,... | collective-permute-start | bytes 147464 | tf_op jit(solution)/shard_map/ppermute | solution.py:357

commit v4 on v3

--- a/solution.py
+++ b/solution.py
@@ -141,7 +141,7 @@
         copy.wait()
 
 
-def pack_cols_kernel(fa_in, pa_in, mine, row_even, row_odd, fa, pa, infos, even_out, odd_out):
+def pack_cols_kernel(fa_in, pa_in, mine, row_even, row_odd, odd_slots, fa, pa, infos, even_out, odd_out):
     at, count = own_index("mx")
     top, bottom = at == 0, at == count - 1
     is_even = lax.rem(at, 2) == 0
@@ -151,25 +151,28 @@
     fa[UP + TILE_R : EXT_F, :] = jnp.where(bottom, 0.0, below[0:DOWN])
     pa[TILE_R:EXT_P, :] = jnp.where(bottom, 0.0, below[DOWN : DOWN + 32])
     infos[0:8, :] = mine[96:104, :]
-    infos[8:16, :] = jnp.where(top, DEAD, above[96:104])
-    infos[16:24, :] = jnp.where(bottom, DEAD, below[96:104])
-
-    def packed(ref, rows, width, start):
+    infos[8:16, :] = jnp.where(top, DEAD, jnp.where(is_even, odd_slots[...], row_even[96:104, :]))
+    infos[16:24, :] = jnp.where(bottom, DEAD, jnp.where(is_even, row_even[96:104, :], odd_slots[...]))
+
+    def packed(ref, rows, width, start, first=0):
         count = LANES // width
         part = rows // count
         lane = lax.broadcasted_iota(jnp.int32, (part, LANES), 1) // width
         total = jnp.zeros((part, LANES), F32)
         for i in range(count):
-            piece = pltpu.roll(ref[i * part : (i + 1) * part, :], (width * i - start) % LANES, 1)
+            piece = pltpu.roll(ref[first + i * part : first + (i + 1) * part, :], (width * i - start) % LANES, 1)
             total = jnp.where(lane == i, piece, total)
         return total
 
     def fill(right, left):
         right[0:88, :] = packed(fa, EXT_F, 32, 96)
-        left[0:176, :] = packed(fa, EXT_F, 64, 0)
-        left[176:248, :] = packed(pa, EXT_P, 32, 0)
-        right[248:272, :] = infos[...]
-        left[248:272, :] = infos[...]
+        left[0:168, :] = packed(fa, EXT_F - 16, 64, 0, 8)
+        left[168:240, :] = packed(pa, EXT_P, 32, 0)
+        third = lax.broadcasted_iota(jnp.int32, (8, LANES), 1) // 32
+        both = jnp.where(third == 1, pltpu.roll(infos[8:16, :], 32, 1), pltpu.roll(infos[16:24, :], 64, 1))
+        both = jnp.where(third == 0, infos[0:8, :], both)
+        right[240:248, :] = both
+        left[240:248, :] = both
 
     is_even = lax.rem(lax.axis_index("my"), 2) == 0
 
@@ -189,8 +192,8 @@
 
 
 def core_kernel(
-    win_row_in, win_col_in, live_in, fa, pa, infos, even_in, odd_in, bands, col_band, tables,
-    oa, ob, fb, pb, fw, y2, z, comb, spec, wide, win_row, win_col, live_count, from_left, from_right, sems,
+    win_row_in, win_col_in, live_in, fa, pa, infos, even_in, odd_in, odd_slots, bands, col_band, tables,
+    own, own_low, side, side_low, oa, ob, fb, pb, fw, y2, z, comb, spec, wide, win_row, win_col, live_count, from_left, from_right, sems,
 ):
     scalar_copies = [
         pltpu.make_async_copy(win_row_in, win_row, sems.at[1]),
@@ -202,22 +205,23 @@
     at_col, col_count = own_index("my")
     leftmost, rightmost = at_col == 0, at_col == col_count - 1
     is_even = lax.rem(at_col, 2) == 0
-    from_left[...] = jnp.where(is_even, odd_in[...], even_in[...])
-    from_right[...] = jnp.where(is_even, even_in[...], odd_in[...])
+    from_left[0:240, :] = jnp.where(is_even, odd_in[0:240, :], even_in[0:240, :])
+    from_right[0:240, :] = jnp.where(is_even, even_in[0:240, :], odd_in[0:240, :])
+    from_left[240:248, :] = jnp.where(is_even, odd_slots[...], even_in[240:248, :])
+    from_right[240:248, :] = jnp.where(is_even, even_in[240:248, :], odd_slots[...])
     lane = lax.broadcasted_iota(jnp.int32, (8, LANES), 1)
+    lane88 = lax.broadcasted_iota(jnp.int32, (88, LANES), 1)
+    lane72 = lax.broadcasted_iota(jnp.int32, (72, LANES), 1)
+    lane168 = lax.broadcasted_iota(jnp.int32, (168, LANES), 1)
     for i in range(4):
-        rows = slice(88 * i, 88 * i + 88)
         rim = pltpu.roll(from_left[0:88, :], 96 - 32 * i, 1)
-        lane88 = lax.broadcasted_iota(jnp.int32, (88, LANES), 1)
-        near = from_right[88 * (i % 2) : 88 * (i % 2) + 88, :]
-        if i >= 2:
-            near = pltpu.roll(near, 64, 1)
-        keep_l = (lane88 >= 96) & jnp.logical_not(leftmost)
-        keep_r = (lane88 < 64) & jnp.logical_not(rightmost)
-        fb[rows, :] = jnp.where(keep_l, rim, jnp.where(keep_r, near, 0.0))
-        lane72 = lax.broadcasted_iota(jnp.int32, (72, LANES), 1)
-        near = pltpu.roll(from_right[176:248, :], (128 - 32 * i) % 128, 1)
+        fb[88 * i : 88 * i + 88, :] = jnp.where((lane88 >= 96) & jnp.logical_not(leftmost), rim, 0.0)
+        near = pltpu.roll(from_right[168:240, :], (128 - 32 * i) % 128, 1)
         pb[72 * i : 72 * i + 72, :] = jnp.where((lane72 < 32) & jnp.logical_not(rightmost), near, 0.0)
+    for i in range(2):
+        rows = slice(8 + 168 * i, 176 + 168 * i)
+        near = from_right[0:168, :] if i == 0 else pltpu.roll(from_right[0:168, :], 64, 1)
+        fb[rows, :] = jnp.where((lane168 < 64) & jnp.logical_not(rightmost), near, fb[rows, :])
     is_row = lax.broadcasted_iota(jnp.int32, (8, LANES), 0) < 2
     cand = jnp.full((8, LANES), DEAD, F32)
     tile = 0
@@ -226,9 +230,9 @@
             if dc == 0:
                 block = infos[8 * n : 8 * n + 8, :]
             elif dc == -1:
-                block = jnp.where(leftmost, DEAD, from_left[248 + 8 * n : 256 + 8 * n, :])
+                block = jnp.where(leftmost, DEAD, pltpu.roll(from_left[240:248, :], (128 - 32 * n) % 128, 1))
             else:
-                block = jnp.where(rightmost, DEAD, from_right[248 + 8 * n : 256 + 8 * n, :])
+                block = jnp.where(rightmost, DEAD, pltpu.roll(from_right[240:248, :], (128 - 32 * n) % 128, 1))
             block = block + jnp.where(is_row, float(TILE_R * dr), float(LANES * dc))
             here = (lane // 16 == tile // 2) & (lax.rem(lane, 4) // 2 == tile % 2)
             cand = jnp.where(here, pltpu.roll(block, 16 * (tile // 2) + 2 * (tile % 2), 1), cand)
@@ -325,6 +329,30 @@
             rows = pl.ds(win_row[0, 0, kk], 128)
             oa[rows, :] += jnp.where(lane128 >= col, patch, 0.0)
             ob[rows, :] += jnp.where(lane128 < col, patch, 0.0)
+    at_row, row_count = own_index("mx")
+    inner = at_row < row_count - 1
+    own[...] = oa[0:TILE_R, :]
+    own_low[...] = jnp.where(inner, oa[TILE_R:OUT_R, :], 0.0)
+    side_low[...] = jnp.where(inner & jnp.logical_not(rightmost), ob[TILE_R:OUT_R, :], 0.0)
+    free = lax.broadcasted_iota(jnp.int32, (64, LANES), 1) >= 96
+    for i in range(3):
+        rows = slice(64 * i, 64 * i + 64)
+        piece = jnp.where(free, pltpu.roll(ob[192:256, :], 96 - 32 * i, 1), ob[rows, :])
+        side[rows, :] = jnp.where(rightmost, 0.0, piece)
+
+
+def peek_kernel(payload, slots):
+    slots[...] = payload[payload.shape[0] - 8 :, :]
+
+
+def add_side_kernel(own, spill, total):
+    lane = lax.broadcasted_iota(jnp.int32, (64, LANES), 1)
+    last = jnp.zeros((64, LANES), F32)
+    for i in range(3):
+        rows = slice(64 * i, 64 * i + 64)
+        total[rows, :] = own[rows, :] + jnp.where(lane < 96, spill[rows, :], 0.0)
+        last = jnp.where(lane // 32 == i, pltpu.roll(spill[rows, :], (32 + 32 * i) % 128, 1), last)
+    total[192:256, :] = own[192:256, :] + last
 
 
 def shape(rows, dtype=F32, cols=LANES):
@@ -357,13 +385,15 @@
     return lax.ppermute(x, ("mx", "my"), pairs)
 
 
-def core_call(win_row, win_col, live_count, fa, pa, infos, even_in, odd_in, bands, col_band, tables):
+def core_call(win_row, win_col, live_count, fa, pa, infos, even_in, odd_in, odd_slots, bands, col_band, tables):
     return pl.pallas_call(
         core_kernel,
-        out_shape=[shape(OUT_R)] * 2,
-        in_specs=[ANY] * 3 + [VMEM] * 8,
-        out_specs=[VMEM] * 2,
+        out_shape=[shape(TILE_R), shape(OUT_R - TILE_R), shape(192), shape(OUT_R - TILE_R)],
+        in_specs=[ANY] * 3 + [VMEM] * 9,
+        out_specs=[VMEM] * 4,
         scratch_shapes=[
+            pltpu.VMEM((OUT_R, LANES), F32),
+            pltpu.VMEM((OUT_R, LANES), F32),
             pltpu.VMEM((EXT_F, LANES), F32),
             pltpu.VMEM((EXT_P, LANES), F32),
             pltpu.VMEM((SLOTS, 128, LANES), F32),
@@ -375,14 +405,24 @@
             pltpu.SMEM((1, 1, SLOTS), jnp.int32),
             pltpu.SMEM((1, 1, SLOTS), jnp.int32),
             pltpu.SMEM((1, 1), jnp.int32),
-            pltpu.VMEM((272, LANES), F32),
-            pltpu.VMEM((272, LANES), F32),
+            pltpu.VMEM((248, LANES), F32),
+            pltpu.VMEM((248, LANES), F32),
             pltpu.SemaphoreType.DMA((4,)),
         ],
         compiler_params=pltpu.CompilerParams(vmem_limit_bytes=40 * 2**20),
     )(
-        win_row, win_col, live_count, fa, pa, infos, even_in, odd_in, bands, col_band, tables,
+        win_row, win_col, live_count, fa, pa, infos, even_in, odd_in, odd_slots, bands, col_band, tables,
     )
+
+
+def peek(payload, params):
+    return pl.pallas_call(
+        peek_kernel,
+        out_shape=shape(8),
+        in_specs=[VMEM],
+        out_specs=VMEM,
+        compiler_params=params,
+    )(payload)
 
 
 def per_device(friction, taps_row, taps_col, probe, win_row, win_col, live_count):
@@ -420,26 +460,30 @@
     )(taps_row, taps_col, jnp.asarray(transform_tables()))
     fa, pa, infos, even_out, odd_out = pl.pallas_call(
         pack_cols_kernel,
-        out_shape=[shape(EXT_F), shape(EXT_P), shape(24), shape(272), shape(272)],
-        in_specs=[VMEM] * 5,
+        out_shape=[shape(EXT_F), shape(EXT_P), shape(24), shape(248), shape(248)],
+        in_specs=[VMEM] * 6,
         out_specs=[VMEM] * 5,
         input_output_aliases={0: 0, 1: 1},
         compiler_params=params,
-    )(fa, pa, row_even_out, row_even, row_odd)
+    )(fa, pa, row_even_out, row_even, row_odd, peek(row_odd, params))
     odd_in = swap(odd_out, "my", True)
     even_in = swap(even_out, "my", False)
-    oa, ob = core_call(
-        win_row, win_col, live_count, fa, pa, infos, even_in, odd_in, bands, col_band, tables
+    own, own_low, side, side_low = core_call(
+        win_row, win_col, live_count, fa, pa, infos, even_in, odd_in, peek(odd_in, params), bands, col_band, tables
     )
-    side, side_low, own, own_low = ob[:TILE_R], ob[TILE_R:], oa[:TILE_R], oa[TILE_R:]
     spill = ring(side, "my", 1)
     corner = diagonal(side_low)
     lower = ring(own_low, "mx", 1)
-    inner_row, inner_col = lax.axis_index("mx") > 0, lax.axis_index("my") > 0
-    result = lax.optimization_barrier(own + jnp.where(inner_col, spill, 0.0))
-    result = lax.optimization_barrier(result.at[:96].add(jnp.where(inner_row & inner_col, corner, 0.0)))
-    low = jnp.where(inner_row, lower, 0.0)
-    return result + jnp.pad(low, ((0, TILE_R - low.shape[0]), (0, 0)))
+    total = pl.pallas_call(
+        add_side_kernel,
+        out_shape=shape(TILE_R),
+        in_specs=[VMEM] * 2,
+        out_specs=VMEM,
+        compiler_params=params,
+    )(own, spill)
+    below = ((0, TILE_R - corner.shape[0]), (0, 0))
+    total = lax.optimization_barrier(total + jnp.pad(corner, below))
+    return total + jnp.pad(lower, below)
 
 
 def solution(mesh):

time: 32 us -> 30.4 us (0.950)
  the two profiles are of different devices: /device:TPU:100 before, /device:TPU:6 now
where the time goes in v4:
time: 30.4 us; the launch traced here: 30.3 us
  waiting for transfers between devices  10.4 us (34%)
  starting transfers between devices  10 us (33%)
  Pallas kernels  8.32 us (27%)
  between operations  0.83 us (3%)
  other arithmetic  0.68 us (2%)
    pallas_call x1, Pallas kernels, core_call(): pl.pallas_call(core_kernel, out_shape=[shape(TILE_R), shape(OUT_R - TILE_...  5.83 us
    ppermute x4, starting transfers between devices, swap(): return lax.ppermute(x, ('mx', 'my'), pairs)  5.69 us
    ppermute x4, waiting for transfers between devices, swap(): return lax.ppermute(x, ('mx', 'my'), pairs)  5.5 us
    ppermute x2, starting transfers between devices, ring(): return lax.ppermute(x, axis, [(i, (i + by) % count) for i in range(count)])  3.12 us
    ppermute x1, waiting for transfers between devices, diagonal(): return lax.ppermute(x, ('mx', 'my'), pairs)  3 us
    ppermute x2, waiting for transfers between devices, ring(): return lax.ppermute(x, axis, [(i, (i + by) % count) for i in range(count)])  1.91 us
    ppermute x1, starting transfers between devices, diagonal(): return lax.ppermute(x, ('mx', 'my'), pairs)  1.19 us
    pallas_call x1, Pallas kernels, per_device(): pl.pallas_call(bands_kernel, out_shape=[shape(224, BF), shape(256, BF, 25...  0.99 us
  transfers between devices with their start and end apart: 7, of which 4 were waited for; matrix products, arithmetic and copies ran while one was open for 0% of the time, Pallas kernels for 5%

profile of v4, /device:TPU:6, one launch (start us, length us, event | category | flops | bytes accessed | tf_op | source)
XLA Modules:
  0.0 30.3 jit_solution(8805304484765614141)
XLA Ops:
  0.0 0.0 copy-start.4
  0.0 0.0 copy-start.3
  0.7 0.0 copy-done.4
  0.7 0.0 copy-done.3
  0.7 0.0 copy-start
  0.7 0.0 copy-start.1
  0.7 0.9 %shard_map.83 = (f32[104,128]{1,0:T(8,128)S(1)}, f32[104,128]{1,0:T(8,128)S(1)}) custom-call(s32[1,1,16]{2,1,0:T(1,128)S(1)} %copy-done.3, s32[1,1,16]{2,1,0:T(1,128)S(1)} %copy-done.4, s32[1,1]{1,0:T(1,128)S(6)} %copy.13.live_count.live_in, f32[256,128]{1,0:T(8,128)} %friction.3, f32[256,128]{1,0:T(8,128)} %probe.3), custom_call_target="tpu_custom_call" | custom-call | tf_op jit(solution)/shard_map/pallas_call | solution.py:430
  1.6 0.0 copy-start.2
  1.6 0.1 collective-permute-start.1
  1.7 3.8 %collective-permute-start = (f32[104,128]{1,0:T(8,128)S(1)}, f32[104,128]{1,0:T(8,128)S(1)}, u32[]{:S(2)}, u32[]{:S(2)}) collective-permute-start(f32[104,128]{1,0:T(8,128)S(1)} %get-tuple-element.23.mine), channel_id=1, source_target_pairs={{0,32},{1,33},{2,34},{3,35},{4,36},{5,37},{6,38},{7,39},{8,40},{9,... | collective-permute-start | bytes 159752 | tf_op jit(solution)/shard_map/ppermute | solution.py:379
  5.6 0.0 copy-done
  5.6 0.0 copy-done.1
  5.6 0.3 %shard_map.82 = (f32[352,128]{1,0:T(8,128)S(1)}, f32[288,128]{1,0:T(8,128)S(1)}) custom-call(f32[256,128]{1,0:T(8,128)S(1)} %copy-done, f32[256,128]{1,0:T(8,128)S(1)} %copy-done.1), custom_call_target="tpu_custom_call" | custom-call | tf_op jit(solution)/shard_map/pallas_call | solution.py:445
  5.9 0.0 collective-permute-done.1.payload.row_odd
  5.9 1.7 %collective-permute-done.row_even = f32[104,128]{1,0:T(8,128)S(1)} collective-permute-done((f32[104,128]{1,0:T(8,128)S(1)}, f32[104,128]{1,0:T(8,128)S(1)}, u32[]{:S(2)}, u32[]{:S(2)}) %collective-permute-start) | collective-permute-done | bytes 53280 | tf_op jit(solution)/shard_map/ppermute | solution.py:379
  7.7 0.2 shard_map.85
  7.8 0.0 copy-start.5
  7.9 0.0 copy-start.6
  7.9 1.7 %collective-permute-start.3 = (f32[248,128]{1,0:T(8,128)S(1)}, f32[248,128]{1,0:T(8,128)S(1)}, u32[]{:S(2)}, u32[]{:S(2)}) collective-permute-start(f32[248,128]{1,0:T(8,128)S(1)} %get-tuple-element.29), channel_id=1, source_target_pairs={{0,32},{1,2},{2,1},{3,4},{4,3},{5,6},{6,5},{7,8},{8,7},{9,10},{10,... | collective-permute-start | bytes 380936 | tf_op jit(solution)/shard_map/ppermute | solution.py:379
  9.5 0.1 collective-permute-start.2
  9.7 0.0 copy-done.2
  9.7 0.0 copy-done.5
  9.7 0.0 copy-done.6
  9.7 1.0 %shard_map.87 = (bf16[224,128]{1,0:T(8,128)(2,1)S(1)}, bf16[256,256]{1,0:T(8,128)(2,1)S(1)}, bf16[256,896]{1,0:T(8,128)(2,1)S(1)}) custom-call(f32[17]{0:T(128)S(1)} %copy-done.5, f32[17]{0:T(128)S(1)} %copy-done.6, bf16[256,896]{1,0:T(8,128)(2,1)S(1)} %copy-done.2), custom_call_target="tpu_custom_call" | custom-call | tf_op jit(solution)/shard_map/pallas_call | solution.py:453
  10.7 3.8 %collective-permute-done.3.payload.odd_in = f32[248,128]{1,0:T(8,128)S(1)} collective-permute-done((f32[248,128]{1,0:T(8,128)S(1)}, f32[248,128]{1,0:T(8,128)S(1)}, u32[]{:S(2)}, u32[]{:S(2)}) %collective-permute-start.3) | collective-permute-done | bytes 127008 | tf_op jit(solution)/shard_map/ppermute | solution.py:379
  14.4 0.0 collective-permute-done.2.even_in
  14.4 5.8 %shard_map.88 = (f32[256,128]{1,0:T(8,128)S(1)}, f32[96,128]{1,0:T(8,128)S(1)}, f32[192,128]{1,0:T(8,128)S(1)}, f32[96,128]{1,0:T(8,128)S(1)}) custom-call(s32[1,1,16]{2,1,0:T(1,128)S(1)} %copy-done.3, s32[1,1,16]{2,1,0:T(1,128)S(1)} %copy-done.4, s32[1,1]{1,0:T(1,128)S(6)} %copy.13.live_count.live_in, f32[352,128]{1,0:T(8,128)S(1)} %get-tuple-element.25.fa, ...), custom_call_target="tpu_custom_call" | custom-call | tf_op jit(solution)/shard_map/pallas_call | solution.py:389
  20.3 0.1 collective-permute-start.4
  20.3 1.2 %collective-permute-start.5 = (f32[96,128]{1,0:T(8,128)S(1)}, f32[96,128]{1,0:T(8,128)S(1)}, u32[]{:S(2)}, u32[]{:S(2)}) collective-permute-start(f32[96,128]{1,0:T(8,128)S(1)} %get-tuple-element.35), channel_id=1, source_target_pairs={{0,33},{1,34},{2,35},{3,36},{4,37},{5,38},{6,39},{7,40},{8,41},{9,... | collective-permute-start | bytes 147464 | tf_op jit(solution)/shard_map/ppermute | solution.py:385
  21.5 3.0 %collective-permute-start.6 = (f32[96,128]{1,0:T(8,128)S(1)}, f32[96,128]{1,0:T(8,128)S(1)}, u32[]{:S(2)}, u32[]{:S(2)}) collective-permute-start(f32[96,128]{1,0:T(8,128)S(1)} %get-tuple-element.36), channel_id=1, source_target_pairs={{0,32},{32,64},{64,96},{96,128},{128,160},{160,192},{192,224},{224... | collective-permute-start | bytes 147464 | tf_op jit(solution)/shard_map/ppermute | solution.py:364
  24.6 1.9 %collective-permute-done.4.spill = f32[192,128]{1,0:T(8,128)S(1)} collective-permute-done((f32[192,128]{1,0:T(8,128)S(1)}, f32[192,128]{1,0:T(8,128)S(1)}, u32[]{:S(2)}, u32[]{:S(2)}) %collective-permute-start.4) | collective-permute-done | bytes 98336 | tf_op jit(solution)/shard_map/ppermute | solution.py:364
  26.5 0.1 shard_map.89
  26.6 3.0 %collective-permute-done.5 = f32[96,128]{1,0:T(8,128)S(1)} collective-permute-done((f32[96,128]{1,0:T(8,128)S(1)}, f32[96,128]{1,0:T(8,128)S(1)}, u32[]{:S(2)}, u32[]{:S(2)}) %collective-permute-start.5) | collective-permute-done | bytes 49184 | tf_op jit(solution)/shard_map/ppermute | solution.py:385
  29.6 0.0 collective-permute-done.6
  29.6 0.7 %pad_add_fusion = f32[256,128]{1,0:T(8,128)} fusion(f32[256,128]{1,0:T(8,128)S(1)} %pad_add_fusion.1, f32[96,128]{1,0:T(8,128)S(1)} %collective-permute-done.6), kind=kLoop, calls=%fused_computation | loop fusion | flops 32768 | bytes 311296 | tf_op jit(solution)/shard_map/add | solution.py:486
  (3 shorter events, 0.0 us)
Async XLA Ops:
  0.0 0.7 %copy-start.4 = (s32[1,1,16]{2,1,0:T(1,128)S(1)}, s32[1,1,16]{2,1,0:T(1,128)}, u32[]{:S(2)}) copy-start(s32[1,1,16]{2,1,0:T(1,128)} %win_col_in.1) | copy-start | bytes 196
  0.0 0.7 %copy-start.3 = (s32[1,1,16]{2,1,0:T(1,128)S(1)}, s32[1,1,16]{2,1,0:T(1,128)}, u32[]{:S(2)}) copy-start(s32[1,1,16]{2,1,0:T(1,128)} %win_row_in.1) | copy-start | bytes 196
  0.7 4.9 %copy-start = (f32[256,128]{1,0:T(8,128)S(1)}, f32[256,128]{1,0:T(8,128)}, u32[]{:S(2)}) copy-start(f32[256,128]{1,0:T(8,128)} %friction.3) | copy-start | bytes 393220
  0.7 4.8 %copy-start.1 = (f32[256,128]{1,0:T(8,128)S(1)}, f32[256,128]{1,0:T(8,128)}, u32[]{:S(2)}) copy-start(f32[256,128]{1,0:T(8,128)} %probe.3) | copy-start | bytes 393220
  1.6 8.0 %copy-start.2 = (bf16[256,896]{1,0:T(8,128)(2,1)S(1)}, bf16[256,896]{1,0:T(8,128)(2,1)}, u32[]{:S(2)}) copy-start(bf16[256,896]{1,0:T(8,128)(2,1)} %constant.5.clone.tables_in) | copy-start | bytes 1376260
  1.6 4.3 %collective-permute-start.1 = (f32[104,128]{1,0:T(8,128)S(1)}, f32[104,128]{1,0:T(8,128)S(1)}, u32[]{:S(2)}, u32[]{:S(2)}) collective-permute-start(f32[104,128]{1,0:T(8,128)S(1)} %get-tuple-element.24), channel_id=1, source_target_pairs={{0,1},{1,0},{2,3},{3,2},{4,5},{5,4},{6,7},{7,6},{8,9},{9,8},{10,11... | collective-permute-start | bytes 159752 | tf_op jit(solution)/shard_map/ppermute | solution.py:379
  1.7 5.9 %collective-permute-start = (f32[104,128]{1,0:T(8,128)S(1)}, f32[104,128]{1,0:T(8,128)S(1)}, u32[]{:S(2)}, u32[]{:S(2)}) collective-permute-start(f32[104,128]{1,0:T(8,128)S(1)} %get-tuple-element.23.mine), channel_id=1, source_target_pairs={{0,32},{1,33},{2,34},{3,35},{4,36},{5,37},{6,38},{7,39},{8,40},{9,... | collective-permute-start | bytes 159752 | tf_op jit(solution)/shard_map/ppermute | solution.py:379
  7.8 1.8 %copy-start.5 = (f32[17]{0:T(128)S(1)}, f32[17]{0:T(128)}, u32[]{:S(2)}) copy-start(f32[17]{0:T(128)} %taps_row.1) | copy-start | bytes 208
  7.9 1.8 %copy-start.6 = (f32[17]{0:T(128)S(1)}, f32[17]{0:T(128)}, u32[]{:S(2)}) copy-start(f32[17]{0:T(128)} %taps_col.1) | copy-start | bytes 208
  7.9 6.5 %collective-permute-start.3 = (f32[248,128]{1,0:T(8,128)S(1)}, f32[248,128]{1,0:T(8,128)S(1)}, u32[]{:S(2)}, u32[]{:S(2)}) collective-permute-start(f32[248,128]{1,0:T(8,128)S(1)} %get-tuple-element.29), channel_id=1, source_target_pairs={{0,32},{1,2},{2,1},{3,4},{4,3},{5,6},{6,5},{7,8},{8,7},{9,10},{10,... | collective-permute-start | bytes 380936 | tf_op jit(solution)/shard_map/ppermute | solution.py:379
  9.5 4.9 %collective-permute-start.2 = (f32[248,128]{1,0:T(8,128)S(1)}, f32[248,128]{1,0:T(8,128)S(1)}, u32[]{:S(2)}, u32[]{:S(2)}) collective-permute-start(f32[248,128]{1,0:T(8,128)S(1)} %get-tuple-element.28), channel_id=1, source_target_pairs={{0,1},{1,0},{2,3},{3,2},{4,5},{5,4},{6,7},{7,6},{8,9},{9,8},{10,11... | collective-permute-start | bytes 380936 | tf_op jit(solution)/shard_map/ppermute | solution.py:379
  20.3 6.2 %collective-permute-start.4 = (f32[192,128]{1,0:T(8,128)S(1)}, f32[192,128]{1,0:T(8,128)S(1)}, u32[]{:S(2)}, u32[]{:S(2)}) collective-permute-start(f32[192,128]{1,0:T(8,128)S(1)} %get-tuple-element.34), channel_id=1, source_target_pairs={{0,1},{1,2},{2,3},{3,4},{4,5},{5,6},{6,7},{7,8},{8,9},{9,10},{10,1... | collective-permute-start | bytes 294920 | tf_op jit(solution)/shard_map/ppermute | solution.py:364
  20.3 9.2 %collective-permute-start.5 = (f32[96,128]{1,0:T(8,128)S(1)}, f32[96,128]{1,0:T(8,128)S(1)}, u32[]{:S(2)}, u32[]{:S(2)}) collective-permute-start(f32[96,128]{1,0:T(8,128)S(1)} %get-tuple-element.35), channel_id=1, source_target_pairs={{0,33},{1,34},{2,35},{3,36},{4,37},{5,38},{6,39},{7,40},{8,41},{9,... | collective-permute-start | bytes 147464 | tf_op jit(solution)/shard_map/ppermute | solution.py:385
  21.5 8.1 %collective-permute-start.6 = (f32[96,128]{1,0:T(8,128)S(1)}, f32[96,128]{1,0:T(8,128)S(1)}, u32[]{:S(2)}, u32[]{:S(2)}) collective-permute-start(f32[96,128]{1,0:T(8,128)S(1)} %get-tuple-element.36), channel_id=1, source_target_pairs={{0,32},{32,64},{64,96},{96,128},{128,160},{160,192},{192,224},{224... | collective-permute-start | bytes 147464 | tf_op jit(solution)/shard_map/ppermute | solution.py:364

commit v5 on v4

--- a/solution.py
+++ b/solution.py
@@ -381,7 +381,11 @@
 
 def diagonal(x):
     rows, cols = lax.axis_size("mx"), lax.axis_size("my")
-    pairs = [(i * cols + j, (i + 1) % rows * cols + (j + 1) % cols) for i in range(rows) for j in range(cols)]
+    pairs = []
+    for i in range(rows):
+        for j in range(cols):
+            to = (i + 1, (j + 1) % cols) if i + 1 < rows else (0, j)
+            pairs.append((i * cols + j, to[0] * cols + to[1]))
     return lax.ppermute(x, ("mx", "my"), pairs)
 
 

time: 30.4 us -> 29.4 us (0.967)
  the two profiles are of different devices: /device:TPU:6 before, /device:TPU:68 now
where the time goes in v5:
time: 29.4 us; the launch traced here: 28.9 us
  waiting for transfers between devices  9.65 us (33%)
  starting transfers between devices  9.41 us (32%)
  Pallas kernels  8.32 us (28%)
  between operations  0.83 us (3%)
  other arithmetic  0.68 us (2%)
    ppermute x4, starting transfers between devices, swap(): return lax.ppermute(x, ('mx', 'my'), pairs)  6.91 us
    pallas_call x1, Pallas kernels, core_call(): pl.pallas_call(core_kernel, out_shape=[shape(TILE_R), shape(OUT_R - TILE_...  5.83 us
    ppermute x4, waiting for transfers between devices, swap(): return lax.ppermute(x, ('mx', 'my'), pairs)  5.5 us
    ppermute x2, waiting for transfers between devices, ring(): return lax.ppermute(x, axis, [(i, (i + by) % count) for i in range(count)])  3.74 us
    ppermute x2, starting transfers between devices, ring(): return lax.ppermute(x, axis, [(i, (i + by) % count) for i in range(count)])  1.29 us
    ppermute x1, starting transfers between devices, diagonal(): return lax.ppermute(x, ('mx', 'my'), pairs)  1.2 us
    pallas_call x1, Pallas kernels, per_device(): pl.pallas_call(bands_kernel, out_shape=[shape(224, BF), shape(256, BF, 25...  0.99 us
    pallas_call x1, Pallas kernels, per_device(): pl.pallas_call(pack_rows_kernel, out_shape=[shape(104), shape(104)], in_s...  0.89 us
  transfers between devices with their start and end apart: 7, of which 4 were waited for; matrix products, arithmetic and copies ran while one was open for 0% of the time, Pallas kernels for 5%

profile of v5, /device:TPU:68, one launch (start us, length us, event | category | flops | bytes accessed | tf_op | source)
XLA Modules:
  0.0 28.9 jit_solution(2776654137741005046)
XLA Ops:
  0.0 0.0 copy-start.4
  0.0 0.0 copy-start.3
  0.7 0.0 copy-done.4
  0.7 0.0 copy-done.3
  0.7 0.0 copy-start
  0.7 0.0 copy-start.1
  0.7 0.9 %shard_map.83 = (f32[104,128]{1,0:T(8,128)S(1)}, f32[104,128]{1,0:T(8,128)S(1)}) custom-call(s32[1,1,16]{2,1,0:T(1,128)S(1)} %copy-done.3, s32[1,1,16]{2,1,0:T(1,128)S(1)} %copy-done.4, s32[1,1]{1,0:T(1,128)S(6)} %copy.13.live_count.live_in, f32[256,128]{1,0:T(8,128)} %friction.3, f32[256,128]{1,0:T(8,128)} %probe.3), custom_call_target="tpu_custom_call" | custom-call | tf_op jit(solution)/shard_map/pallas_call | solution.py:434
  1.6 0.0 copy-start.2
  1.6 0.2 collective-permute-start.1
  1.8 4.9 %collective-permute-start = (f32[104,128]{1,0:T(8,128)S(1)}, f32[104,128]{1,0:T(8,128)S(1)}, u32[]{:S(2)}, u32[]{:S(2)}) collective-permute-start(f32[104,128]{1,0:T(8,128)S(1)} %get-tuple-element.23.mine), channel_id=1, source_target_pairs={{0,32},{1,33},{2,34},{3,35},{4,36},{5,37},{6,38},{7,39},{8,40},{9,... | collective-permute-start | bytes 159752 | tf_op jit(solution)/shard_map/ppermute | solution.py:379
  6.8 0.0 copy-done
  6.8 0.0 copy-done.1
  6.8 0.3 %shard_map.82 = (f32[352,128]{1,0:T(8,128)S(1)}, f32[288,128]{1,0:T(8,128)S(1)}) custom-call(f32[256,128]{1,0:T(8,128)S(1)} %copy-done, f32[256,128]{1,0:T(8,128)S(1)} %copy-done.1), custom_call_target="tpu_custom_call" | custom-call | tf_op jit(solution)/shard_map/pallas_call | solution.py:449
  7.1 0.0 collective-permute-done.1.payload.row_odd
  7.1 1.7 %collective-permute-done.row_even = f32[104,128]{1,0:T(8,128)S(1)} collective-permute-done((f32[104,128]{1,0:T(8,128)S(1)}, f32[104,128]{1,0:T(8,128)S(1)}, u32[]{:S(2)}, u32[]{:S(2)}) %collective-permute-start) | collective-permute-done | bytes 53280 | tf_op jit(solution)/shard_map/ppermute | solution.py:379
  8.9 0.2 shard_map.85
  9.1 0.0 copy-start.5
  9.1 0.0 copy-start.6
  9.1 1.4 %collective-permute-start.3 = (f32[248,128]{1,0:T(8,128)S(1)}, f32[248,128]{1,0:T(8,128)S(1)}, u32[]{:S(2)}, u32[]{:S(2)}) collective-permute-start(f32[248,128]{1,0:T(8,128)S(1)} %get-tuple-element.29), channel_id=1, source_target_pairs={{0,32},{1,2},{2,1},{3,4},{4,3},{5,6},{6,5},{7,8},{8,7},{9,10},{10,... | collective-permute-start | bytes 380936 | tf_op jit(solution)/shard_map/ppermute | solution.py:379
  10.4 0.4 %collective-permute-start.2 = (f32[248,128]{1,0:T(8,128)S(1)}, f32[248,128]{1,0:T(8,128)S(1)}, u32[]{:S(2)}, u32[]{:S(2)}) collective-permute-start(f32[248,128]{1,0:T(8,128)S(1)} %get-tuple-element.28), channel_id=1, source_target_pairs={{0,1},{1,0},{2,3},{3,2},{4,5},{5,4},{6,7},{7,6},{8,9},{9,8},{10,11... | collective-permute-start | bytes 380936 | tf_op jit(solution)/shard_map/ppermute | solution.py:379
  10.9 0.0 copy-done.2
  10.9 0.0 copy-done.5
  10.9 0.0 copy-done.6
  10.9 1.0 %shard_map.87 = (bf16[224,128]{1,0:T(8,128)(2,1)S(1)}, bf16[256,256]{1,0:T(8,128)(2,1)S(1)}, bf16[256,896]{1,0:T(8,128)(2,1)S(1)}) custom-call(f32[17]{0:T(128)S(1)} %copy-done.5, f32[17]{0:T(128)S(1)} %copy-done.6, bf16[256,896]{1,0:T(8,128)(2,1)S(1)} %copy-done.2), custom_call_target="tpu_custom_call" | custom-call | tf_op jit(solution)/shard_map/pallas_call | solution.py:457
  11.9 3.8 %collective-permute-done.3.payload.odd_in = f32[248,128]{1,0:T(8,128)S(1)} collective-permute-done((f32[248,128]{1,0:T(8,128)S(1)}, f32[248,128]{1,0:T(8,128)S(1)}, u32[]{:S(2)}, u32[]{:S(2)}) %collective-permute-start.3) | collective-permute-done | bytes 127008 | tf_op jit(solution)/shard_map/ppermute | solution.py:379
  15.6 0.0 collective-permute-done.2.even_in
  15.6 5.8 %shard_map.88 = (f32[256,128]{1,0:T(8,128)S(1)}, f32[96,128]{1,0:T(8,128)S(1)}, f32[192,128]{1,0:T(8,128)S(1)}, f32[96,128]{1,0:T(8,128)S(1)}) custom-call(s32[1,1,16]{2,1,0:T(1,128)S(1)} %copy-done.3, s32[1,1,16]{2,1,0:T(1,128)S(1)} %copy-done.4, s32[1,1]{1,0:T(1,128)S(6)} %copy.13.live_count.live_in, f32[352,128]{1,0:T(8,128)S(1)} %get-tuple-element.25.fa, ...), custom_call_target="tpu_custom_call" | custom-call | tf_op jit(solution)/shard_map/pallas_call | solution.py:393
  21.5 0.1 collective-permute-start.4
  21.6 1.2 %collective-permute-start.5 = (f32[96,128]{1,0:T(8,128)S(1)}, f32[96,128]{1,0:T(8,128)S(1)}, u32[]{:S(2)}, u32[]{:S(2)}) collective-permute-start(f32[96,128]{1,0:T(8,128)S(1)} %get-tuple-element.35), channel_id=1, source_target_pairs={{0,33},{1,34},{2,35},{3,36},{4,37},{5,38},{6,39},{7,40},{8,41},{9,... | collective-permute-start | bytes 147464 | tf_op jit(solution)/shard_map/ppermute | solution.py:389
  22.8 1.2 %collective-permute-start.6 = (f32[96,128]{1,0:T(8,128)S(1)}, f32[96,128]{1,0:T(8,128)S(1)}, u32[]{:S(2)}, u32[]{:S(2)}) collective-permute-start(f32[96,128]{1,0:T(8,128)S(1)} %get-tuple-element.36), channel_id=1, source_target_pairs={{0,32},{32,64},{64,96},{96,128},{128,160},{160,192},{192,224},{224... | collective-permute-start | bytes 147464 | tf_op jit(solution)/shard_map/ppermute | solution.py:364
  24.0 3.7 %collective-permute-done.4.spill = f32[192,128]{1,0:T(8,128)S(1)} collective-permute-done((f32[192,128]{1,0:T(8,128)S(1)}, f32[192,128]{1,0:T(8,128)S(1)}, u32[]{:S(2)}, u32[]{:S(2)}) %collective-permute-start.4) | collective-permute-done | bytes 98336 | tf_op jit(solution)/shard_map/ppermute | solution.py:364
  27.7 0.1 shard_map.89
  27.8 0.4 %collective-permute-done.5 = f32[96,128]{1,0:T(8,128)S(1)} collective-permute-done((f32[96,128]{1,0:T(8,128)S(1)}, f32[96,128]{1,0:T(8,128)S(1)}, u32[]{:S(2)}, u32[]{:S(2)}) %collective-permute-start.5) | collective-permute-done | bytes 49184 | tf_op jit(solution)/shard_map/ppermute | solution.py:389
  28.2 0.0 collective-permute-done.6
  28.2 0.7 %pad_add_fusion = f32[256,128]{1,0:T(8,128)} fusion(f32[256,128]{1,0:T(8,128)S(1)} %pad_add_fusion.1, f32[96,128]{1,0:T(8,128)S(1)} %collective-permute-done.6), kind=kLoop, calls=%fused_computation | loop fusion | flops 32768 | bytes 311296 | tf_op jit(solution)/shard_map/add | solution.py:490
  (3 shorter events, 0.0 us)
Async XLA Ops:
  0.0 0.7 %copy-start.4 = (s32[1,1,16]{2,1,0:T(1,128)S(1)}, s32[1,1,16]{2,1,0:T(1,128)}, u32[]{:S(2)}) copy-start(s32[1,1,16]{2,1,0:T(1,128)} %win_col_in.1) | copy-start | bytes 196
  0.0 0.7 %copy-start.3 = (s32[1,1,16]{2,1,0:T(1,128)S(1)}, s32[1,1,16]{2,1,0:T(1,128)}, u32[]{:S(2)}) copy-start(s32[1,1,16]{2,1,0:T(1,128)} %win_row_in.1) | copy-start | bytes 196
  0.7 6.1 %copy-start = (f32[256,128]{1,0:T(8,128)S(1)}, f32[256,128]{1,0:T(8,128)}, u32[]{:S(2)}) copy-start(f32[256,128]{1,0:T(8,128)} %friction.3) | copy-start | bytes 393220
  0.7 6.1 %copy-start.1 = (f32[256,128]{1,0:T(8,128)S(1)}, f32[256,128]{1,0:T(8,128)}, u32[]{:S(2)}) copy-start(f32[256,128]{1,0:T(8,128)} %probe.3) | copy-start | bytes 393220
  1.6 9.2 %copy-start.2 = (bf16[256,896]{1,0:T(8,128)(2,1)S(1)}, bf16[256,896]{1,0:T(8,128)(2,1)}, u32[]{:S(2)}) copy-start(bf16[256,896]{1,0:T(8,128)(2,1)} %constant.5.clone.tables_in) | copy-start | bytes 1376260
  1.6 5.5 %collective-permute-start.1 = (f32[104,128]{1,0:T(8,128)S(1)}, f32[104,128]{1,0:T(8,128)S(1)}, u32[]{:S(2)}, u32[]{:S(2)}) collective-permute-start(f32[104,128]{1,0:T(8,128)S(1)} %get-tuple-element.24), channel_id=1, source_target_pairs={{0,1},{1,0},{2,3},{3,2},{4,5},{5,4},{6,7},{7,6},{8,9},{9,8},{10,11... | collective-permute-start | bytes 159752 | tf_op jit(solution)/shard_map/ppermute | solution.py:379
  1.8 7.0 %collective-permute-start = (f32[104,128]{1,0:T(8,128)S(1)}, f32[104,128]{1,0:T(8,128)S(1)}, u32[]{:S(2)}, u32[]{:S(2)}) collective-permute-start(f32[104,128]{1,0:T(8,128)S(1)} %get-tuple-element.23.mine), channel_id=1, source_target_pairs={{0,32},{1,33},{2,34},{3,35},{4,36},{5,37},{6,38},{7,39},{8,40},{9,... | collective-permute-start | bytes 159752 | tf_op jit(solution)/shard_map/ppermute | solution.py:379
  9.1 1.8 %copy-start.5 = (f32[17]{0:T(128)S(1)}, f32[17]{0:T(128)}, u32[]{:S(2)}) copy-start(f32[17]{0:T(128)} %taps_row.1) | copy-start | bytes 208
  9.1 1.8 %copy-start.6 = (f32[17]{0:T(128)S(1)}, f32[17]{0:T(128)}, u32[]{:S(2)}) copy-start(f32[17]{0:T(128)} %taps_col.1) | copy-start | bytes 208
  9.1 6.5 %collective-permute-start.3 = (f32[248,128]{1,0:T(8,128)S(1)}, f32[248,128]{1,0:T(8,128)S(1)}, u32[]{:S(2)}, u32[]{:S(2)}) collective-permute-start(f32[248,128]{1,0:T(8,128)S(1)} %get-tuple-element.29), channel_id=1, source_target_pairs={{0,32},{1,2},{2,1},{3,4},{4,3},{5,6},{6,5},{7,8},{8,7},{9,10},{10,... | collective-permute-start | bytes 380936 | tf_op jit(solution)/shard_map/ppermute | solution.py:379
  10.4 5.2 %collective-permute-start.2 = (f32[248,128]{1,0:T(8,128)S(1)}, f32[248,128]{1,0:T(8,128)S(1)}, u32[]{:S(2)}, u32[]{:S(2)}) collective-permute-start(f32[248,128]{1,0:T(8,128)S(1)} %get-tuple-element.28), channel_id=1, source_target_pairs={{0,1},{1,0},{2,3},{3,2},{4,5},{5,4},{6,7},{7,6},{8,9},{9,8},{10,11... | collective-permute-start | bytes 380936 | tf_op jit(solution)/shard_map/ppermute | solution.py:379
  21.5 6.2 %collective-permute-start.4 = (f32[192,128]{1,0:T(8,128)S(1)}, f32[192,128]{1,0:T(8,128)S(1)}, u32[]{:S(2)}, u32[]{:S(2)}) collective-permute-start(f32[192,128]{1,0:T(8,128)S(1)} %get-tuple-element.34), channel_id=1, source_target_pairs={{0,1},{1,2},{2,3},{3,4},{4,5},{5,6},{6,7},{7,8},{8,9},{9,10},{10,1... | collective-permute-start | bytes 294920 | tf_op jit(solution)/shard_map/ppermute | solution.py:364
  21.6 6.7 %collective-permute-start.5 = (f32[96,128]{1,0:T(8,128)S(1)}, f32[96,128]{1,0:T(8,128)S(1)}, u32[]{:S(2)}, u32[]{:S(2)}) collective-permute-start(f32[96,128]{1,0:T(8,128)S(1)} %get-tuple-element.35), channel_id=1, source_target_pairs={{0,33},{1,34},{2,35},{3,36},{4,37},{5,38},{6,39},{7,40},{8,41},{9,... | collective-permute-start | bytes 147464 | tf_op jit(solution)/shard_map/ppermute | solution.py:389
  22.8 5.5 %collective-permute-start.6 = (f32[96,128]{1,0:T(8,128)S(1)}, f32[96,128]{1,0:T(8,128)S(1)}, u32[]{:S(2)}, u32[]{:S(2)}) collective-permute-start(f32[96,128]{1,0:T(8,128)S(1)} %get-tuple-element.36), channel_id=1, source_target_pairs={{0,32},{32,64},{64,96},{96,128},{128,160},{160,192},{192,224},{224... | collective-permute-start | bytes 147464 | tf_op jit(solution)/shard_map/ppermute | solution.py:364

commit v6 on v5

--- a/solution.py
+++ b/solution.py
@@ -88,7 +88,9 @@
     return lax.axis_index(axis), lax.axis_size(axis)
 
 
-def pack_rows_kernel(win_row, win_col, live_count, friction, probe, even_out, odd_out, rows, cols, count, sems):
+def pack_rows_kernel(
+    win_row, win_col, live_count, friction, probe, even_out, odd_out, scalars, rows, cols, count, sems
+):
     def fetch(down, up):
         return [
             pltpu.make_async_copy(friction.at[pl.ds(TILE_R - UP, UP)], down.at[pl.ds(0, UP)], sems.at[3]),
@@ -124,6 +126,10 @@
     wide = jnp.concatenate([jnp.concatenate([x, jnp.zeros((1, LANES - SLOTS), F32)], 1) for x in (row, col)], 0)
     turned = pltpu.roll(wide, LANES - 2, 1)
     info = jnp.concatenate([wide[0:1], turned[0:1], wide[1:2], turned[1:2], jnp.zeros((4, LANES), F32)], 0)
+    none = jnp.zeros((1, LANES - SLOTS), jnp.int32)
+    many = jnp.broadcast_to(count[...], (1, SLOTS))
+    whole = [jnp.concatenate([x, none], 1) for x in (rows[...], cols[...], many)]
+    scalars[...] = jnp.concatenate(whole + [jnp.zeros((5, LANES), jnp.int32)], 0)
     even_out[96:104, :] = info
     odd_out[96:104, :] = info
     for copy in fetch(even_out, odd_out):
@@ -192,16 +198,11 @@
 
 
 def core_kernel(
-    win_row_in, win_col_in, live_in, fa, pa, infos, even_in, odd_in, odd_slots, bands, col_band, tables,
-    own, own_low, side, side_low, oa, ob, fb, pb, fw, y2, z, comb, spec, wide, win_row, win_col, live_count, from_left, from_right, sems,
+    scalars_in, fa, pa, infos, even_in, odd_in, odd_slots, bands, col_band, tables,
+    own, own_low, side, side_low, oa, ob, fb, pb, fw, y2, z, comb, spec, wide, scalars, from_left, from_right, sem,
 ):
-    scalar_copies = [
-        pltpu.make_async_copy(win_row_in, win_row, sems.at[1]),
-        pltpu.make_async_copy(win_col_in, win_col, sems.at[2]),
-        pltpu.make_async_copy(live_in, live_count, sems.at[3]),
-    ]
-    for copy in scalar_copies:
-        copy.start()
+    scalar_copy = pltpu.make_async_copy(scalars_in, scalars, sem)
+    scalar_copy.start()
     at_col, col_count = own_index("my")
     leftmost, rightmost = at_col == 0, at_col == col_count - 1
     is_even = lax.rem(at_col, 2) == 0
@@ -254,11 +255,10 @@
         for m in range(2):
             hi, lo = split(t[:, 128 * m : 128 * m + 128])
             y2[pl.ds((k + m) * 112, 112), :] = jnp.concatenate([hi, lo], 1)
-    for copy in scalar_copies:
-        copy.wait()
+    scalar_copy.wait()
     for k in range(SLOTS):
-        rows = pl.ds(win_row[0, 0, k], 128)
-        fw[k] = window(fa[rows, :], fb[rows, :], win_col[0, 0, k] - 32)
+        rows = pl.ds(scalars[0, k], 128)
+        fw[k] = window(fa[rows, :], fb[rows, :], scalars[1, k] - 32)
     first, n = 8, 112
     while True:
         o = halves(dot(y2[0 : SLOTS * n, :], col_band[...]), 1)
@@ -285,8 +285,8 @@
 
     ker_hi, ker_lo = lane_transform(o.reshape(SLOTS * PATCH, 128))
     for k in range(SLOTS):
-        rows = pl.ds(win_row[0, 0, k], PATCH)
-        z[pl.ds(k * PATCH, PATCH), :] = window(pa[rows, :], pb[rows, :], win_col[0, 0, k] - 32)
+        rows = pl.ds(scalars[0, k], PATCH)
+        z[pl.ds(k * PATCH, PATCH), :] = window(pa[rows, :], pb[rows, :], scalars[1, k] - 32)
     win_hi, win_lo = lane_transform(z[...])
     left_half = lax.broadcasted_iota(jnp.int32, (PATCH, 128), 1) < 64
     sign = jnp.where(left_half, -1.0, 1.0)
@@ -323,10 +323,10 @@
         t = halves(dot(tables[:, 512:768], wide[k // 2]), 0)
         for m in range(2):
             kk = k + m
-            col = win_col[0, 0, kk]
-            live = jnp.where(kk < live_count[0, 0], 1.0, 0.0)
+            col = scalars[1, kk]
+            live = jnp.where(kk < scalars[2, 0], 1.0, 0.0)
             patch = pltpu.roll(t[:, 128 * m : 128 * m + 128] * live, col, 1)
-            rows = pl.ds(win_row[0, 0, kk], 128)
+            rows = pl.ds(scalars[0, kk], 128)
             oa[rows, :] += jnp.where(lane128 >= col, patch, 0.0)
             ob[rows, :] += jnp.where(lane128 < col, patch, 0.0)
     at_row, row_count = own_index("mx")
@@ -389,11 +389,11 @@
     return lax.ppermute(x, ("mx", "my"), pairs)
 
 
-def core_call(win_row, win_col, live_count, fa, pa, infos, even_in, odd_in, odd_slots, bands, col_band, tables):
+def core_call(scalars, fa, pa, infos, even_in, odd_in, odd_slots, bands, col_band, tables):
     return pl.pallas_call(
         core_kernel,
         out_shape=[shape(TILE_R), shape(OUT_R - TILE_R), shape(192), shape(OUT_R - TILE_R)],
-        in_specs=[ANY] * 3 + [VMEM] * 9,
+        in_specs=[VMEM] * 10,
         out_specs=[VMEM] * 4,
         scratch_shapes=[
             pltpu.VMEM((OUT_R, LANES), F32),
@@ -406,16 +406,14 @@
             pltpu.VMEM((SLOTS // 2, 128, 256), BF),
             pltpu.VMEM((SLOTS * 128, 256), BF),
             pltpu.VMEM((SLOTS // 2, 256, 256), BF),
-            pltpu.SMEM((1, 1, SLOTS), jnp.int32),
-            pltpu.SMEM((1, 1, SLOTS), jnp.int32),
-            pltpu.SMEM((1, 1), jnp.int32),
+            pltpu.SMEM((8, LANES), jnp.int32),
             pltpu.VMEM((248, LANES), F32),
             pltpu.VMEM((248, LANES), F32),
-            pltpu.SemaphoreType.DMA((4,)),
+            pltpu.SemaphoreType.DMA,
         ],
         compiler_params=pltpu.CompilerParams(vmem_limit_bytes=40 * 2**20),
     )(
-        win_row, win_col, live_count, fa, pa, infos, even_in, odd_in, odd_slots, bands, col_band, tables,
+        scalars, fa, pa, infos, even_in, odd_in, odd_slots, bands, col_band, tables,
     )
 
 
@@ -431,11 +429,11 @@
 
 def per_device(friction, taps_row, taps_col, probe, win_row, win_col, live_count):
     params = pltpu.CompilerParams(vmem_limit_bytes=40 * 2**20)
-    row_even_out, row_odd_out = pl.pallas_call(
+    row_even_out, row_odd_out, scalars = pl.pallas_call(
         pack_rows_kernel,
-        out_shape=[shape(104), shape(104)],
+        out_shape=[shape(104), shape(104), shape(8, jnp.int32)],
         in_specs=[ANY] * 5,
-        out_specs=[VMEM] * 2,
+        out_specs=[VMEM] * 3,
         scratch_shapes=[
             pltpu.VMEM((1, SLOTS), jnp.int32),
             pltpu.VMEM((1, SLOTS), jnp.int32),
@@ -473,7 +471,7 @@
     odd_in = swap(odd_out, "my", True)
     even_in = swap(even_out, "my", False)
     own, own_low, side, side_low = core_call(
-        win_row, win_col, live_count, fa, pa, infos, even_in, odd_in, peek(odd_in, params), bands, col_band, tables
+        scalars, fa, pa, infos, even_in, odd_in, peek(odd_in, params), bands, col_band, tables
     )
     spill = ring(side, "my", 1)
     corner = diagonal(side_low)

time: 29.4 us -> 29 us (0.986)
  Pallas kernels: 8.32 us -> 7.93 us
    pallas_call x1, Pallas kernels: 5.83 us -> 5.44 us  [core_call(): pl.pallas_call(core_kernel, out_shape=[shape(TILE_R), shape(OUT_R - TILE_...]
where the time goes in v6:
time: 29 us; the launch traced here: 28.5 us
  waiting for transfers between devices  9.65 us (33%)
  starting transfers between devices  9.41 us (32%)
  Pallas kernels  7.93 us (27%)
  between operations  0.83 us (3%)
  other arithmetic  0.68 us (2%)
    ppermute x4, starting transfers between devices, swap(): return lax.ppermute(x, ('mx', 'my'), pairs)  6.91 us
    ppermute x4, waiting for transfers between devices, swap(): return lax.ppermute(x, ('mx', 'my'), pairs)  5.5 us
    pallas_call x1, Pallas kernels, core_call(): pl.pallas_call(core_kernel, out_shape=[shape(TILE_R), shape(OUT_R - TILE_...  5.44 us
    ppermute x2, waiting for transfers between devices, ring(): return lax.ppermute(x, axis, [(i, (i + by) % count) for i in range(count)])  3.74 us
    ppermute x2, starting transfers between devices, ring(): return lax.ppermute(x, axis, [(i, (i + by) % count) for i in range(count)])  1.33 us
    ppermute x1, starting transfers between devices, diagonal(): return lax.ppermute(x, ('mx', 'my'), pairs)  1.17 us
    pallas_call x1, Pallas kernels, per_device(): pl.pallas_call(bands_kernel, out_shape=[shape(224, BF), shape(256, BF, 25...  0.99 us
    pallas_call x1, Pallas kernels, per_device(): pl.pallas_call(pack_rows_kernel, out_shape=[shape(104), shape(104), shape...  0.89 us
  transfers between devices with their start and end apart: 7, of which 4 were waited for; matrix products, arithmetic and copies ran while one was open for 0% of the time, Pallas kernels for 5%

profile of v6, /device:TPU:68, one launch (start us, length us, event | category | flops | bytes accessed | tf_op | source)
XLA Modules:
  0.0 28.5 jit_solution(5663006986226837680)
XLA Ops:
  0.0 0.0 copy-start.4
  0.0 0.0 copy-start.3
  0.7 0.0 copy-done.4
  0.7 0.0 copy-done.3
  0.7 0.0 copy-start
  0.7 0.0 copy-start.1
  0.7 0.9 %shard_map.82 = (f32[104,128]{1,0:T(8,128)S(1)}, f32[104,128]{1,0:T(8,128)S(1)}, s32[8,128]{1,0:T(8,128)S(1)}) custom-call(s32[1,1,16]{2,1,0:T(1,128)S(1)} %copy-done.3, s32[1,1,16]{2,1,0:T(1,128)S(1)} %copy-done.4, s32[1,1]{1,0:T(1,128)S(6)} %copy.13.live_count, f32[256,128]{1,0:T(8,128)} %friction.3, f32[256,128]{1,0:T(8,128)} %probe.3), custom_call_target="tpu_custom_call" | custom-call | tf_op jit(solution)/shard_map/pallas_call | solution.py:432
  1.6 0.0 copy-start.2
  1.6 0.2 collective-permute-start.1
  1.8 4.9 %collective-permute-start = (f32[104,128]{1,0:T(8,128)S(1)}, f32[104,128]{1,0:T(8,128)S(1)}, u32[]{:S(2)}, u32[]{:S(2)}) collective-permute-start(f32[104,128]{1,0:T(8,128)S(1)} %get-tuple-element.25.mine), channel_id=1, source_target_pairs={{0,32},{1,33},{2,34},{3,35},{4,36},{5,37},{6,38},{7,39},{8,40},{9,... | collective-permute-start | bytes 159752 | tf_op jit(solution)/shard_map/ppermute | solution.py:379
  6.8 0.0 copy-done
  6.8 0.0 copy-done.1
  6.8 0.3 %shard_map.83 = (f32[352,128]{1,0:T(8,128)S(1)}, f32[288,128]{1,0:T(8,128)S(1)}) custom-call(f32[256,128]{1,0:T(8,128)S(1)} %copy-done, f32[256,128]{1,0:T(8,128)S(1)} %copy-done.1), custom_call_target="tpu_custom_call" | custom-call | tf_op jit(solution)/shard_map/pallas_call | solution.py:447
  7.1 0.0 collective-permute-done.1.payload.row_odd
  7.1 1.7 %collective-permute-done.row_even = f32[104,128]{1,0:T(8,128)S(1)} collective-permute-done((f32[104,128]{1,0:T(8,128)S(1)}, f32[104,128]{1,0:T(8,128)S(1)}, u32[]{:S(2)}, u32[]{:S(2)}) %collective-permute-start) | collective-permute-done | bytes 53280 | tf_op jit(solution)/shard_map/ppermute | solution.py:379
  8.9 0.2 shard_map.85
  9.1 0.0 copy-start.5
  9.1 0.0 copy-start.6
  9.1 1.4 %collective-permute-start.3 = (f32[248,128]{1,0:T(8,128)S(1)}, f32[248,128]{1,0:T(8,128)S(1)}, u32[]{:S(2)}, u32[]{:S(2)}) collective-permute-start(f32[248,128]{1,0:T(8,128)S(1)} %get-tuple-element.31), channel_id=1, source_target_pairs={{0,32},{1,2},{2,1},{3,4},{4,3},{5,6},{6,5},{7,8},{8,7},{9,10},{10,... | collective-permute-start | bytes 380936 | tf_op jit(solution)/shard_map/ppermute | solution.py:379
  10.4 0.4 %collective-permute-start.2 = (f32[248,128]{1,0:T(8,128)S(1)}, f32[248,128]{1,0:T(8,128)S(1)}, u32[]{:S(2)}, u32[]{:S(2)}) collective-permute-start(f32[248,128]{1,0:T(8,128)S(1)} %get-tuple-element.30), channel_id=1, source_target_pairs={{0,1},{1,0},{2,3},{3,2},{4,5},{5,4},{6,7},{7,6},{8,9},{9,8},{10,11... | collective-permute-start | bytes 380936 | tf_op jit(solution)/shard_map/ppermute | solution.py:379
  10.9 0.0 copy-done.2
  10.9 0.0 copy-done.5
  10.9 0.0 copy-done.6
  10.9 1.0 %shard_map.87 = (bf16[224,128]{1,0:T(8,128)(2,1)S(1)}, bf16[256,256]{1,0:T(8,128)(2,1)S(1)}, bf16[256,896]{1,0:T(8,128)(2,1)S(1)}) custom-call(f32[17]{0:T(128)S(1)} %copy-done.5, f32[17]{0:T(128)S(1)} %copy-done.6, bf16[256,896]{1,0:T(8,128)(2,1)S(1)} %copy-done.2), custom_call_target="tpu_custom_call" | custom-call | tf_op jit(solution)/shard_map/pallas_call | solution.py:455
  11.9 3.8 %collective-permute-done.3.payload.odd_in = f32[248,128]{1,0:T(8,128)S(1)} collective-permute-done((f32[248,128]{1,0:T(8,128)S(1)}, f32[248,128]{1,0:T(8,128)S(1)}, u32[]{:S(2)}, u32[]{:S(2)}) %collective-permute-start.3) | collective-permute-done | bytes 127008 | tf_op jit(solution)/shard_map/ppermute | solution.py:379
  15.6 0.0 collective-permute-done.2.even_in
  15.6 5.4 %shard_map.88 = (f32[256,128]{1,0:T(8,128)S(1)}, f32[96,128]{1,0:T(8,128)S(1)}, f32[192,128]{1,0:T(8,128)S(1)}, f32[96,128]{1,0:T(8,128)S(1)}) custom-call(s32[8,128]{1,0:T(8,128)S(1)} %get-tuple-element.22.scalars_in, f32[352,128]{1,0:T(8,128)S(1)} %get-tuple-element.27.fa, f32[288,128]{1,0:T(8,128)S(1)} %get-tuple-element.28.pa, ...), custom_call_target="tpu_custom_call" | custom-call | tf_op jit(solution)/shard_map/pallas_call | solution.py:393
  21.1 0.1 collective-permute-start.4
  21.2 1.2 %collective-permute-start.5 = (f32[96,128]{1,0:T(8,128)S(1)}, f32[96,128]{1,0:T(8,128)S(1)}, u32[]{:S(2)}, u32[]{:S(2)}) collective-permute-start(f32[96,128]{1,0:T(8,128)S(1)} %get-tuple-element.37), channel_id=1, source_target_pairs={{0,33},{1,34},{2,35},{3,36},{4,37},{5,38},{6,39},{7,40},{8,41},{9,... | collective-permute-start | bytes 147464 | tf_op jit(solution)/shard_map/ppermute | solution.py:389
  22.3 1.2 %collective-permute-start.6 = (f32[96,128]{1,0:T(8,128)S(1)}, f32[96,128]{1,0:T(8,128)S(1)}, u32[]{:S(2)}, u32[]{:S(2)}) collective-permute-start(f32[96,128]{1,0:T(8,128)S(1)} %get-tuple-element.38), channel_id=1, source_target_pairs={{0,32},{32,64},{64,96},{96,128},{128,160},{160,192},{192,224},{224... | collective-permute-start | bytes 147464 | tf_op jit(solution)/shard_map/ppermute | solution.py:364
  23.6 3.7 %collective-permute-done.4.spill = f32[192,128]{1,0:T(8,128)S(1)} collective-permute-done((f32[192,128]{1,0:T(8,128)S(1)}, f32[192,128]{1,0:T(8,128)S(1)}, u32[]{:S(2)}, u32[]{:S(2)}) %collective-permute-start.4) | collective-permute-done | bytes 98336 | tf_op jit(solution)/shard_map/ppermute | solution.py:364
  27.3 0.1 shard_map.89
  27.4 0.4 %collective-permute-done.5 = f32[96,128]{1,0:T(8,128)S(1)} collective-permute-done((f32[96,128]{1,0:T(8,128)S(1)}, f32[96,128]{1,0:T(8,128)S(1)}, u32[]{:S(2)}, u32[]{:S(2)}) %collective-permute-start.5) | collective-permute-done | bytes 49184 | tf_op jit(solution)/shard_map/ppermute | solution.py:389
  27.9 0.0 collective-permute-done.6
  27.9 0.7 %pad_add_fusion = f32[256,128]{1,0:T(8,128)} fusion(f32[256,128]{1,0:T(8,128)S(1)} %pad_add_fusion.1, f32[96,128]{1,0:T(8,128)S(1)} %collective-permute-done.6), kind=kLoop, calls=%fused_computation | loop fusion | flops 32768 | bytes 311296 | tf_op jit(solution)/shard_map/add | solution.py:488
  (3 shorter events, 0.0 us)
Async XLA Ops:
  0.0 0.7 %copy-start.4 = (s32[1,1,16]{2,1,0:T(1,128)S(1)}, s32[1,1,16]{2,1,0:T(1,128)}, u32[]{:S(2)}) copy-start(s32[1,1,16]{2,1,0:T(1,128)} %win_col.1) | copy-start | bytes 196
  0.0 0.7 %copy-start.3 = (s32[1,1,16]{2,1,0:T(1,128)S(1)}, s32[1,1,16]{2,1,0:T(1,128)}, u32[]{:S(2)}) copy-start(s32[1,1,16]{2,1,0:T(1,128)} %win_row.1) | copy-start | bytes 196
  0.7 6.1 %copy-start = (f32[256,128]{1,0:T(8,128)S(1)}, f32[256,128]{1,0:T(8,128)}, u32[]{:S(2)}) copy-start(f32[256,128]{1,0:T(8,128)} %friction.3) | copy-start | bytes 393220
  0.7 6.1 %copy-start.1 = (f32[256,128]{1,0:T(8,128)S(1)}, f32[256,128]{1,0:T(8,128)}, u32[]{:S(2)}) copy-start(f32[256,128]{1,0:T(8,128)} %probe.3) | copy-start | bytes 393220
  1.6 9.2 %copy-start.2 = (bf16[256,896]{1,0:T(8,128)(2,1)S(1)}, bf16[256,896]{1,0:T(8,128)(2,1)}, u32[]{:S(2)}) copy-start(bf16[256,896]{1,0:T(8,128)(2,1)} %constant.5.clone.tables_in) | copy-start | bytes 1376260
  1.6 5.5 %collective-permute-start.1 = (f32[104,128]{1,0:T(8,128)S(1)}, f32[104,128]{1,0:T(8,128)S(1)}, u32[]{:S(2)}, u32[]{:S(2)}) collective-permute-start(f32[104,128]{1,0:T(8,128)S(1)} %get-tuple-element.26), channel_id=1, source_target_pairs={{0,1},{1,0},{2,3},{3,2},{4,5},{5,4},{6,7},{7,6},{8,9},{9,8},{10,11... | collective-permute-start | bytes 159752 | tf_op jit(solution)/shard_map/ppermute | solution.py:379
  1.8 7.0 %collective-permute-start = (f32[104,128]{1,0:T(8,128)S(1)}, f32[104,128]{1,0:T(8,128)S(1)}, u32[]{:S(2)}, u32[]{:S(2)}) collective-permute-start(f32[104,128]{1,0:T(8,128)S(1)} %get-tuple-element.25.mine), channel_id=1, source_target_pairs={{0,32},{1,33},{2,34},{3,35},{4,36},{5,37},{6,38},{7,39},{8,40},{9,... | collective-permute-start | bytes 159752 | tf_op jit(solution)/shard_map/ppermute | solution.py:379
  9.1 1.8 %copy-start.5 = (f32[17]{0:T(128)S(1)}, f32[17]{0:T(128)}, u32[]{:S(2)}) copy-start(f32[17]{0:T(128)} %taps_row.1) | copy-start | bytes 208
  9.1 1.8 %copy-start.6 = (f32[17]{0:T(128)S(1)}, f32[17]{0:T(128)}, u32[]{:S(2)}) copy-start(f32[17]{0:T(128)} %taps_col.1) | copy-start | bytes 208
  9.1 6.5 %collective-permute-start.3 = (f32[248,128]{1,0:T(8,128)S(1)}, f32[248,128]{1,0:T(8,128)S(1)}, u32[]{:S(2)}, u32[]{:S(2)}) collective-permute-start(f32[248,128]{1,0:T(8,128)S(1)} %get-tuple-element.31), channel_id=1, source_target_pairs={{0,32},{1,2},{2,1},{3,4},{4,3},{5,6},{6,5},{7,8},{8,7},{9,10},{10,... | collective-permute-start | bytes 380936 | tf_op jit(solution)/shard_map/ppermute | solution.py:379
  10.4 5.2 %collective-permute-start.2 = (f32[248,128]{1,0:T(8,128)S(1)}, f32[248,128]{1,0:T(8,128)S(1)}, u32[]{:S(2)}, u32[]{:S(2)}) collective-permute-start(f32[248,128]{1,0:T(8,128)S(1)} %get-tuple-element.30), channel_id=1, source_target_pairs={{0,1},{1,0},{2,3},{3,2},{4,5},{5,4},{6,7},{7,6},{8,9},{9,8},{10,11... | collective-permute-start | bytes 380936 | tf_op jit(solution)/shard_map/ppermute | solution.py:379
  21.1 6.2 %collective-permute-start.4 = (f32[192,128]{1,0:T(8,128)S(1)}, f32[192,128]{1,0:T(8,128)S(1)}, u32[]{:S(2)}, u32[]{:S(2)}) collective-permute-start(f32[192,128]{1,0:T(8,128)S(1)} %get-tuple-element.36), channel_id=1, source_target_pairs={{0,1},{1,2},{2,3},{3,4},{4,5},{5,6},{6,7},{7,8},{8,9},{9,10},{10,1... | collective-permute-start | bytes 294920 | tf_op jit(solution)/shard_map/ppermute | solution.py:364
  21.2 6.7 %collective-permute-start.5 = (f32[96,128]{1,0:T(8,128)S(1)}, f32[96,128]{1,0:T(8,128)S(1)}, u32[]{:S(2)}, u32[]{:S(2)}) collective-permute-start(f32[96,128]{1,0:T(8,128)S(1)} %get-tuple-element.37), channel_id=1, source_target_pairs={{0,33},{1,34},{2,35},{3,36},{4,37},{5,38},{6,39},{7,40},{8,41},{9,... | collective-permute-start | bytes 147464 | tf_op jit(solution)/shard_map/ppermute | solution.py:389
  22.3 5.5 %collective-permute-start.6 = (f32[96,128]{1,0:T(8,128)S(1)}, f32[96,128]{1,0:T(8,128)S(1)}, u32[]{:S(2)}, u32[]{:S(2)}) collective-permute-start(f32[96,128]{1,0:T(8,128)S(1)} %get-tuple-element.38), channel_id=1, source_target_pairs={{0,32},{32,64},{64,96},{96,128},{128,160},{160,192},{192,224},{224... | collective-permute-start | bytes 147464 | tf_op jit(solution)/shard_map/ppermute | solution.py:364

commit v7 on v6

--- a/solution.py
+++ b/solution.py
@@ -333,7 +333,11 @@
     inner = at_row < row_count - 1
     own[...] = oa[0:TILE_R, :]
     own_low[...] = jnp.where(inner, oa[TILE_R:OUT_R, :], 0.0)
-    side_low[...] = jnp.where(inner & jnp.logical_not(rightmost), ob[TILE_R:OUT_R, :], 0.0)
+    free = lax.broadcasted_iota(jnp.int32, (24, LANES), 1) >= 96
+    for i in range(3):
+        rest = pltpu.roll(ob[TILE_R + 72 : OUT_R, :], 96 - 32 * i, 1)
+        piece = jnp.where(free, rest, ob[TILE_R + 24 * i : TILE_R + 24 * i + 24, :])
+        side_low[24 * i : 24 * i + 24, :] = jnp.where(inner & jnp.logical_not(rightmost), piece, 0.0)
     free = lax.broadcasted_iota(jnp.int32, (64, LANES), 1) >= 96
     for i in range(3):
         rows = slice(64 * i, 64 * i + 64)
@@ -343,6 +347,17 @@
 
 def peek_kernel(payload, slots):
     slots[...] = payload[payload.shape[0] - 8 :, :]
+
+
+def add_low_kernel(own, corner, total):
+    lane = lax.broadcasted_iota(jnp.int32, (24, LANES), 1)
+    last = jnp.zeros((24, LANES), F32)
+    for i in range(3):
+        rows = slice(24 * i, 24 * i + 24)
+        total[rows, :] = own[rows, :] + jnp.where(lane < 96, corner[rows, :], 0.0)
+        last = jnp.where(lane // 32 == i, pltpu.roll(corner[rows, :], (32 + 32 * i) % 128, 1), last)
+    total[72:96, :] = own[72:96, :] + last
+    total[96:TILE_R, :] = own[96:TILE_R, :]
 
 
 def add_side_kernel(own, spill, total):
@@ -392,7 +407,7 @@
 def core_call(scalars, fa, pa, infos, even_in, odd_in, odd_slots, bands, col_band, tables):
     return pl.pallas_call(
         core_kernel,
-        out_shape=[shape(TILE_R), shape(OUT_R - TILE_R), shape(192), shape(OUT_R - TILE_R)],
+        out_shape=[shape(TILE_R), shape(OUT_R - TILE_R), shape(192), shape(72)],
         in_specs=[VMEM] * 10,
         out_specs=[VMEM] * 4,
         scratch_shapes=[
@@ -476,6 +491,7 @@
     spill = ring(side, "my", 1)
     corner = diagonal(side_low)
     lower = ring(own_low, "mx", 1)
+    below = ((0, TILE_R - lower.shape[0]), (0, 0))
     total = pl.pallas_call(
         add_side_kernel,
         out_shape=shape(TILE_R),
@@ -483,8 +499,13 @@
         out_specs=VMEM,
         compiler_params=params,
     )(own, spill)
-    below = ((0, TILE_R - corner.shape[0]), (0, 0))
-    total = lax.optimization_barrier(total + jnp.pad(corner, below))
+    total = pl.pallas_call(
+        add_low_kernel,
+        out_shape=shape(TILE_R),
+        in_specs=[VMEM] * 2,
+        out_specs=VMEM,
+        compiler_params=params,
+    )(total, corner)
     return total + jnp.pad(lower, below)
 
 

time: 29 us -> 30.7 us (1.059)
  waiting for transfers between devices: 9.65 us -> 11.7 us
    ppermute x1, waiting for transfers between devices: 0.42 us -> 2.26 us  [diagonal(): return lax.ppermute(x, ('mx', 'my'), pairs)]
    ppermute x1, starting transfers between devices: 1.17 us -> 0.05 us  [diagonal(): return lax.ppermute(x, ('mx', 'my'), pairs)]
    ppermute x2, starting transfers between devices: 1.33 us -> 2.19 us  [ring(): return lax.ppermute(x, axis, [(i, (i + by) % count) for i in range(count)])]
where the time goes in v7:
time: 30.7 us; the launch traced here: 30.5 us
  waiting for transfers between devices  11.7 us (38%)
  starting transfers between devices  9.14 us (30%)
  Pallas kernels  8.08 us (26%)
  between operations  0.81 us (3%)
  other arithmetic  0.67 us (2%)
    ppermute x4, starting transfers between devices, swap(): return lax.ppermute(x, ('mx', 'my'), pairs)  6.91 us
    pallas_call x1, Pallas kernels, core_call(): pl.pallas_call(core_kernel, out_shape=[shape(TILE_R), shape(OUT_R - TILE_...  5.5 us
    ppermute x4, waiting for transfers between devices, swap(): return lax.ppermute(x, ('mx', 'my'), pairs)  5.5 us
    ppermute x2, waiting for transfers between devices, ring(): return lax.ppermute(x, axis, [(i, (i + by) % count) for i in range(count)])  3.99 us
    ppermute x1, waiting for transfers between devices, diagonal(): return lax.ppermute(x, ('mx', 'my'), pairs)  2.26 us
    ppermute x2, starting transfers between devices, ring(): return lax.ppermute(x, axis, [(i, (i + by) % count) for i in range(count)])  2.19 us
    pallas_call x1, Pallas kernels, per_device(): pl.pallas_call(bands_kernel, out_shape=[shape(224, BF), shape(256, BF, 25...  0.99 us
    pallas_call x1, Pallas kernels, per_device(): pl.pallas_call(pack_rows_kernel, out_shape=[shape(104), shape(104), shape...  0.89 us
  transfers between devices with their start and end apart: 7, of which 4 were waited for; matrix products, arithmetic and copies ran while one was open for 0% of the time, Pallas kernels for 5%

profile of v7, /device:TPU:68, one launch (start us, length us, event | category | flops | bytes accessed | tf_op | source)
XLA Modules:
  0.0 30.5 jit_solution(9844535110603636284)
XLA Ops:
  0.0 0.0 copy-start.4
  0.0 0.0 copy-start.3
  0.7 0.0 copy-done.4
  0.7 0.0 copy-done.3
  0.7 0.0 copy-start
  0.7 0.0 copy-start.1
  0.7 0.9 %shard_map.82 = (f32[104,128]{1,0:T(8,128)S(1)}, f32[104,128]{1,0:T(8,128)S(1)}, s32[8,128]{1,0:T(8,128)S(1)}) custom-call(s32[1,1,16]{2,1,0:T(1,128)S(1)} %copy-done.3, s32[1,1,16]{2,1,0:T(1,128)S(1)} %copy-done.4, s32[1,1]{1,0:T(1,128)S(6)} %copy.13.live_count, f32[256,128]{1,0:T(8,128)} %friction.3, f32[256,128]{1,0:T(8,128)} %probe.3), custom_call_target="tpu_custom_call" | custom-call | tf_op jit(solution)/shard_map/pallas_call | solution.py:447
  1.6 0.0 copy-start.2
  1.6 0.2 collective-permute-start.1
  1.8 4.9 %collective-permute-start = (f32[104,128]{1,0:T(8,128)S(1)}, f32[104,128]{1,0:T(8,128)S(1)}, u32[]{:S(2)}, u32[]{:S(2)}) collective-permute-start(f32[104,128]{1,0:T(8,128)S(1)} %get-tuple-element.25.mine), channel_id=1, source_target_pairs={{0,32},{1,33},{2,34},{3,35},{4,36},{5,37},{6,38},{7,39},{8,40},{9,... | collective-permute-start | bytes 159752 | tf_op jit(solution)/shard_map/ppermute | solution.py:394
  6.8 0.0 copy-done
  6.8 0.0 copy-done.1
  6.8 0.3 %shard_map.83 = (f32[352,128]{1,0:T(8,128)S(1)}, f32[288,128]{1,0:T(8,128)S(1)}) custom-call(f32[256,128]{1,0:T(8,128)S(1)} %copy-done, f32[256,128]{1,0:T(8,128)S(1)} %copy-done.1), custom_call_target="tpu_custom_call" | custom-call | tf_op jit(solution)/shard_map/pallas_call | solution.py:462
  7.1 0.0 collective-permute-done.1.payload.row_odd
  7.1 1.7 %collective-permute-done.row_even = f32[104,128]{1,0:T(8,128)S(1)} collective-permute-done((f32[104,128]{1,0:T(8,128)S(1)}, f32[104,128]{1,0:T(8,128)S(1)}, u32[]{:S(2)}, u32[]{:S(2)}) %collective-permute-start) | collective-permute-done | bytes 53280 | tf_op jit(solution)/shard_map/ppermute | solution.py:394
  8.9 0.2 shard_map.85
  9.1 0.0 copy-start.5
  9.1 0.0 copy-start.6
  9.1 1.4 %collective-permute-start.3 = (f32[248,128]{1,0:T(8,128)S(1)}, f32[248,128]{1,0:T(8,128)S(1)}, u32[]{:S(2)}, u32[]{:S(2)}) collective-permute-start(f32[248,128]{1,0:T(8,128)S(1)} %get-tuple-element.31), channel_id=1, source_target_pairs={{0,32},{1,2},{2,1},{3,4},{4,3},{5,6},{6,5},{7,8},{8,7},{9,10},{10,... | collective-permute-start | bytes 380936 | tf_op jit(solution)/shard_map/ppermute | solution.py:394
  10.4 0.4 %collective-permute-start.2 = (f32[248,128]{1,0:T(8,128)S(1)}, f32[248,128]{1,0:T(8,128)S(1)}, u32[]{:S(2)}, u32[]{:S(2)}) collective-permute-start(f32[248,128]{1,0:T(8,128)S(1)} %get-tuple-element.30), channel_id=1, source_target_pairs={{0,1},{1,0},{2,3},{3,2},{4,5},{5,4},{6,7},{7,6},{8,9},{9,8},{10,11... | collective-permute-start | bytes 380936 | tf_op jit(solution)/shard_map/ppermute | solution.py:394
  10.9 0.0 copy-done.2
  10.9 0.0 copy-done.5
  10.9 0.0 copy-done.6
  10.9 1.0 %shard_map.87 = (bf16[224,128]{1,0:T(8,128)(2,1)S(1)}, bf16[256,256]{1,0:T(8,128)(2,1)S(1)}, bf16[256,896]{1,0:T(8,128)(2,1)S(1)}) custom-call(f32[17]{0:T(128)S(1)} %copy-done.5, f32[17]{0:T(128)S(1)} %copy-done.6, bf16[256,896]{1,0:T(8,128)(2,1)S(1)} %copy-done.2), custom_call_target="tpu_custom_call" | custom-call | tf_op jit(solution)/shard_map/pallas_call | solution.py:470
  11.9 3.8 %collective-permute-done.3.payload.odd_in = f32[248,128]{1,0:T(8,128)S(1)} collective-permute-done((f32[248,128]{1,0:T(8,128)S(1)}, f32[248,128]{1,0:T(8,128)S(1)}, u32[]{:S(2)}, u32[]{:S(2)}) %collective-permute-start.3) | collective-permute-done | bytes 127008 | tf_op jit(solution)/shard_map/ppermute | solution.py:394
  15.6 0.0 collective-permute-done.2.even_in
  15.6 5.5 %shard_map.88 = (f32[256,128]{1,0:T(8,128)S(1)}, f32[96,128]{1,0:T(8,128)S(1)}, f32[192,128]{1,0:T(8,128)S(1)}, f32[72,128]{1,0:T(8,128)S(1)}) custom-call(s32[8,128]{1,0:T(8,128)S(1)} %get-tuple-element.22.scalars_in, f32[352,128]{1,0:T(8,128)S(1)} %get-tuple-element.27.fa, f32[288,128]{1,0:T(8,128)S(1)} %get-tuple-element.28.pa, ...), custom_call_target="tpu_custom_call" | custom-call | tf_op jit(solution)/shard_map/pallas_call | solution.py:408
  21.1 0.1 collective-permute-start.4
  21.2 2.1 %collective-permute-start.6 = (f32[96,128]{1,0:T(8,128)S(1)}, f32[96,128]{1,0:T(8,128)S(1)}, u32[]{:S(2)}, u32[]{:S(2)}) collective-permute-start(f32[96,128]{1,0:T(8,128)S(1)} %get-tuple-element.38), channel_id=1, source_target_pairs={{0,32},{32,64},{64,96},{96,128},{128,160},{160,192},{192,224},{224... | collective-permute-start | bytes 147464 | tf_op jit(solution)/shard_map/ppermute | solution.py:379
  23.3 0.0 collective-permute-start.5
  23.4 4.0 %collective-permute-done.4.spill = f32[192,128]{1,0:T(8,128)S(1)} collective-permute-done((f32[192,128]{1,0:T(8,128)S(1)}, f32[192,128]{1,0:T(8,128)S(1)}, u32[]{:S(2)}, u32[]{:S(2)}) %collective-permute-start.4) | collective-permute-done | bytes 98336 | tf_op jit(solution)/shard_map/ppermute | solution.py:379
  27.4 0.1 shard_map.89.own
  27.5 2.3 %collective-permute-done.5.corner = f32[72,128]{1,0:T(8,128)S(1)} collective-permute-done((f32[72,128]{1,0:T(8,128)S(1)}, f32[72,128]{1,0:T(8,128)S(1)}, u32[]{:S(2)}, u32[]{:S(2)}) %collective-permute-start.5) | collective-permute-done | bytes 36896 | tf_op jit(solution)/shard_map/ppermute | solution.py:404
  29.7 0.1 shard_map.90
  29.8 0.0 collective-permute-done.6
  29.8 0.7 %pad_add_fusion = f32[256,128]{1,0:T(8,128)} fusion(f32[256,128]{1,0:T(8,128)S(1)} %shard_map.90, f32[96,128]{1,0:T(8,128)S(1)} %collective-permute-done.6), kind=kLoop, calls=%fused_computation | loop fusion | flops 32768 | bytes 311296 | tf_op jit(solution)/shard_map/add | solution.py:509
  (2 shorter events, 0.0 us)
Async XLA Ops:
  0.0 0.7 %copy-start.4 = (s32[1,1,16]{2,1,0:T(1,128)S(1)}, s32[1,1,16]{2,1,0:T(1,128)}, u32[]{:S(2)}) copy-start(s32[1,1,16]{2,1,0:T(1,128)} %win_col.1) | copy-start | bytes 196
  0.0 0.7 %copy-start.3 = (s32[1,1,16]{2,1,0:T(1,128)S(1)}, s32[1,1,16]{2,1,0:T(1,128)}, u32[]{:S(2)}) copy-start(s32[1,1,16]{2,1,0:T(1,128)} %win_row.1) | copy-start | bytes 196
  0.7 6.1 %copy-start = (f32[256,128]{1,0:T(8,128)S(1)}, f32[256,128]{1,0:T(8,128)}, u32[]{:S(2)}) copy-start(f32[256,128]{1,0:T(8,128)} %friction.3) | copy-start | bytes 393220
  0.7 6.1 %copy-start.1 = (f32[256,128]{1,0:T(8,128)S(1)}, f32[256,128]{1,0:T(8,128)}, u32[]{:S(2)}) copy-start(f32[256,128]{1,0:T(8,128)} %probe.3) | copy-start | bytes 393220
  1.6 9.2 %copy-start.2 = (bf16[256,896]{1,0:T(8,128)(2,1)S(1)}, bf16[256,896]{1,0:T(8,128)(2,1)}, u32[]{:S(2)}) copy-start(bf16[256,896]{1,0:T(8,128)(2,1)} %constant.5.clone.tables_in) | copy-start | bytes 1376260
  1.6 5.5 %collective-permute-start.1 = (f32[104,128]{1,0:T(8,128)S(1)}, f32[104,128]{1,0:T(8,128)S(1)}, u32[]{:S(2)}, u32[]{:S(2)}) collective-permute-start(f32[104,128]{1,0:T(8,128)S(1)} %get-tuple-element.26), channel_id=1, source_target_pairs={{0,1},{1,0},{2,3},{3,2},{4,5},{5,4},{6,7},{7,6},{8,9},{9,8},{10,11... | collective-permute-start | bytes 159752 | tf_op jit(solution)/shard_map/ppermute | solution.py:394
  1.8 7.0 %collective-permute-start = (f32[104,128]{1,0:T(8,128)S(1)}, f32[104,128]{1,0:T(8,128)S(1)}, u32[]{:S(2)}, u32[]{:S(2)}) collective-permute-start(f32[104,128]{1,0:T(8,128)S(1)} %get-tuple-element.25.mine), channel_id=1, source_target_pairs={{0,32},{1,33},{2,34},{3,35},{4,36},{5,37},{6,38},{7,39},{8,40},{9,... | collective-permute-start | bytes 159752 | tf_op jit(solution)/shard_map/ppermute | solution.py:394
  9.1 1.8 %copy-start.5 = (f32[17]{0:T(128)S(1)}, f32[17]{0:T(128)}, u32[]{:S(2)}) copy-start(f32[17]{0:T(128)} %taps_row.1) | copy-start | bytes 208
  9.1 1.8 %copy-start.6 = (f32[17]{0:T(128)S(1)}, f32[17]{0:T(128)}, u32[]{:S(2)}) copy-start(f32[17]{0:T(128)} %taps_col.1) | copy-start | bytes 208
  9.1 6.5 %collective-permute-start.3 = (f32[248,128]{1,0:T(8,128)S(1)}, f32[248,128]{1,0:T(8,128)S(1)}, u32[]{:S(2)}, u32[]{:S(2)}) collective-permute-start(f32[248,128]{1,0:T(8,128)S(1)} %get-tuple-element.31), channel_id=1, source_target_pairs={{0,32},{1,2},{2,1},{3,4},{4,3},{5,6},{6,5},{7,8},{8,7},{9,10},{10,... | collective-permute-start | bytes 380936 | tf_op jit(solution)/shard_map/ppermute | solution.py:394
  10.4 5.2 %collective-permute-start.2 = (f32[248,128]{1,0:T(8,128)S(1)}, f32[248,128]{1,0:T(8,128)S(1)}, u32[]{:S(2)}, u32[]{:S(2)}) collective-permute-start(f32[248,128]{1,0:T(8,128)S(1)} %get-tuple-element.30), channel_id=1, source_target_pairs={{0,1},{1,0},{2,3},{3,2},{4,5},{5,4},{6,7},{7,6},{8,9},{9,8},{10,11... | collective-permute-start | bytes 380936 | tf_op jit(solution)/shard_map/ppermute | solution.py:394
  21.1 6.2 %collective-permute-start.4 = (f32[192,128]{1,0:T(8,128)S(1)}, f32[192,128]{1,0:T(8,128)S(1)}, u32[]{:S(2)}, u32[]{:S(2)}) collective-permute-start(f32[192,128]{1,0:T(8,128)S(1)} %get-tuple-element.36), channel_id=1, source_target_pairs={{0,1},{1,2},{2,3},{3,4},{4,5},{5,6},{6,7},{7,8},{8,9},{9,10},{10,1... | collective-permute-start | bytes 294920 | tf_op jit(solution)/shard_map/ppermute | solution.py:379
  21.2 8.6 %collective-permute-start.6 = (f32[96,128]{1,0:T(8,128)S(1)}, f32[96,128]{1,0:T(8,128)S(1)}, u32[]{:S(2)}, u32[]{:S(2)}) collective-permute-start(f32[96,128]{1,0:T(8,128)S(1)} %get-tuple-element.38), channel_id=1, source_target_pairs={{0,32},{32,64},{64,96},{96,128},{128,160},{160,192},{192,224},{224... | collective-permute-start | bytes 147464 | tf_op jit(solution)/shard_map/ppermute | solution.py:379
  23.3 6.4 %collective-permute-start.5 = (f32[72,128]{1,0:T(8,128)S(1)}, f32[72,128]{1,0:T(8,128)S(1)}, u32[]{:S(2)}, u32[]{:S(2)}) collective-permute-start(f32[72,128]{1,0:T(8,128)S(1)} %get-tuple-element.37), channel_id=1, source_target_pairs={{0,33},{1,34},{2,35},{3,36},{4,37},{5,38},{6,39},{7,40},{8,41},{9,... | collective-permute-start | bytes 110600 | tf_op jit(solution)/shard_map/ppermute | solution.py:404

commit v8 on v6

--- a/solution.py
+++ b/solution.py
@@ -206,7 +206,7 @@
     at_col, col_count = own_index("my")
     leftmost, rightmost = at_col == 0, at_col == col_count - 1
     is_even = lax.rem(at_col, 2) == 0
-    from_left[0:240, :] = jnp.where(is_even, odd_in[0:240, :], even_in[0:240, :])
+    from_left[0:88, :] = jnp.where(is_even, odd_in[0:88, :], even_in[0:88, :])
     from_right[0:240, :] = jnp.where(is_even, even_in[0:240, :], odd_in[0:240, :])
     from_left[240:248, :] = jnp.where(is_even, odd_slots[...], even_in[240:248, :])
     from_right[240:248, :] = jnp.where(is_even, even_in[240:248, :], odd_slots[...])
@@ -259,6 +259,14 @@
     for k in range(SLOTS):
         rows = pl.ds(scalars[0, k], 128)
         fw[k] = window(fa[rows, :], fb[rows, :], scalars[1, k] - 32)
+    def lane_transform(x):
+        hi, lo = split(x)
+        return split(halves(dot(jnp.concatenate([hi, lo], 1), tables[:, 0:256]), 1))
+
+    for k in range(SLOTS):
+        rows = pl.ds(scalars[0, k], PATCH)
+        z[pl.ds(k * PATCH, PATCH), :] = window(pa[rows, :], pb[rows, :], scalars[1, k] - 32)
+    win_hi, win_lo = lane_transform(z[...])
     first, n = 8, 112
     while True:
         o = halves(dot(y2[0 : SLOTS * n, :], col_band[...]), 1)
@@ -279,15 +287,7 @@
                 y2[pl.ds((k + i) * m, m), :] = jnp.concatenate([hi, lo], 1)
         first, n = first + 8, m
 
-    def lane_transform(x):
-        hi, lo = split(x)
-        return split(halves(dot(jnp.concatenate([hi, lo], 1), tables[:, 0:256]), 1))
-
     ker_hi, ker_lo = lane_transform(o.reshape(SLOTS * PATCH, 128))
-    for k in range(SLOTS):
-        rows = pl.ds(scalars[0, k], PATCH)
-        z[pl.ds(k * PATCH, PATCH), :] = window(pa[rows, :], pb[rows, :], scalars[1, k] - 32)
-    win_hi, win_lo = lane_transform(z[...])
     left_half = lax.broadcasted_iota(jnp.int32, (PATCH, 128), 1) < 64
     sign = jnp.where(left_half, -1.0, 1.0)
 

time: 29 us -> 28.9 us (level)
  no operation moved by 1% of the time
where the time goes in v8:
time: 28.9 us; the launch traced here: 28.4 us
  waiting for transfers between devices  9.64 us (33%)
  starting transfers between devices  9.42 us (33%)
  Pallas kernels  7.84 us (27%)
  between operations  0.83 us (3%)
  other arithmetic  0.68 us (2%)
    ppermute x4, starting transfers between devices, swap(): return lax.ppermute(x, ('mx', 'my'), pairs)  6.91 us
    ppermute x4, waiting for transfers between devices, swap(): return lax.ppermute(x, ('mx', 'my'), pairs)  5.5 us
    pallas_call x1, Pallas kernels, core_call(): pl.pallas_call(core_kernel, out_shape=[shape(TILE_R), shape(OUT_R - TILE_...  5.35 us
    ppermute x2, waiting for transfers between devices, ring(): return lax.ppermute(x, axis, [(i, (i + by) % count) for i in range(count)])  3.72 us
    ppermute x2, starting transfers between devices, ring(): return lax.ppermute(x, axis, [(i, (i + by) % count) for i in range(count)])  1.3 us
    ppermute x1, starting transfers between devices, diagonal(): return lax.ppermute(x, ('mx', 'my'), pairs)  1.21 us
    pallas_call x1, Pallas kernels, per_device(): pl.pallas_call(bands_kernel, out_shape=[shape(224, BF), shape(256, BF, 25...  0.99 us
    pallas_call x1, Pallas kernels, per_device(): pl.pallas_call(pack_rows_kernel, out_shape=[shape(104), shape(104), shape...  0.89 us
  transfers between devices with their start and end apart: 7, of which 4 were waited for; matrix products, arithmetic and copies ran while one was open for 0% of the time, Pallas kernels for 5%

profile of v8, /device:TPU:68, one launch (start us, length us, event | category | flops | bytes accessed | tf_op | source)
XLA Modules:
  0.0 28.4 jit_solution(4990754850629631684)
XLA Ops:
  0.0 0.0 copy-start.4
  0.0 0.0 copy-start.3
  0.7 0.0 copy-done.4
  0.7 0.0 copy-done.3
  0.7 0.0 copy-start
  0.7 0.0 copy-start.1
  0.7 0.9 %shard_map.82 = (f32[104,128]{1,0:T(8,128)S(1)}, f32[104,128]{1,0:T(8,128)S(1)}, s32[8,128]{1,0:T(8,128)S(1)}) custom-call(s32[1,1,16]{2,1,0:T(1,128)S(1)} %copy-done.3, s32[1,1,16]{2,1,0:T(1,128)S(1)} %copy-done.4, s32[1,1]{1,0:T(1,128)S(6)} %copy.13.live_count, f32[256,128]{1,0:T(8,128)} %friction.3, f32[256,128]{1,0:T(8,128)} %probe.3), custom_call_target="tpu_custom_call" | custom-call | tf_op jit(solution)/shard_map/pallas_call | solution.py:432
  1.6 0.0 copy-start.2
  1.6 0.2 collective-permute-start.1
  1.8 4.9 %collective-permute-start = (f32[104,128]{1,0:T(8,128)S(1)}, f32[104,128]{1,0:T(8,128)S(1)}, u32[]{:S(2)}, u32[]{:S(2)}) collective-permute-start(f32[104,128]{1,0:T(8,128)S(1)} %get-tuple-element.25.mine), channel_id=1, source_target_pairs={{0,32},{1,33},{2,34},{3,35},{4,36},{5,37},{6,38},{7,39},{8,40},{9,... | collective-permute-start | bytes 159752 | tf_op jit(solution)/shard_map/ppermute | solution.py:379
  6.8 0.0 copy-done
  6.8 0.0 copy-done.1
  6.8 0.3 %shard_map.83 = (f32[352,128]{1,0:T(8,128)S(1)}, f32[288,128]{1,0:T(8,128)S(1)}) custom-call(f32[256,128]{1,0:T(8,128)S(1)} %copy-done, f32[256,128]{1,0:T(8,128)S(1)} %copy-done.1), custom_call_target="tpu_custom_call" | custom-call | tf_op jit(solution)/shard_map/pallas_call | solution.py:447
  7.1 0.0 collective-permute-done.1.payload.row_odd
  7.1 1.7 %collective-permute-done.row_even = f32[104,128]{1,0:T(8,128)S(1)} collective-permute-done((f32[104,128]{1,0:T(8,128)S(1)}, f32[104,128]{1,0:T(8,128)S(1)}, u32[]{:S(2)}, u32[]{:S(2)}) %collective-permute-start) | collective-permute-done | bytes 53280 | tf_op jit(solution)/shard_map/ppermute | solution.py:379
  8.9 0.2 shard_map.85
  9.1 0.0 copy-start.5
  9.1 0.0 copy-start.6
  9.1 1.4 %collective-permute-start.3 = (f32[248,128]{1,0:T(8,128)S(1)}, f32[248,128]{1,0:T(8,128)S(1)}, u32[]{:S(2)}, u32[]{:S(2)}) collective-permute-start(f32[248,128]{1,0:T(8,128)S(1)} %get-tuple-element.31), channel_id=1, source_target_pairs={{0,32},{1,2},{2,1},{3,4},{4,3},{5,6},{6,5},{7,8},{8,7},{9,10},{10,... | collective-permute-start | bytes 380936 | tf_op jit(solution)/shard_map/ppermute | solution.py:379
  10.4 0.4 %collective-permute-start.2 = (f32[248,128]{1,0:T(8,128)S(1)}, f32[248,128]{1,0:T(8,128)S(1)}, u32[]{:S(2)}, u32[]{:S(2)}) collective-permute-start(f32[248,128]{1,0:T(8,128)S(1)} %get-tuple-element.30), channel_id=1, source_target_pairs={{0,1},{1,0},{2,3},{3,2},{4,5},{5,4},{6,7},{7,6},{8,9},{9,8},{10,11... | collective-permute-start | bytes 380936 | tf_op jit(solution)/shard_map/ppermute | solution.py:379
  10.9 0.0 copy-done.2
  10.9 0.0 copy-done.5
  10.9 0.0 copy-done.6
  10.9 1.0 %shard_map.87 = (bf16[224,128]{1,0:T(8,128)(2,1)S(1)}, bf16[256,256]{1,0:T(8,128)(2,1)S(1)}, bf16[256,896]{1,0:T(8,128)(2,1)S(1)}) custom-call(f32[17]{0:T(128)S(1)} %copy-done.5, f32[17]{0:T(128)S(1)} %copy-done.6, bf16[256,896]{1,0:T(8,128)(2,1)S(1)} %copy-done.2), custom_call_target="tpu_custom_call" | custom-call | tf_op jit(solution)/shard_map/pallas_call | solution.py:455
  11.9 3.8 %collective-permute-done.3.payload.odd_in = f32[248,128]{1,0:T(8,128)S(1)} collective-permute-done((f32[248,128]{1,0:T(8,128)S(1)}, f32[248,128]{1,0:T(8,128)S(1)}, u32[]{:S(2)}, u32[]{:S(2)}) %collective-permute-start.3) | collective-permute-done | bytes 127008 | tf_op jit(solution)/shard_map/ppermute | solution.py:379
  15.6 0.0 collective-permute-done.2.even_in
  15.6 5.3 %shard_map.88 = (f32[256,128]{1,0:T(8,128)S(1)}, f32[96,128]{1,0:T(8,128)S(1)}, f32[192,128]{1,0:T(8,128)S(1)}, f32[96,128]{1,0:T(8,128)S(1)}) custom-call(s32[8,128]{1,0:T(8,128)S(1)} %get-tuple-element.22.scalars_in, f32[352,128]{1,0:T(8,128)S(1)} %get-tuple-element.27.fa, f32[288,128]{1,0:T(8,128)S(1)} %get-tuple-element.28.pa, ...), custom_call_target="tpu_custom_call" | custom-call | tf_op jit(solution)/shard_map/pallas_call | solution.py:393
  21.0 0.1 collective-permute-start.4
  21.1 1.2 %collective-permute-start.5 = (f32[96,128]{1,0:T(8,128)S(1)}, f32[96,128]{1,0:T(8,128)S(1)}, u32[]{:S(2)}, u32[]{:S(2)}) collective-permute-start(f32[96,128]{1,0:T(8,128)S(1)} %get-tuple-element.37), channel_id=1, source_target_pairs={{0,33},{1,34},{2,35},{3,36},{4,37},{5,38},{6,39},{7,40},{8,41},{9,... | collective-permute-start | bytes 147464 | tf_op jit(solution)/shard_map/ppermute | solution.py:389
  22.3 1.2 %collective-permute-start.6 = (f32[96,128]{1,0:T(8,128)S(1)}, f32[96,128]{1,0:T(8,128)S(1)}, u32[]{:S(2)}, u32[]{:S(2)}) collective-permute-start(f32[96,128]{1,0:T(8,128)S(1)} %get-tuple-element.38), channel_id=1, source_target_pairs={{0,32},{32,64},{64,96},{96,128},{128,160},{160,192},{192,224},{224... | collective-permute-start | bytes 147464 | tf_op jit(solution)/shard_map/ppermute | solution.py:364
  23.5 3.7 %collective-permute-done.4.spill = f32[192,128]{1,0:T(8,128)S(1)} collective-permute-done((f32[192,128]{1,0:T(8,128)S(1)}, f32[192,128]{1,0:T(8,128)S(1)}, u32[]{:S(2)}, u32[]{:S(2)}) %collective-permute-start.4) | collective-permute-done | bytes 98336 | tf_op jit(solution)/shard_map/ppermute | solution.py:364
  27.2 0.1 shard_map.89
  27.3 0.4 %collective-permute-done.5 = f32[96,128]{1,0:T(8,128)S(1)} collective-permute-done((f32[96,128]{1,0:T(8,128)S(1)}, f32[96,128]{1,0:T(8,128)S(1)}, u32[]{:S(2)}, u32[]{:S(2)}) %collective-permute-start.5) | collective-permute-done | bytes 49184 | tf_op jit(solution)/shard_map/ppermute | solution.py:389
  27.8 0.0 collective-permute-done.6
  27.8 0.7 %pad_add_fusion = f32[256,128]{1,0:T(8,128)} fusion(f32[256,128]{1,0:T(8,128)S(1)} %pad_add_fusion.1, f32[96,128]{1,0:T(8,128)S(1)} %collective-permute-done.6), kind=kLoop, calls=%fused_computation | loop fusion | flops 32768 | bytes 311296 | tf_op jit(solution)/shard_map/add | solution.py:488
  (3 shorter events, 0.0 us)
Async XLA Ops:
  0.0 0.7 %copy-start.4 = (s32[1,1,16]{2,1,0:T(1,128)S(1)}, s32[1,1,16]{2,1,0:T(1,128)}, u32[]{:S(2)}) copy-start(s32[1,1,16]{2,1,0:T(1,128)} %win_col.1) | copy-start | bytes 196
  0.0 0.7 %copy-start.3 = (s32[1,1,16]{2,1,0:T(1,128)S(1)}, s32[1,1,16]{2,1,0:T(1,128)}, u32[]{:S(2)}) copy-start(s32[1,1,16]{2,1,0:T(1,128)} %win_row.1) | copy-start | bytes 196
  0.7 6.1 %copy-start = (f32[256,128]{1,0:T(8,128)S(1)}, f32[256,128]{1,0:T(8,128)}, u32[]{:S(2)}) copy-start(f32[256,128]{1,0:T(8,128)} %friction.3) | copy-start | bytes 393220
  0.7 6.1 %copy-start.1 = (f32[256,128]{1,0:T(8,128)S(1)}, f32[256,128]{1,0:T(8,128)}, u32[]{:S(2)}) copy-start(f32[256,128]{1,0:T(8,128)} %probe.3) | copy-start | bytes 393220
  1.6 9.2 %copy-start.2 = (bf16[256,896]{1,0:T(8,128)(2,1)S(1)}, bf16[256,896]{1,0:T(8,128)(2,1)}, u32[]{:S(2)}) copy-start(bf16[256,896]{1,0:T(8,128)(2,1)} %constant.5.clone.tables_in) | copy-start | bytes 1376260
  1.6 5.5 %collective-permute-start.1 = (f32[104,128]{1,0:T(8,128)S(1)}, f32[104,128]{1,0:T(8,128)S(1)}, u32[]{:S(2)}, u32[]{:S(2)}) collective-permute-start(f32[104,128]{1,0:T(8,128)S(1)} %get-tuple-element.26), channel_id=1, source_target_pairs={{0,1},{1,0},{2,3},{3,2},{4,5},{5,4},{6,7},{7,6},{8,9},{9,8},{10,11... | collective-permute-start | bytes 159752 | tf_op jit(solution)/shard_map/ppermute | solution.py:379
  1.8 7.0 %collective-permute-start = (f32[104,128]{1,0:T(8,128)S(1)}, f32[104,128]{1,0:T(8,128)S(1)}, u32[]{:S(2)}, u32[]{:S(2)}) collective-permute-start(f32[104,128]{1,0:T(8,128)S(1)} %get-tuple-element.25.mine), channel_id=1, source_target_pairs={{0,32},{1,33},{2,34},{3,35},{4,36},{5,37},{6,38},{7,39},{8,40},{9,... | collective-permute-start | bytes 159752 | tf_op jit(solution)/shard_map/ppermute | solution.py:379
  9.1 1.8 %copy-start.5 = (f32[17]{0:T(128)S(1)}, f32[17]{0:T(128)}, u32[]{:S(2)}) copy-start(f32[17]{0:T(128)} %taps_row.1) | copy-start | bytes 208
  9.1 1.8 %copy-start.6 = (f32[17]{0:T(128)S(1)}, f32[17]{0:T(128)}, u32[]{:S(2)}) copy-start(f32[17]{0:T(128)} %taps_col.1) | copy-start | bytes 208
  9.1 6.5 %collective-permute-start.3 = (f32[248,128]{1,0:T(8,128)S(1)}, f32[248,128]{1,0:T(8,128)S(1)}, u32[]{:S(2)}, u32[]{:S(2)}) collective-permute-start(f32[248,128]{1,0:T(8,128)S(1)} %get-tuple-element.31), channel_id=1, source_target_pairs={{0,32},{1,2},{2,1},{3,4},{4,3},{5,6},{6,5},{7,8},{8,7},{9,10},{10,... | collective-permute-start | bytes 380936 | tf_op jit(solution)/shard_map/ppermute | solution.py:379
  10.4 5.2 %collective-permute-start.2 = (f32[248,128]{1,0:T(8,128)S(1)}, f32[248,128]{1,0:T(8,128)S(1)}, u32[]{:S(2)}, u32[]{:S(2)}) collective-permute-start(f32[248,128]{1,0:T(8,128)S(1)} %get-tuple-element.30), channel_id=1, source_target_pairs={{0,1},{1,0},{2,3},{3,2},{4,5},{5,4},{6,7},{7,6},{8,9},{9,8},{10,11... | collective-permute-start | bytes 380936 | tf_op jit(solution)/shard_map/ppermute | solution.py:379
  21.0 6.2 %collective-permute-start.4 = (f32[192,128]{1,0:T(8,128)S(1)}, f32[192,128]{1,0:T(8,128)S(1)}, u32[]{:S(2)}, u32[]{:S(2)}) collective-permute-start(f32[192,128]{1,0:T(8,128)S(1)} %get-tuple-element.36), channel_id=1, source_target_pairs={{0,1},{1,2},{2,3},{3,4},{4,5},{5,6},{6,7},{7,8},{8,9},{9,10},{10,1... | collective-permute-start | bytes 294920 | tf_op jit(solution)/shard_map/ppermute | solution.py:364
  21.1 6.7 %collective-permute-start.5 = (f32[96,128]{1,0:T(8,128)S(1)}, f32[96,128]{1,0:T(8,128)S(1)}, u32[]{:S(2)}, u32[]{:S(2)}) collective-permute-start(f32[96,128]{1,0:T(8,128)S(1)} %get-tuple-element.37), channel_id=1, source_target_pairs={{0,33},{1,34},{2,35},{3,36},{4,37},{5,38},{6,39},{7,40},{8,41},{9,... | collective-permute-start | bytes 147464 | tf_op jit(solution)/shard_map/ppermute | solution.py:389
  22.3 5.5 %collective-permute-start.6 = (f32[96,128]{1,0:T(8,128)S(1)}, f32[96,128]{1,0:T(8,128)S(1)}, u32[]{:S(2)}, u32[]{:S(2)}) collective-permute-start(f32[96,128]{1,0:T(8,128)S(1)} %get-tuple-element.38), channel_id=1, source_target_pairs={{0,32},{32,64},{64,96},{96,128},{128,160},{160,192},{192,224},{224... | collective-permute-start | bytes 147464 | tf_op jit(solution)/shard_map/ppermute | solution.py:364
